TPU v7x, 32 devices: a whole 2x2x4 slice. The times are simulated.
32 devices in a mesh: batch: 8 (over y, x, core), ctx: 4 (over z).
Axes of the slice: x: 2, y: 2, z: 4, core: 2. Of those that a mesh axis runs over, the one named last changes fastest.
Arguments:
- block_in: bfloat16 [8, 8, 128, 768], P('batch', 'ctx'), may hold values from -6 to 6
- cotangent: bfloat16 [8, 8, 128, 768], P('batch', 'ctx'), may hold values from -6 to 6
- w_qkv: float32 [768, 2304], P('batch', 'ctx'), may hold values from -0.21875 to 0.21875
- w_out: float32 [768, 768], P('batch', 'ctx'), may hold values from -0.875 to 0.875
- w_fc: float32 [768, 3072], P('batch', 'ctx'), may hold values from -0.21875 to 0.21875
- w_proj: float32 [3072, 768], P('batch', 'ctx'), may hold values from -0.109375 to 0.109375
- vectors: float32 [12, 768], P(None, 'ctx'), may hold values from -0.5 to 1.5, as said below
- qkv_first: float32 [768, 2304], P('batch', 'ctx'), may hold values from -16 to 16
- qkv_second: float32 [768, 2304], P('batch', 'ctx'), may hold values from 0.73728 to 2.94912
- out_first: float32 [768, 768], P('batch', 'ctx'), may hold values from -28 to 28
- out_second: float32 [768, 768], P('batch', 'ctx'), may hold values from 2.048 to 8.192
- fc_first: float32 [768, 3072], P('batch', 'ctx'), may hold values from -28 to 28
- fc_second: float32 [768, 3072], P('batch', 'ctx'), may hold values from 2.048 to 8.192
- proj_first: float32 [3072, 768], P('batch', 'ctx'), may hold values from -28 to 28
- proj_second: float32 [3072, 768], P('batch', 'ctx'), may hold values from 2.048 to 8.192
- vec_first: float32 [12, 768], P(None, 'ctx'), may hold values from -56 to 56
- vec_second: float32 [12, 768], P(None, 'ctx'), may hold values from 8.192 to 32.768
Outputs:
- out_block: bfloat16 [8, 8, 128, 768], P('batch', 'ctx')
- grad_input: float32 [8, 8, 128, 768], P('batch', 'ctx')
- qkv_first_new: float32 [768, 2304], P('batch', 'ctx')
- qkv_second_new: float32 [768, 2304], P('batch', 'ctx')
- qkv_new: float32 [768, 2304], P('batch', 'ctx')
- out_first_new: float32 [768, 768], P('batch', 'ctx')
- out_second_new: float32 [768, 768], P('batch', 'ctx')
- out_new: float32 [768, 768], P('batch', 'ctx')
- fc_first_new: float32 [768, 3072], P('batch', 'ctx')
- fc_second_new: float32 [768, 3072], P('batch', 'ctx')
- fc_new: float32 [768, 3072], P('batch', 'ctx')
- proj_first_new: float32 [3072, 768], P('batch', 'ctx')
- proj_second_new: float32 [3072, 768], P('batch', 'ctx')
- proj_new: float32 [3072, 768], P('batch', 'ctx')
- vec_first_new: float32 [12, 768], P(None, 'ctx')
- vec_second_new: float32 [12, 768], P(None, 'ctx')
- vec_new: float32 [12, 768], P(None, 'ctx')
Inputs may be any that keep to these rules, and one draw needn't show every extreme that they name: `vectors`: rows 0 and 2 are gains between 0.5 and 1.5; the other rows are biases between -0.5 and 0.5.
All inputs are finite; a program needn't handle non-finite values.
Results may differ from a plain program's by a relative error of at most 0.0085.
The roundings to bfloat16 on the way count: a program that leaves them out, or rounds other values in their place, can miss the bound.
Values may be sent and summed in bfloat16 or wider, within the bound.
No kernel may reach another device: no remote copies, remote signals or barrier semaphores. Data moves between devices by JAX's collectives and lax.ppermute only.
A program may use at most 128 MiB of HBM per device.

v0:
```python
import math

import jax
import jax.numpy as jnp
from jax import lax
from jax.sharding import PartitionSpec as P

HEADS = 12
STEP = 10


def layer_norm(value, gain, shift):
    mean = jnp.mean(value, axis=-1, keepdims=True)
    centred = value - mean
    spread = jnp.mean(centred * centred, axis=-1, keepdims=True)
    return centred * lax.rsqrt(spread + 1e-05) * gain + shift


def gelu_tanh(value):
    return (
        0.5
        * value
        * (1.0 + jnp.tanh(0.7978845608028654 * (value + 0.044715 * value * value * value)))
    )


def block_places(index, count, half):
    offsets = jnp.arange(half, dtype=jnp.int32)
    first = index * half + offsets
    second = (2 * count - 1 - index) * half + offsets
    return jnp.concatenate([first, second])


def scores_of(queries, keys, scale, allowed):
    raw = jnp.einsum("sqhd,skhd->shqk", queries, keys, preferred_element_type=jnp.float32) * scale
    return jnp.where(allowed[None, None], raw, -1e30)


def pair_grads(queries, grads, keys, values, top, total, delta, scale, allowed):
    score = scores_of(queries, keys, scale, allowed)
    weights = jnp.exp(score - top[..., None]) / total[..., None]
    back_weights = jnp.einsum("sqhd,skhd->shqk", grads, values, preferred_element_type=jnp.float32)
    grad_score = (weights * (back_weights - delta[..., None])).astype(jnp.bfloat16)
    return (weights.astype(jnp.bfloat16), grad_score)


def rows_product(left, right):
    return jnp.einsum("ra,rb->ab", left, right, preferred_element_type=jnp.float32)


def back_product(grad, weight):
    return jnp.einsum("rb,ab->ra", grad, weight, preferred_element_type=jnp.float32)


def adamw(weight, grad, first, second, rate, decay):
    first = 0.9 * first + 0.1 * grad
    second = 0.999 * second + 0.001 * grad * grad
    first_hat = first / (1.0 - 0.9**STEP)
    second_hat = second / (1.0 - 0.999**STEP)
    weight = weight - rate * (first_hat / (jnp.sqrt(second_hat) + 1e-08) + decay * weight)
    return (first, second, weight)


def local(
    block_in,
    cotangent,
    w_qkv,
    w_out,
    w_fc,
    w_proj,
    vectors,
    qkv_first,
    qkv_second,
    out_first,
    out_second,
    fc_first,
    fc_second,
    proj_first,
    proj_second,
    vec_first,
    vec_second,
):
    low_type = jnp.bfloat16
    wide = jnp.float32
    row_parts = (
        lax.all_gather(w_qkv.astype(low_type), "batch", axis=0, tiled=True),
        lax.all_gather(w_out.astype(low_type), "batch", axis=0, tiled=True),
        lax.all_gather(w_fc.astype(low_type), "batch", axis=0, tiled=True),
        lax.all_gather(w_proj.astype(low_type), "batch", axis=0, tiled=True),
    )
    full_qkv, full_out, full_fc, full_proj, full_vec = (
        lax.all_gather(row_parts[0], "ctx", axis=1, tiled=True),
        lax.all_gather(row_parts[1], "ctx", axis=1, tiled=True),
        lax.all_gather(row_parts[2], "ctx", axis=1, tiled=True),
        lax.all_gather(row_parts[3], "ctx", axis=1, tiled=True),
        lax.all_gather(vectors.astype(low_type), "ctx", axis=1, tiled=True),
    )
    params = full_vec.astype(wide)
    seqs, pair, half, width = block_in.shape
    heads = HEADS
    head = width // heads
    rows = seqs * pair * half
    span = pair * half
    count = lax.axis_size("ctx")
    index = lax.axis_index("ctx")
    scale = 1.0 / math.sqrt(head)
    inputs = block_in.astype(wide).reshape(rows, width)
    normed_one = layer_norm(inputs, params[0], params[1]).astype(low_type)
    mixed = jnp.dot(normed_one, full_qkv, preferred_element_type=wide)
    queries = (mixed[:, :width] + params[4]).astype(low_type)
    keys = mixed[:, width : 2 * width].astype(low_type)
    values = (mixed[:, 2 * width :] + params[5]).astype(low_type)
    key_all, value_all = (
        lax.all_gather(keys.reshape(seqs, pair, half, width), "ctx", axis=1, tiled=True),
        lax.all_gather(values.reshape(seqs, pair, half, width), "ctx", axis=1, tiled=True),
    )
    query_heads = queries.reshape(seqs, span, heads, head)
    own_places = block_places(index, count, half)

    def piece_of(source, piece):
        return lax.dynamic_slice_in_dim(source, 2 * piece, 2, 1).reshape(seqs, span, heads, head)

    def allowed_for(piece):
        return own_places[:, None] >= block_places(piece, count, half)[None, :]

    def stats_step(piece, carry):
        top, total = carry
        score = scores_of(query_heads, piece_of(key_all, piece), scale, allowed_for(piece))
        new_top = jnp.maximum(top, jnp.max(score, axis=-1))
        total = total * jnp.exp(top - new_top) + jnp.sum(
            jnp.exp(score - new_top[..., None]), axis=-1
        )
        return (new_top, total)

    start_stats = (jnp.full((seqs, heads, span), -1e30, wide), jnp.zeros((seqs, heads, span), wide))
    top, total = lax.fori_loop(0, count, stats_step, start_stats)

    def output_step(piece, acc):
        score = scores_of(query_heads, piece_of(key_all, piece), scale, allowed_for(piece))
        weights = (jnp.exp(score - top[..., None]) / total[..., None]).astype(low_type)
        return acc + jnp.einsum(
            "shqk,skhd->sqhd", weights, piece_of(value_all, piece), preferred_element_type=wide
        )

    attended = lax.fori_loop(0, count, output_step, jnp.zeros((seqs, span, heads, head), wide))
    att_low = attended.reshape(rows, width).astype(low_type)
    mid = inputs + jnp.dot(att_low, full_out, preferred_element_type=wide) + params[6]
    normed_two = layer_norm(mid, params[2], params[3]).astype(low_type)
    pre = jnp.dot(normed_two, full_fc, preferred_element_type=wide) + params[8:12].reshape(-1)
    act_low = gelu_tanh(pre).astype(low_type)
    result = mid + jnp.dot(act_low, full_proj, preferred_element_type=wide) + params[7]
    out_block = result.astype(low_type).reshape(block_in.shape)
    grad_low = cotangent.reshape(rows, width)
    grad_out = grad_low.astype(wide)
    grad_wproj = rows_product(act_low, grad_low)
    back_act = back_product(grad_low, full_proj)
    grad_pre = jax.vjp(gelu_tanh, pre)[1](back_act)[0].astype(low_type)
    grad_wfc = rows_product(normed_two, grad_pre)
    back_two = back_product(grad_pre, full_fc)
    back_mid, grad_gain_two, grad_shift_two = jax.vjp(layer_norm, mid, params[2], params[3])[1](
        back_two
    )
    grad_mid = grad_out + back_mid
    grad_att_low = grad_mid.astype(low_type)
    grad_wout = rows_product(att_low, grad_att_low)
    back_att = back_product(grad_att_low, full_out)
    grad_heads = back_att.astype(low_type).reshape(seqs, span, heads, head)
    delta = jnp.einsum("sqhd,sqhd->shq", grad_heads.astype(wide), attended)
    query_all, grad_all = (
        lax.all_gather(queries.reshape(seqs, pair, half, width), "ctx", axis=1, tiled=True),
        lax.all_gather(grad_heads.reshape(seqs, pair, half, width), "ctx", axis=1, tiled=True),
    )
    top_all, total_all, delta_all = (
        lax.all_gather(top.reshape(seqs, heads, pair, half), "ctx", axis=2, tiled=True),
        lax.all_gather(total.reshape(seqs, heads, pair, half), "ctx", axis=2, tiled=True),
        lax.all_gather(delta.reshape(seqs, heads, pair, half), "ctx", axis=2, tiled=True),
    )

    def query_step(piece, grad_query):
        key_part = piece_of(key_all, piece)
        value_part = piece_of(value_all, piece)
        weights_low, grad_score = pair_grads(
            query_heads,
            grad_heads,
            key_part,
            value_part,
            top,
            total,
            delta,
            scale,
            allowed_for(piece),
        )
        return grad_query + jnp.einsum(
            "shqk,skhd->sqhd", grad_score, key_part, preferred_element_type=wide
        )

    grad_query = lax.fori_loop(0, count, query_step, jnp.zeros((seqs, span, heads, head), wide))
    key_heads = keys.reshape(seqs, span, heads, head)
    value_heads = values.reshape(seqs, span, heads, head)

    def stat_piece(source, piece):
        return lax.dynamic_slice_in_dim(source, 2 * piece, 2, 2).reshape(seqs, heads, span)

    def key_step(piece, carry):
        grad_key, grad_value = carry
        query_part = piece_of(query_all, piece)
        grad_part = piece_of(grad_all, piece)
        allowed = block_places(piece, count, half)[:, None] >= own_places[None, :]
        weights_low, grad_score = pair_grads(
            query_part,
            grad_part,
            key_heads,
            value_heads,
            stat_piece(top_all, piece),
            stat_piece(total_all, piece),
            stat_piece(delta_all, piece),
            scale,
            allowed,
        )
        grad_key = grad_key + jnp.einsum(
            "shqk,sqhd->skhd", grad_score, query_part, preferred_element_type=wide
        )
        grad_value = grad_value + jnp.einsum(
            "shqk,sqhd->skhd", weights_low, grad_part, preferred_element_type=wide
        )
        return (grad_key, grad_value)

    start_keys = (
        jnp.zeros((seqs, span, heads, head), wide),
        jnp.zeros((seqs, span, heads, head), wide),
    )
    grad_key, grad_value = lax.fori_loop(0, count, key_step, start_keys)
    grad_keys = (grad_key * scale).reshape(seqs, pair, half, width)
    grad_values = grad_value.reshape(seqs, pair, half, width)
    grad_q_low = (grad_query * scale).reshape(rows, width).astype(low_type)
    grad_k_low = grad_keys.reshape(rows, width).astype(low_type)
    grad_v_low = grad_values.reshape(rows, width).astype(low_type)
    grad_mixed = jnp.concatenate([grad_q_low, grad_k_low, grad_v_low], axis=1)
    grad_wqkv = rows_product(normed_one, grad_mixed)
    back_one = back_product(grad_mixed, full_qkv)
    back_in, grad_gain_one, grad_shift_one = jax.vjp(layer_norm, inputs, params[0], params[1])[1](
        back_one
    )
    grad_input = (grad_mid + back_in).reshape(block_in.shape)
    grad_bias_q = jnp.sum(grad_q_low.astype(wide), axis=0)
    grad_bias_v = jnp.sum(grad_v_low.astype(wide), axis=0)
    grad_bias_out = jnp.sum(grad_att_low.astype(wide), axis=0)
    grad_bias_proj = jnp.sum(grad_out, axis=0)
    grad_bias_fc = jnp.sum(grad_pre.astype(wide), axis=0).reshape(4, width)
    small_rows = jnp.stack(
        [
            grad_gain_one,
            grad_shift_one,
            grad_gain_two,
            grad_shift_two,
            grad_bias_q,
            grad_bias_v,
            grad_bias_out,
            grad_bias_proj,
        ]
    )
    grad_vectors = jnp.concatenate([small_rows, grad_bias_fc], axis=0)
    col_sums = (
        lax.psum_scatter(grad_wqkv, "ctx", scatter_dimension=1, tiled=True),
        lax.psum_scatter(grad_wout, "ctx", scatter_dimension=1, tiled=True),
        lax.psum_scatter(grad_wfc, "ctx", scatter_dimension=1, tiled=True),
        lax.psum_scatter(grad_wproj, "ctx", scatter_dimension=1, tiled=True),
        lax.psum_scatter(grad_vectors, "ctx", scatter_dimension=1, tiled=True),
    )
    qkv_grad, out_grad, fc_grad, proj_grad = (
        lax.psum_scatter(col_sums[0], "batch", scatter_dimension=0, tiled=True),
        lax.psum_scatter(col_sums[1], "batch", scatter_dimension=0, tiled=True),
        lax.psum_scatter(col_sums[2], "batch", scatter_dimension=0, tiled=True),
        lax.psum_scatter(col_sums[3], "batch", scatter_dimension=0, tiled=True),
    )
    vec_grad = lax.psum(col_sums[4], "batch")
    qkv_m, qkv_s, qkv_w = adamw(w_qkv, qkv_grad, qkv_first, qkv_second, 0.06, 0.1)
    out_m, out_s, out_w = adamw(w_out, out_grad, out_first, out_second, 0.06, 0.1)
    fc_m, fc_s, fc_w = adamw(w_fc, fc_grad, fc_first, fc_second, 0.06, 0.1)
    proj_m, proj_s, proj_w = adamw(w_proj, proj_grad, proj_first, proj_second, 0.06, 0.1)
    vec_m, vec_s, vec_w = adamw(vectors, vec_grad, vec_first, vec_second, 0.2, 0.0)
    return (
        out_block,
        grad_input,
        qkv_m,
        qkv_s,
        qkv_w,
        out_m,
        out_s,
        out_w,
        fc_m,
        fc_s,
        fc_w,
        proj_m,
        proj_s,
        proj_w,
        vec_m,
        vec_s,
        vec_w,
    )


def solution(mesh):
    in_specs = (
        P("batch", "ctx", None, None),
        P("batch", "ctx", None, None),
        P("batch", "ctx"),
        P("batch", "ctx"),
        P("batch", "ctx"),
        P("batch", "ctx"),
        P(None, "ctx"),
        P("batch", "ctx"),
        P("batch", "ctx"),
        P("batch", "ctx"),
        P("batch", "ctx"),
        P("batch", "ctx"),
        P("batch", "ctx"),
        P("batch", "ctx"),
        P("batch", "ctx"),
        P(None, "ctx"),
        P(None, "ctx"),
    )
    out_specs = (
        P("batch", "ctx", None, None),
        P("batch", "ctx", None, None),
        P("batch", "ctx"),
        P("batch", "ctx"),
        P("batch", "ctx"),
        P("batch", "ctx"),
        P("batch", "ctx"),
        P("batch", "ctx"),
        P("batch", "ctx"),
        P("batch", "ctx"),
        P("batch", "ctx"),
        P("batch", "ctx"),
        P("batch", "ctx"),
        P("batch", "ctx"),
        P(None, "ctx"),
        P(None, "ctx"),
        P(None, "ctx"),
    )
    return jax.shard_map(local, mesh=mesh, in_specs=in_specs, out_specs=out_specs, check_vma=False)
```

profile of v0, /device:TPU:0, one launch (start us, length us, event | category | flops | bytes accessed | tf_op | source)
XLA Modules:
  0.0 1265.8 jit_solution(10799548325004580338)
XLA Ops:
  8.3 12.3 all_gather.49
  22.7 13.5 %all-gather = bf16[4,192,12]{1,2,0:T(8,128)(2,1)S(1)} all-gather(bf16[1,192,12]{1,2,0:T(8,128)(2,1)S(1)} %convert_bitcast_fusion), channel_id=1, replica_groups=mesh['batch'=8,'ctx'=4] {'ctx'}, dimensions={0}, use_global_device_ids=true | all-gather | bytes 23040 | tf_op jit(solution)/shard_map/all_gather | solution.py:96
  37.6 54.8 %all-gather.12.cloned.1.call-done = bf16[768,2304]{0,1:T(8,128)(2,1)} async-done(((bf16[768,576]{0,1:T(8,128)(2,1)}), bf16[768,2304]{0,1:T(8,128)(2,1)}) %all-gather.12.cloned.1.call-update) | async-done | bytes 3538960 | tf_op jit(solution)/shard_map/all_gather | solution.py:92
  92.5 3.1 fusion.78
  97.4 10.1 all_gather.53
  109.7 8.1 all-gather.20.cloned.1.call-done
  118.1 38.3 %all-gather.16.cloned.1.call-done = bf16[1,8,128,768]{3,2,0,1:T(8,128)(2,1)} async-done(((bf16[1,2,128,768]{3,2,0,1:T(8,128)(2,1)}), bf16[1,8,128,768]{3,2,0,1:T(8,128)(2,1)}) %all-gather.16.cloned.1.call-update) | async-done | bytes 1572880 | tf_op jit(solution)/shard_map/all_gather | solution.py:114
  156.4 3.0 copy.175
  159.4 39.7 %while.60 = (s32[]{:T(128)}, f32[1,12,256]{2,1,0:T(8,128)S(1)}, f32[1,12,256]{2,1,0:T(8,128)}, s32[256]{0:T(256)}, bf16[1,8,128,768]{2,1,3,0:T(8,128)(2,1)}, /*i...) while((s32[]{:T(128)}, f32[1,12,256]{2,1,0:T(8,128)S(1)}, ...), condition=%wide.region_5.6_spmd.clone, body=%wide.region_2.5_spmd.clone.sunk | while | flops 106249736 | bytes 9012446 | solution.py:136
  163.6 2.3 fusion.131
  173.0 2.3 fusion.131
  199.1 3.0 copy.174
  202.1 24.5 %while.61 = (s32[]{:T(128)}, f32[1,256,12,64]{1,3,2,0:T(8,128)S(1)}, bf16[1,8,128,768]{2,1,3,0:T(8,128)(2,1)}, s32[256]{0:T(256)}, bf16[1,8,128,768]{2,1,3,0:T(8...) while((s32[]{:T(128)}, ...), condition=%wide.region_7.8_spmd.clone, body=%wide.region_6.7_spmd.clone.sunk | while | flops 205718032 | bytes 6059245 | solution.py:145
  202.1 2.9 constant_dynamic-slice_fusion.17
  208.4 2.7 constant_dynamic-slice_fusion.17
  214.5 2.7 constant_dynamic-slice_fusion.17
  220.6 2.7 constant_dynamic-slice_fusion.17
  229.1 86.7 %all-gather.22.cloned.1.call-done = bf16[768,3072]{1,0:T(8,128)(2,1)} async-done(((bf16[768,768]{1,0:T(8,128)(2,1)}), bf16[768,3072]{1,0:T(8,128)(2,1)}) %all-gather.22.cloned.1.call-update) | async-done | bytes 4718608 | tf_op jit(solution)/shard_map/all_gather | solution.py:94
  315.7 3.9 convolution_add_fusion
  321.3 5.2 fusion.67
  326.7 159.8 %reduce-scatter.24.cloned.1.call-done = f32[3072,192]{0,1:T(8,128)} async-done(((f32[3072,768]{0,1:T(8,128)}), f32[3072,192]{0,1:T(8,128)}) %reduce-scatter.24.cloned.1.call-update) | async-done | bytes 2359312 | tf_op jit(solution)/shard_map/reduce_scatter | solution.py:267
  486.5 46.6 %reduce-scatter.26.cloned.1.call-done = f32[384,192]{0,1:T(8,128)} async-done(((f32[3072,192]{0,1:T(8,128)}), f32[384,192]{0,1:T(8,128)}) %reduce-scatter.26.cloned.1.call-update) | async-done | bytes 294928 | tf_op jit(solution)/shard_map/reduce_scatter | solution.py:274
  535.5 24.5 %all-gather.24.cloned.1.call-done = bf16[3072,192]{0,1:T(8,128)(2,1)} async-done(((bf16[384,192]{0,1:T(8,128)(2,1)}), bf16[3072,192]{0,1:T(8,128)(2,1)}) %all-gather.24.cloned.1.call-update) | async-done | bytes 1179664 | tf_op jit(solution)/shard_map/all_gather | solution.py:89
  562.7 14.0 %all_gather.60 = f32[1,12,8,128]{3,0,1,2:T(1,128)} all-gather(f32[1,12,2,128]{3,0,1,2:T(1,128)S(1)} %copy.183), channel_id=1, replica_groups=mesh['batch'=8,'ctx'=4] {'ctx'}, dimensions={2}, use_global_device_ids=true | all-gather | bytes 61440 | tf_op jit(solution)/shard_map/all_gather | solution.py:174
  576.8 15.1 %all_gather.61 = f32[1,12,8,128]{3,0,1,2:T(1,128)} all-gather(f32[1,12,2,128]{3,0,1,2:T(1,128)S(1)} %copy.184), channel_id=1, replica_groups=mesh['batch'=8,'ctx'=4] {'ctx'}, dimensions={2}, use_global_device_ids=true | all-gather | bytes 61440 | tf_op jit(solution)/shard_map/all_gather | solution.py:175
  591.8 59.9 %all-gather.26.cloned.1.call-done = bf16[3072,768]{0,1:T(8,128)(2,1)} async-done(((bf16[3072,192]{0,1:T(8,128)(2,1)}), bf16[3072,768]{0,1:T(8,128)(2,1)}) %all-gather.26.cloned.1.call-update) | async-done | bytes 4718608 | tf_op jit(solution)/shard_map/all_gather | solution.py:95
  651.7 7.6 convert_reduce_fusion
  659.3 5.1 multiply_reduce_fusion
  669.7 53.5 %while.62 = (s32[]{:T(128)}, f32[1,256,12,64]{1,3,2,0:T(8,128)}, bf16[1,8,128,768]{2,1,3,0:T(8,128)(2,1)}, s32[256]{0:T(256)}, bf16[1,256,12,64]{1,3,2,0:T(8,128...) while((s32[]{:T(128)}, f32[1,256,12,64]{1,3,2,0:T(8,128)}, ...), condition=%wide.region_13.14_spmd.clone, body=%wide.region_12.13_spmd.clone.sunk | while | flops 307954176 | bytes 13149437 | solution.py:197
  669.7 3.5 constant_dynamic-slice_fusion.18
  679.3 3.6 fusion.142
  682.9 3.5 constant_dynamic-slice_fusion.18
  692.4 3.9 fusion.142
  696.3 3.6 constant_dynamic-slice_fusion.18
  705.9 3.9 fusion.142
  709.8 3.5 constant_dynamic-slice_fusion.18
  719.4 3.9 fusion.142
  724.0 13.8 %all_gather.63 = f32[1,12,8,128]{3,0,1,2:T(1,128)} all-gather(f32[1,12,2,128]{3,0,1,2:T(1,128)S(1)} %copy.187), channel_id=1, replica_groups=mesh['batch'=8,'ctx'=4] {'ctx'}, dimensions={2}, use_global_device_ids=true | all-gather | bytes 61440 | tf_op jit(solution)/shard_map/all_gather | solution.py:176
  737.8 2.5 convert_reduce_fusion.4
  740.3 3.1 fusion.79
  743.9 68.8 %while.63 = (s32[]{:T(128)}, f32[1,256,12,64]{1,3,2,0:T(8,128)}, f32[1,256,12,64]{1,3,2,0:T(8,128)}, bf16[1,8,128,768]{3,2,0,1:T(8,128)(2,1)}, s32[256]{0:T(256)...) while((s32[]{:T(128)}, f32[1,256,12,64]{1,3,2,0:T(8,128)}, ...), condition=%wide.region_15.16_spmd.clone, body=%wide.region_14.15_spmd.clone.sunk | while | flops 409797120 | bytes 21738812 | solution.py:232
  750.1 2.4 exponential_divide_fusion.2
  757.0 3.0 fusion.150
  766.2 2.4 exponential_divide_fusion.2
  771.9 2.4 fusion.151
  774.3 3.2 fusion.150
  783.8 2.4 exponential_divide_fusion.2
  789.4 2.4 fusion.151
  791.9 3.2 fusion.150
  801.3 2.4 exponential_divide_fusion.2
  806.9 2.4 fusion.151
  809.4 3.2 fusion.150
  815.7 5.0 fusion.54
  822.4 6.0 fusion.66
  832.6 3.2 fusion.68
  841.9 101.0 %reduce-scatter.16.cloned.1.call-done = f32[768,576]{0,1:T(8,128)} async-done(((f32[768,2304]{0,1:T(8,128)}), f32[768,576]{0,1:T(8,128)}) %reduce-scatter.16.cloned.1.call-update) | async-done | bytes 1769488 | tf_op jit(solution)/shard_map/reduce_scatter | solution.py:264
  942.9 2.9 copy.217
  945.8 161.2 %reduce-scatter.20.cloned.1.call-done = f32[768,768]{1,0:T(8,128)} async-done(((f32[768,3072]{1,0:T(8,128)}), f32[768,768]{1,0:T(8,128)}) %reduce-scatter.20.cloned.1.call-update) | async-done | bytes 2359312 | tf_op jit(solution)/shard_map/reduce_scatter | solution.py:266
  1109.7 6.1 fusion.49
  1117.2 13.5 %reduce-scatter.32.cloned.1.call-done = f32[192,12]{1,0:T(8,128)} async-done(((f32[768,12]{1,0:T(8,128)}), f32[192,12]{1,0:T(8,128)}) %reduce-scatter.32.cloned.1.call-update) | async-done | bytes 9232
  1131.7 22.8 %psum.7 = f32[12,192]{1,0:T(8,128)S(1)} all-reduce(f32[12,192]{1,0:T(8,128)S(1)} %copy.222), channel_id=1, replica_groups=mesh['batch'=8,'ctx'=4] {'batch'}, use_global_device_ids=true, to_apply=%region_36.37 | all-reduce | flops 2304 | bytes 18432 | tf_op jit(solution)/shard_map/psum | solution.py:276
  1155.1 11.8 reduce-scatter.30.cloned.1.call-done
  1170.2 40.3 %reduce-scatter.28.cloned.1.call-done = f32[96,576]{1,0:T(8,128)} async-done(((f32[768,576]{1,0:T(8,128)}), f32[96,576]{1,0:T(8,128)}) %reduce-scatter.28.cloned.1.call-update) | async-done | bytes 221200
  1214.5 42.3 %reduce-scatter.22.cloned.1.call-done = f32[96,768]{1,0:T(8,128)} async-done(((f32[768,768]{1,0:T(8,128)}), f32[96,768]{1,0:T(8,128)}) %reduce-scatter.22.cloned.1.call-update) | async-done | bytes 294928 | tf_op jit(solution)/shard_map/reduce_scatter | solution.py:273
  (434 shorter events, 165.0 us)
Async XLA Ops:
  7.2 14.8 %copy-start.23 = (f32[96,768]{1,0:T(8,128)S(1)}, f32[96,768]{1,0:T(8,128)}, u32[]{:S(2)}) copy-start(f32[96,768]{1,0:T(8,128)} %param.29) | copy-start | bytes 884740
  7.2 15.5 %copy-start.39 = (f32[12,192]{1,0:T(8,128)S(1)}, f32[12,192]{1,0:T(8,128)}, u32[]{:S(2)}) copy-start(f32[12,192]{1,0:T(8,128)} %param.31) | copy-start | bytes 27652
  7.2 29.7 %copy-start.1 = (bf16[1,2,128,768]{3,2,1,0:T(8,128)(2,1)S(1)}, bf16[1,2,128,768]{3,2,1,0:T(8,128)(2,1)}, u32[]{:S(2)}) copy-start(bf16[1,2,128,768]{3,2,1,0:T(8,128)(2,1)} %param.25) | copy-start | bytes 1179652
  7.2 85.2 %all-gather.12.cloned.1.call-start = ((), (), s32[]{:S(2)}) async-start(), calls=%async_computation.9 | async-start | bytes 4423680 | tf_op jit(solution)/shard_map/all_gather | solution.py:92
  21.9 95.8 %all-gather.20.cloned.1.call-start = ((), (), s32[]{:S(2)}) async-start(), calls=%async_computation.13 | async-start | bytes 1327104 | tf_op jit(solution)/shard_map/all_gather | solution.py:88
  22.7 133.8 %all-gather.16.cloned.1.call-start = ((), (), s32[]{:S(2)}) async-start(), calls=%async_computation.11 | async-start | bytes 1966080 | tf_op jit(solution)/shard_map/all_gather | solution.py:114
  36.9 55.5 %copy-start.37 = (f32[768]{0:T(1024)}, f32[768]{0:T(1024)S(1)}, u32[]{:S(2)}) copy-start(f32[768]{0:T(1024)S(1)} %get-tuple-element.1001) | copy-start | bytes 9220
  37.1 55.4 %copy-start.44 = (f32[256]{0:T(256)}, f32[256]{0:T(256)S(1)}, u32[]{:S(2)}) copy-start(f32[256]{0:T(256)S(1)} %get-tuple-element.1118) | copy-start | bytes 3076
  37.3 55.1 %copy-start.60 = (f32[2,128]{1,0:T(2,128)}, f32[2,128]{1,0:T(2,128)S(1)}, u32[]{:S(2)}) copy-start(f32[2,128]{1,0:T(2,128)S(1)} %multiply_reduce_fusion.5) | copy-start | bytes 3076
  37.4 55.1 %copy-start.47 = (f32[256]{0:T(256)}, f32[256]{0:T(256)S(1)}, u32[]{:S(2)}) copy-start(f32[256]{0:T(256)S(1)} %bitcast_rsqrt_fusion) | copy-start | bytes 3076
  37.6 58.0 %copy-start.12 = (bf16[256,768]{1,0:T(8,128)(2,1)}, bf16[256,768]{1,0:T(8,128)(2,1)S(1)}, u32[]{:S(2)}) copy-start(bf16[256,768]{1,0:T(8,128)(2,1)S(1)} %add_convert_fusion.1) | copy-start | bytes 1179652
  96.4 102.7 %all-gather.14.cloned.1.call-start = ((), (), s32[]{:S(2)}) async-start(), calls=%async_computation.10 | async-start | bytes 1966080 | tf_op jit(solution)/shard_map/all_gather | solution.py:115
  97.3 62.1 %copy-start.13 = (bf16[256,768]{1,0:T(8,128)(2,1)}, bf16[256,768]{1,0:T(8,128)(2,1)S(1)}, u32[]{:S(2)}) copy-start(bf16[256,768]{1,0:T(8,128)(2,1)S(1)} %get-tuple-element.1115) | copy-start | bytes 1179652
  97.4 129.4 %all-gather.18.cloned.1.call-start = ((), (), s32[]{:S(2)}) async-start(), calls=%async_computation.12 | async-start | bytes 1474560 | tf_op jit(solution)/shard_map/all_gather | solution.py:93
  108.4 207.3 %all-gather.22.cloned.1.call-start = ((), (), s32[]{:S(2)}) async-start(), calls=%async_computation.14 | async-start | bytes 5898240 | tf_op jit(solution)/shard_map/all_gather | solution.py:94
  117.8 368.7 %reduce-scatter.24.cloned.1.call-start = ((), (), s32[]{:S(2)}) async-start(), calls=%async_computation.23 | async-start | bytes 11796480 | tf_op jit(solution)/shard_map/reduce_scatter | solution.py:267
  202.1 24.7 %copy-start.2 = (bf16[1,2,128,768]{3,2,1,0:T(8,128)(2,1)S(1)}, bf16[1,2,128,768]{3,2,1,0:T(8,128)(2,1)}, u32[]{:S(2)}) copy-start(bf16[1,2,128,768]{3,2,1,0:T(8,128)(2,1)} %param.25) | copy-start | bytes 1179652
  202.1 24.7 %copy-start.50 = (f32[768]{0:T(1024)S(1)}, f32[768]{0:T(1024)}, u32[]{:S(2)}) copy-start(f32[768]{0:T(1024)} %get-tuple-element.997) | copy-start | bytes 9220
  226.7 89.1 %copy-start.32 = (f32[768]{0:T(1024)S(1)}, f32[768]{0:T(1024)}, u32[]{:S(2)}) copy-start(f32[768]{0:T(1024)} %get-tuple-element.994) | copy-start | bytes 9220
  226.7 89.0 %copy-start.34 = (f32[768]{0:T(1024)S(1)}, f32[768]{0:T(1024)}, u32[]{:S(2)}) copy-start(f32[768]{0:T(1024)} %get-tuple-element.996) | copy-start | bytes 9220
  226.7 89.0 %copy-start.57 = (f32[3072]{0:T(1024)S(1)}, f32[3072]{0:T(1024)}, u32[]{:S(2)}) copy-start(f32[3072]{0:T(1024)} %add.491) | copy-start | bytes 36868
  226.8 92.8 %copy-start.15 = (bf16[1,256,12,64]{1,3,2,0:T(8,128)(2,1)}, bf16[1,256,12,64]{1,3,2,0:T(8,128)(2,1)S(1)}, u32[]{:S(2)}) copy-start(bf16[1,256,12,64]{1,3,2,0:T(8,128)(2,1)S(1)} %convert_element_type.135) | copy-start | bytes 1179652
  228.8 435.6 %copy-start.4 = (f32[256,768]{1,0:T(8,128)}, f32[256,768]{1,0:T(8,128)S(1)}, u32[]{:S(2)}) copy-start(f32[256,768]{1,0:T(8,128)S(1)} %get-tuple-element.1121) | copy-start | bytes 2359300
  228.8 435.6 %copy-start.42 = (f32[256]{0:T(256)}, f32[256]{0:T(256)S(1)}, u32[]{:S(2)}) copy-start(f32[256]{0:T(256)S(1)} %broadcast_multiply_fusion) | copy-start | bytes 3076
  229.1 435.4 %copy-start.54 = (f32[256]{0:T(256)}, f32[256]{0:T(256)S(1)}, u32[]{:S(2)}) copy-start(f32[256]{0:T(256)S(1)} %fusion.61) | copy-start | bytes 3076
  315.7 5.6 copy-start.8
  326.6 206.6 %copy-start.28 = (f32[384,192]{0,1:T(8,128)S(1)}, f32[384,192]{0,1:T(8,128)}, u32[]{:S(2)}) copy-start(f32[384,192]{0,1:T(8,128)} %param.30) | copy-start | bytes 884740
  326.6 233.4 %copy-start.14 = (bf16[256,768]{1,0:T(8,128)(2,1)S(1)}, bf16[256,768]{1,0:T(8,128)(2,1)}, u32[]{:S(2)}) copy-start(bf16[256,768]{1,0:T(8,128)(2,1)} %get-tuple-element.1116) | copy-start | bytes 1179652
  326.6 206.6 %reduce-scatter.26.cloned.1.call-start = ((), (), s32[]{:S(2)}) async-start(), calls=%async_computation.24 | async-start | bytes 2654208 | tf_op jit(solution)/shard_map/reduce_scatter | solution.py:274
  486.5 74.5 %copy-start.16 = (bf16[256,768]{1,0:T(8,128)(2,1)S(1)}, bf16[256,768]{1,0:T(8,128)(2,1)}, u32[]{:S(2)}) copy-start(bf16[256,768]{1,0:T(8,128)(2,1)} %slice.78) | copy-start | bytes 1179652
  486.5 73.4 %all-gather.24.cloned.1.call-start = ((), (), s32[]{:S(2)}) async-start(), calls=%async_computation.15 | async-start | bytes 1327104 | tf_op jit(solution)/shard_map/all_gather | solution.py:89
  535.4 116.3 %all-gather.26.cloned.1.call-start = ((), (), s32[]{:S(2)}) async-start(), calls=%async_computation.16 | async-start | bytes 5898240 | tf_op jit(solution)/shard_map/all_gather | solution.py:95
  560.0 183.9 %all-gather.28.cloned.1.call-start = ((), (), s32[]{:S(2)}) async-start(), calls=%async_computation.17 | async-start | bytes 1966080 | tf_op jit(solution)/shard_map/all_gather | solution.py:170
  561.9 181.9 %all-gather.30.cloned.1.call-start = ((), (), s32[]{:S(2)}) async-start(), calls=%async_computation.18 | async-start | bytes 1966080 | tf_op jit(solution)/shard_map/all_gather | solution.py:171
  659.3 5.1 copy-start.21
  669.7 169.9 %reduce-scatter.18.cloned.1.call-start = ((), (), s32[]{:S(2)}) async-start(), calls=%async_computation.20 | async-start | bytes 2949120 | tf_op jit(solution)/shard_map/reduce_scatter | solution.py:265
  743.5 199.3 %reduce-scatter.16.cloned.1.call-start = ((), (), s32[]{:S(2)}) async-start(), calls=%async_computation.19 | async-start | bytes 8847360 | tf_op jit(solution)/shard_map/reduce_scatter | solution.py:264
  746.5 6.0 copy-start
  762.6 6.0 copy-start
  780.2 6.0 copy-start
  797.7 6.0 copy-start
  820.8 286.2 %reduce-scatter.20.cloned.1.call-start = ((), (), s32[]{:S(2)}) async-start(), calls=%async_computation.21 | async-start | bytes 11796480 | tf_op jit(solution)/shard_map/reduce_scatter | solution.py:266
  828.5 4.0 copy-start.3
  828.6 302.2 %reduce-scatter.32.cloned.1.call-start = ((), (), s32[]{:S(2)}) async-start(), calls=%async_computation.27 | async-start | bytes 491520
  839.4 327.5 %reduce-scatter.30.cloned.1.call-start = ((), (), s32[]{:S(2)}) async-start(), calls=%async_computation.26 | async-start | bytes 884736
  841.8 265.3 %copy-start.25 = (f32[96,576]{1,0:T(8,128)S(1)}, f32[96,576]{1,0:T(8,128)}, u32[]{:S(2)}) copy-start(f32[96,576]{1,0:T(8,128)} %param.27) | copy-start | bytes 663556
  841.8 368.8 %reduce-scatter.28.cloned.1.call-start = ((), (), s32[]{:S(2)}) async-start(), calls=%async_computation.25 | async-start | bytes 2211840
  945.8 161.4 %copy-start.27 = (f32[96,192]{1,0:T(8,128)S(1)}, f32[96,192]{1,0:T(8,128)}, u32[]{:S(2)}) copy-start(f32[96,192]{1,0:T(8,128)} %param.28) | copy-start | bytes 221188
  945.8 161.6 %copy-start.31 = (f32[96,576]{1,0:T(8,128)S(1)}, f32[96,576]{1,0:T(8,128)}, u32[]{:S(2)}) copy-start(f32[96,576]{1,0:T(8,128)} %param.32) | copy-start | bytes 663556
  945.8 162.8 %copy-start.36 = (f32[96,192]{1,0:T(8,128)S(1)}, f32[96,192]{1,0:T(8,128)}, u32[]{:S(2)}) copy-start(f32[96,192]{1,0:T(8,128)} %param.34) | copy-start | bytes 221188
  945.8 163.9 %copy-start.65 = (f32[768]{0:T(1024)S(1)}, f32[768]{0:T(1024)}, u32[]{:S(2)}) copy-start(f32[768]{0:T(1024)} %get-tuple-element.995) | copy-start | bytes 9220
  945.8 311.0 %reduce-scatter.22.cloned.1.call-start = ((), (), s32[]{:S(2)}) async-start(), calls=%async_computation.22 | async-start | bytes 2654208 | tf_op jit(solution)/shard_map/reduce_scatter | solution.py:273
  1109.7 6.2 copy-start.64
  1109.7 6.2 copy-start.7
  1109.7 6.2 copy-start.46
  1109.7 6.2 copy-start.49
  1109.7 6.2 copy-start.59
  1109.7 6.2 copy-start.63
  1115.9 38.6 %copy-start.40 = (f32[12,192]{1,0:T(8,128)S(1)}, f32[12,192]{1,0:T(8,128)}, u32[]{:S(2)}) copy-start(f32[12,192]{1,0:T(8,128)} %param.31) | copy-start | bytes 27652
  1115.9 38.6 %copy-start.52 = (f32[12,192]{1,0:T(8,128)S(1)}, f32[12,192]{1,0:T(8,128)}, u32[]{:S(2)}) copy-start(f32[12,192]{1,0:T(8,128)} %param.41) | copy-start | bytes 27652
  1115.9 38.6 %copy-start.53 = (f32[12,192]{1,0:T(8,128)S(1)}, f32[12,192]{1,0:T(8,128)}, u32[]{:S(2)}) copy-start(f32[12,192]{1,0:T(8,128)} %param.40) | copy-start | bytes 27652
  1117.2 139.6 %copy-start.24 = (f32[96,768]{1,0:T(8,128)S(1)}, f32[96,768]{1,0:T(8,128)}, u32[]{:S(2)}) copy-start(f32[96,768]{1,0:T(8,128)} %param.29) | copy-start | bytes 884740
  1117.2 139.6 %copy-start.29 = (f32[96,768]{1,0:T(8,128)S(1)}, f32[96,768]{1,0:T(8,128)}, u32[]{:S(2)}) copy-start(f32[96,768]{1,0:T(8,128)} %param.37) | copy-start | bytes 884740
  1117.2 139.6 %copy-start.30 = (f32[96,768]{1,0:T(8,128)S(1)}, f32[96,768]{1,0:T(8,128)}, u32[]{:S(2)}) copy-start(f32[96,768]{1,0:T(8,128)} %param.36) | copy-start | bytes 884740
  (26 other events, 60.8 us)
Sparse Core Ops, SparseCore 0:
  22.0 70.3 all-gather.11
  94.9 22.7 all-gather.19
  119.3 37.0 all-gather.15
  158.4 35.9 all-gather.13
  196.4 29.2 all-gather.17
  227.2 88.5 all-gather.21
  326.7 159.7 reduce-scatter.23
  489.8 43.3 reduce-scatter.25
  535.8 24.1 all-gather.23
  561.4 90.2 all-gather.25
  653.4 35.5 all-gather.27
  690.5 35.9 all-gather.29
  743.6 46.3 reduce-scatter.17
  821.0 121.8 reduce-scatter.15
  945.2 161.7 reduce-scatter.19
  1109.3 21.4 reduce-scatter.31
  1133.7 33.2 reduce-scatter.29
  1170.2 40.3 reduce-scatter.27
  1214.3 42.4 reduce-scatter.21
where the time goes:
time: 1270 us
  waiting for transfers between devices  849 us (67%)
  local copies, waits for them, and re-layouts  126 us (10%)
  matrix products  121 us (10%)
  blocking collectives  102 us (8%)
  other arithmetic  51.5 us (4%)
  between operations  15.4 us (1%)
    reduce_scatter x1, waiting for transfers between devices, local(): lax.psum_scatter(grad_wfc, 'ctx', scatter_dimension=1, tiled=True)  161 us
    reduce_scatter x1, waiting for transfers between devices, local(): lax.psum_scatter(grad_wproj, 'ctx', scatter_dimension=1, tiled=True)  160 us
    reduce_scatter x1, waiting for transfers between devices, local(): lax.psum_scatter(grad_wqkv, 'ctx', scatter_dimension=1, tiled=True)  101 us
    all_gather x1, waiting for transfers between devices, local(): lax.all_gather(row_parts[2], 'ctx', axis=1, tiled=True)  86.7 us
    unnamed x22, waiting for transfers between devices  66 us
    all_gather x1, waiting for transfers between devices, local(): lax.all_gather(row_parts[3], 'ctx', axis=1, tiled=True)  59.9 us
    all_gather x1, waiting for transfers between devices, local(): lax.all_gather(row_parts[0], 'ctx', axis=1, tiled=True)  54.8 us
    dynamic_slice x24, local copies, waits for them, and re-layouts, piece_of(): lax.dynamic_slice_in_dim(source, 2 * piece, 2, 1)  49.7 us
  transfers between devices with their start and end apart: 19, of which 14 were waited for; matrix products, arithmetic and copies ran while one was open for 22% of the time, Pallas kernels for 0%

commit v1 on v0

--- a/solution.py
+++ b/solution.py
@@ -1,8 +1,11 @@
+import functools
 import math
 
 import jax
 import jax.numpy as jnp
 from jax import lax
+from jax.experimental import pallas as pl
+from jax.experimental.pallas import tpu as pltpu
 from jax.sharding import PartitionSpec as P
 
 HEADS = 12
@@ -61,7 +64,7 @@
     return (first, second, weight)
 
 
-def local(
+def local_any(
     block_in,
     cotangent,
     w_qkv,
@@ -300,6 +303,606 @@
     )
 
 
+BATCH = 8
+CTX = 4
+WIDTH = 768
+HEAD = 64
+GROUP = WIDTH // CTX
+TOKENS = 256
+HALF = 128
+FF_SIDE = 384
+SPAN = TOKENS * CTX
+TILE = 256
+LOW = jnp.bfloat16
+WIDE = jnp.float32
+CORE, XBIT, YBIT = 1, 2, 4
+SOURCES = (0, 0, 2, 2, 4, 4, 6, 6, 1, 1, 3, 3, 5, 5, 7, 7)
+VMEM_LIMIT = 56 * 1024 * 1024
+
+
+def swap(value, axis, bit):
+    size = BATCH if axis == "batch" else CTX
+    return lax.ppermute(value, axis, [(i, i ^ bit) for i in range(size)])
+
+
+def mm(left, right):
+    return lax.dot_general(left, right, (((1,), (0,)), ((), ())), preferred_element_type=WIDE)
+
+
+def mt(left, right):
+    return lax.dot_general(left, right, (((1,), (1,)), ((), ())), preferred_element_type=WIDE)
+
+
+def tm(left, right):
+    return lax.dot_general(left, right, (((0,), (0,)), ((), ())), preferred_element_type=WIDE)
+
+
+def turned(value):
+    return value.astype(WIDE).T.astype(LOW)
+
+
+def moments(value):
+    mean = jnp.mean(value, axis=-1, keepdims=True)
+    centred = value - mean
+    spread = jnp.mean(centred * centred, axis=-1, keepdims=True)
+    return centred, lax.rsqrt(spread + 1e-05)
+
+
+def norm_back(grad, normed, inverse, gain):
+    part = grad * gain
+    mean = jnp.mean(part, axis=-1, keepdims=True)
+    cross = jnp.mean(part * normed, axis=-1, keepdims=True)
+    return inverse * (part - mean - normed * cross)
+
+
+def gather_weight(piece):
+    near, far, last = swap(piece, "ctx", 1), swap(piece, "ctx", 2), swap(piece, "ctx", 3)
+    one, two = jnp.stack([piece, near]), jnp.stack([far, last])
+    one_x, two_y = swap(one, "batch", XBIT), swap(two, "batch", YBIT)
+    one_y, two_x = swap(one, "batch", YBIT), swap(two, "batch", XBIT)
+    one_xy, two_xy = swap(one_x, "batch", YBIT), swap(two_y, "batch", XBIT)
+    held = [one, two, one_x, two_x, one_y, two_y, one_xy, two_xy]
+    return held + [swap(part, "batch", CORE) for part in held]
+
+
+def scatter_grad(mine, theirs):
+    came = swap(theirs, "batch", CORE)
+    total = mine.astype(WIDE) + came.astype(WIDE)
+    total = total.reshape((2, 2) + total.shape[1:])
+    one, two = total[:, :, 0:2], total[:, :, 2:4]
+    one_back = swap(one[1].astype(LOW), "batch", YBIT)
+    two_back = swap(two[:, 1].astype(LOW), "batch", XBIT)
+    one = one[0] + one_back.astype(WIDE)
+    two = two[:, 0] + two_back.astype(WIDE)
+    one_back = swap(one[1].astype(LOW), "batch", XBIT)
+    two_back = swap(two[1].astype(LOW), "batch", YBIT)
+    one = one[0] + one_back.astype(WIDE)
+    two = two[0] + two_back.astype(WIDE)
+    near = swap(one[1].astype(LOW), "ctx", 1)
+    far = swap(two[0].astype(LOW), "ctx", 2)
+    last = swap(two[1].astype(LOW), "ctx", 3)
+    return one[0] + near.astype(WIDE) + (far.astype(WIDE) + last.astype(WIDE))
+
+
+def rows_place(held, batch, ctx):
+    size = WIDTH // BATCH
+    return held.at[ctx, pl.ds(pl.multiple_of(batch * size, 16), size), :]
+
+
+def columns_place(held, batch, ctx):
+    return held.at[batch, pl.ds(pl.multiple_of(ctx * GROUP, 16), GROUP), :]
+
+
+def load_weight(meta, parts, held, place, sems, lanes=None):
+    copies = []
+    for index, (part, source) in enumerate(zip(parts, SOURCES)):
+        for half in range(2):
+            ctx = meta[1] ^ (2 * (index % 2) + half)
+            origin = part.at[half] if lanes is None else part.at[half, :, lanes]
+            copy = pltpu.make_async_copy(
+                origin, place(held, meta[0] ^ source, ctx), sems.at[2 * index + half]
+            )
+            copy.start()
+            copies.append(copy)
+    return copies
+
+
+def store_grad(meta, held, place, mine, theirs, sems):
+    copies = []
+    for batch in range(BATCH):
+        for ctx in range(CTX):
+            target = theirs if batch % 2 else mine
+            copy = pltpu.make_async_copy(
+                place(held, meta[0] ^ batch, meta[1] ^ ctx),
+                target.at[batch // 2, ctx],
+                sems.at[batch * CTX + ctx],
+            )
+            copy.start()
+            copies.append(copy)
+    for copy in copies:
+        copy.wait()
+
+
+def wait_all(copies):
+    for copy in copies:
+        copy.wait()
+
+
+def in_place(ctx, block):
+    first = ctx if block == 0 else 2 * CTX - 1 - ctx
+    return pl.ds(pl.multiple_of(first * HALF, HALF), HALF)
+
+
+def qkv_kernel(meta, x_ref, vec_ref, bias_ref, *refs):
+    parts, (h_ref, own, near, far, last, held, units, sems) = refs[:16], refs[16:]
+    copies = load_weight(meta, parts, held, rows_place, sems)
+    centred, inverse = moments(x_ref[...].astype(WIDE))
+    normed = (centred * inverse * vec_ref[0:1] + vec_ref[1:2]).astype(LOW)
+    h_ref[...] = normed
+    wait_all(copies)
+    for chunk in range(CTX):
+        mixed = mm(normed, held[chunk, :, : 3 * GROUP]) + bias_ref[chunk]
+        mixed = mixed.astype(LOW)
+        for part in range(3):
+            unit = 3 * chunk + part
+            units[unit % CTX, :, (unit // CTX) * GROUP : (unit // CTX + 1) * GROUP] = mixed[
+                :, part * GROUP : (part + 1) * GROUP
+            ]
+    for ctx, target in enumerate((own, near, far, last)):
+        target[...] = units[meta[1] ^ ctx]
+
+
+def read_sequence(meta, pieces, targets):
+    for ctx, piece in enumerate(pieces):
+        for block in range(2):
+            place = in_place(meta[1] ^ ctx, block)
+            rows = piece[block * HALF : (block + 1) * HALF, :]
+            for index, target in enumerate(targets):
+                target[place, :] = rows[:, index * GROUP : (index + 1) * GROUP]
+
+
+def write_sequence(meta, pieces, sources):
+    for ctx, piece in enumerate(pieces):
+        for block in range(2):
+            place = in_place(meta[1] ^ ctx, block)
+            for index, source in enumerate(sources):
+                piece[
+                    block * HALF : (block + 1) * HALF, index * GROUP : (index + 1) * GROUP
+                ] = source[place, :].astype(LOW)
+
+
+def head_mask(head, scale=1.0):
+    lane = lax.broadcasted_iota(jnp.int32, (1, GROUP), 1)
+    inside = (lane >= head * HEAD) & (lane < (head + 1) * HEAD)
+    return jnp.where(inside, scale, 0.0).astype(LOW)
+
+
+def tile_of(index):
+    return slice(index * TILE, (index + 1) * TILE)
+
+
+def weights_of(queries, k_seq, tile, causal):
+    scores = [mt(queries, k_seq[tile_of(other), :]) for other in range(tile + 1)]
+    scores[tile] = jnp.where(causal, scores[tile], -1e30)
+    top = jnp.max(functools.reduce(jnp.maximum, scores), axis=-1, keepdims=True)
+    expo = [jnp.exp(score - top) for score in scores]
+    total = jnp.sum(functools.reduce(jnp.add, expo), axis=-1, keepdims=True)
+    inverse = 1.0 / total
+    return [value * inverse for value in expo]
+
+
+def causal_tile():
+    row = lax.broadcasted_iota(jnp.int32, (TILE, TILE), 0)
+    column = lax.broadcasted_iota(jnp.int32, (TILE, TILE), 1)
+    return row >= column
+
+
+def attend_kernel(meta, *refs):
+    pieces, results, (q_seq, k_seq, v_seq, out) = refs[:4], refs[4:8], refs[8:]
+    read_sequence(meta, pieces, (q_seq, k_seq, v_seq))
+    causal = causal_tile()
+    scale = 1.0 / math.sqrt(HEAD)
+    for tile in range(SPAN // TILE):
+
+        def one_head(head, total, tile=tile):
+            mask = head_mask(head)
+            queries = q_seq[tile_of(tile), :] * head_mask(head, scale)
+            weights = weights_of(queries, k_seq, tile, causal)
+            for other, weight in enumerate(weights):
+                total = total + mm(weight.astype(LOW), v_seq[tile_of(other), :] * mask)
+            return total
+
+        out[tile_of(tile), :] = lax.fori_loop(
+            0, GROUP // HEAD, one_head, jnp.zeros((TILE, GROUP), WIDE)
+        )
+    write_sequence(meta, results, (out,))
+
+
+def attend_back_kernel(meta, *refs):
+    pieces, grads, results = refs[:4], refs[4:8], refs[8:12]
+    q_seq, k_seq, v_seq, g_seq, dq, dk, dv = refs[12:]
+    read_sequence(meta, pieces, (q_seq, k_seq, v_seq))
+    read_sequence(meta, grads, (g_seq,))
+    causal = causal_tile()
+    scale = 1.0 / math.sqrt(HEAD)
+    dk[...] = jnp.zeros_like(dk)
+    dv[...] = jnp.zeros_like(dv)
+    for tile in range(SPAN // TILE):
+
+        def one_head(head, total, tile=tile):
+            mask = head_mask(head)
+            scaled = head_mask(head, scale)
+            queries = q_seq[tile_of(tile), :] * scaled
+            grad = g_seq[tile_of(tile), :] * mask
+            weights = weights_of(queries, k_seq, tile, causal)
+            backs = [mt(grad, v_seq[tile_of(other), :]) for other in range(tile + 1)]
+            products = [weight * back for weight, back in zip(weights, backs)]
+            delta = jnp.sum(functools.reduce(jnp.add, products), axis=-1, keepdims=True)
+            for other, (weight, back) in enumerate(zip(weights, backs)):
+                step = (weight * (back - delta)).astype(LOW)
+                total = total + mm(step, k_seq[tile_of(other), :] * scaled)
+                dk[tile_of(other), :] += tm(step, queries)
+                dv[tile_of(other), :] += tm(weight.astype(LOW), grad)
+            return total
+
+        dq[tile_of(tile), :] = lax.fori_loop(
+            0, GROUP // HEAD, one_head, jnp.zeros((TILE, GROUP), WIDE)
+        )
+    write_sequence(meta, results, (dq, dk, dv))
+
+
+def middle_kernel(meta, x_ref, dy_ref, vec_ref, bias_ref, *refs):
+    pieces, refs = refs[:4], refs[4:]
+    parts_one, parts_two, parts_three, refs = refs[:16], refs[16:32], refs[32:48], refs[48:]
+    (out_ref, att_ref, h_ref, act_ref, dpre_ref, datt_ref, dmid_ref), refs = refs[:7], refs[7:]
+    results, (rows_ref, dbias_ref), refs = refs[:4], refs[4:6], refs[6:]
+    out_parts, held_out, held_fc, held_proj, units, total, back, sem_one, sem_two, sem_three = refs
+    lanes = pl.ds(2 * TILE, TILE)
+    copies_one = load_weight(meta, parts_one, out_parts, rows_place, sem_one, lanes)
+    copies_two = load_weight(meta, parts_two, held_fc, rows_place, sem_two)
+    copies_three = load_weight(meta, parts_three, held_proj, columns_place, sem_three)
+    for ctx, piece in enumerate(pieces):
+        units[meta[1] ^ ctx] = piece[...]
+    att = jnp.concatenate([units[index] for index in range(CTX)], axis=1)
+    att_ref[...] = att
+    wait_all(copies_one)
+    for chunk in range(CTX):
+        held_out[:, chunk * GROUP : (chunk + 1) * GROUP] = out_parts[chunk, :, TILE - GROUP :]
+    mid = x_ref[...].astype(WIDE) + mm(att, held_out[...]) + vec_ref[6:7]
+    centred, inverse = moments(mid)
+    normed = centred * inverse
+    h_ref[...] = (normed * vec_ref[2:3] + vec_ref[3:4]).astype(LOW)
+    total[...] = mid + vec_ref[7:8]
+    back[...] = jnp.zeros_like(back)
+    wait_all(copies_two)
+    wait_all(copies_three)
+    side = FF_SIDE
+
+    def chunk_step(chunk, carry):
+        pre = mm(h_ref[...], held_fc[chunk]) + bias_ref[chunk]
+        square = pre * pre
+        tanh = jnp.tanh(0.7978845608028654 * (pre + 0.044715 * square * pre))
+        act = (0.5 * pre * (1.0 + tanh)).astype(LOW)
+        slope = 0.5 * (1.0 + tanh) + 0.5 * pre * (1.0 - tanh * tanh) * (
+            0.7978845608028654 * (1.0 + 3.0 * 0.044715 * square)
+        )
+        act_ref[chunk] = act
+        grads = []
+        for half in range(2):
+            weight = held_proj[2 * chunk + half]
+            total[...] += mt(act[:, half * side : (half + 1) * side], weight)
+            grads.append(mm(dy_ref[...], weight))
+        dpre = (jnp.concatenate(grads, axis=1) * slope).astype(LOW)
+        dpre_ref[chunk] = dpre
+        dbias_ref[chunk] = jnp.sum(dpre.astype(WIDE), axis=0, keepdims=True)
+        back[...] += mt(dpre, held_fc[chunk])
+        return carry
+
+    lax.fori_loop(0, CTX, chunk_step, 0)
+    out_ref[...] = total[...].astype(LOW)
+    grad = back[...]
+    dy = dy_ref[...].astype(WIDE)
+    dmid = dy + norm_back(grad, normed, inverse, vec_ref[2:3])
+    dmid_ref[...] = dmid
+    datt = dmid.astype(LOW)
+    datt_ref[...] = datt
+    rows_ref[0:1] = jnp.sum(grad * normed, axis=0, keepdims=True)
+    rows_ref[1:2] = jnp.sum(grad, axis=0, keepdims=True)
+    rows_ref[2:3] = jnp.sum(datt.astype(WIDE), axis=0, keepdims=True)
+    rows_ref[3:4] = jnp.sum(dy, axis=0, keepdims=True)
+    rows_ref[4:8] = jnp.zeros((4, WIDTH), WIDE)
+    dout = mt(datt, held_out[...]).astype(LOW)
+    for index in range(CTX):
+        units[index] = dout[:, index * GROUP : (index + 1) * GROUP]
+    for ctx, target in enumerate(results):
+        target[...] = units[meta[1] ^ ctx]
+
+
+def proj_grad_kernel(meta, dy_ref, act_ref, mine, theirs, held, sems):
+    left = turned(dy_ref[...])
+    for chunk in range(CTX):
+        for half in range(2):
+            held[2 * chunk + half] = mm(
+                left, act_ref[chunk, :, half * FF_SIDE : (half + 1) * FF_SIDE]
+            ).astype(LOW)
+    store_grad(meta, held, columns_place, mine, theirs, sems)
+
+
+def fc_grad_kernel(meta, h_ref, dpre_ref, mine, theirs, held, sems):
+    left = turned(h_ref[...])
+    for chunk in range(CTX):
+        held[chunk] = mm(left, dpre_ref[chunk]).astype(LOW)
+    store_grad(meta, held, rows_place, mine, theirs, sems)
+
+
+def qkv_grad_kernel(meta, h_ref, att_ref, datt_ref, *refs):
+    pieces, (mine, theirs, mixed_ref, dbias_ref, held, units, sems) = refs[:4], refs[4:]
+    for ctx, piece in enumerate(pieces):
+        for part in range(3):
+            units[CTX * part + (meta[1] ^ ctx)] = piece[:, part * GROUP : (part + 1) * GROUP]
+    left, att = turned(h_ref[...]), turned(att_ref[...])
+    for chunk in range(CTX):
+        mixed = jnp.concatenate([units[3 * chunk + part] for part in range(3)], axis=1)
+        mixed_ref[chunk] = mixed
+        dbias_ref[chunk] = jnp.sum(mixed.astype(WIDE), axis=0, keepdims=True)
+        held[chunk, :, : 3 * GROUP] = mm(left, mixed).astype(LOW)
+        held[chunk, :, 3 * GROUP :] = mm(
+            att, datt_ref[:, chunk * GROUP : (chunk + 1) * GROUP]
+        ).astype(LOW)
+    store_grad(meta, held, rows_place, mine, theirs, sems)
+
+
+def input_grad_kernel(meta, x_ref, vec_ref, dmid_ref, mixed_ref, *refs):
+    parts, (grad_ref, rows_ref, held, sems) = refs[:16], refs[16:]
+    copies = load_weight(meta, parts, held, rows_place, sems)
+    centred, inverse = moments(x_ref[...].astype(WIDE))
+    normed = centred * inverse
+    wait_all(copies)
+    grad = jnp.zeros((TOKENS, WIDTH), WIDE)
+    for chunk in range(CTX):
+        grad = grad + mt(mixed_ref[chunk], held[chunk, :, : 3 * GROUP])
+    grad_ref[...] = dmid_ref[...] + norm_back(grad, normed, inverse, vec_ref[0:1])
+    rows_ref[0:1] = jnp.sum(grad * normed, axis=0, keepdims=True)
+    rows_ref[1:2] = jnp.sum(grad, axis=0, keepdims=True)
+    rows_ref[2:8] = jnp.zeros((6, WIDTH), WIDE)
+
+
+def shape_of(dtype, *dims):
+    return jax.ShapeDtypeStruct(dims, dtype)
+
+
+def call(kernel, arguments, kinds, outputs, out_kinds, scratch, flops):
+    spec = {
+        "v": pl.BlockSpec(memory_space=pltpu.VMEM),
+        "s": pl.BlockSpec(memory_space=pltpu.SMEM),
+        "a": pl.BlockSpec(memory_space=pl.ANY),
+    }
+    moved = sum(math.prod(value.shape) * value.dtype.itemsize for value in arguments)
+    moved += sum(math.prod(value.shape) * value.dtype.itemsize for value in outputs)
+    return pl.pallas_call(
+        kernel,
+        out_shape=tuple(outputs),
+        in_specs=[spec[kind] for kind in kinds],
+        out_specs=tuple(spec[kind] for kind in out_kinds),
+        scratch_shapes=scratch,
+        cost_estimate=pl.CostEstimate(
+            flops=int(flops), bytes_accessed=int(moved), transcendentals=0
+        ),
+        compiler_params=pltpu.CompilerParams(vmem_limit_bytes=VMEM_LIMIT),
+    )(*arguments)
+
+
+def local_fast(
+    block_in,
+    cotangent,
+    w_qkv,
+    w_out,
+    w_fc,
+    w_proj,
+    vectors,
+    qkv_first,
+    qkv_second,
+    out_first,
+    out_second,
+    fc_first,
+    fc_second,
+    proj_first,
+    proj_second,
+    vec_first,
+    vec_second,
+):
+    batch, ctx = lax.axis_index("batch"), lax.axis_index("ctx")
+    meta = jnp.stack([batch, ctx]).astype(jnp.int32)
+    inputs = block_in.reshape(TOKENS, WIDTH)
+    grad_low = cotangent.reshape(TOKENS, WIDTH)
+    order = ctx ^ jnp.arange(CTX, dtype=jnp.int32)
+    rows = WIDTH // BATCH
+    dma = pltpu.SemaphoreType.DMA((BATCH * CTX,))
+    held_shape = pltpu.VMEM((CTX, WIDTH, WIDTH), LOW)
+    proj_shape = pltpu.VMEM((BATCH, WIDTH, FF_SIDE), LOW)
+
+    low_vec = vectors.astype(LOW)
+    vec_parts = jnp.stack([low_vec] + [swap(low_vec, "ctx", bit) for bit in (1, 2, 3)])
+    params = vec_parts[order].astype(WIDE).transpose(1, 0, 2).reshape(12, WIDTH)
+    qkv_bias = jnp.concatenate([params[4], jnp.zeros((WIDTH,), WIDE), params[5]])
+    qkv_bias = qkv_bias.reshape(CTX, 1, 3 * GROUP)
+    fc_bias = params[8:12].reshape(CTX, 1, WIDTH)
+
+    piece_one = jnp.concatenate([w_qkv.astype(LOW), w_out.astype(LOW)], axis=1)
+    parts_one = gather_weight(piece_one)
+    parts_two = gather_weight(w_fc.astype(LOW))
+    parts_three = gather_weight(w_proj.astype(LOW).T)
+
+    packed = shape_of(LOW, TOKENS, 3 * GROUP)
+    single = shape_of(LOW, TOKENS, GROUP)
+    square = WIDTH * WIDTH
+    h_one, own, *sent = call(
+        qkv_kernel,
+        (meta, inputs, params, qkv_bias, *parts_one),
+        "svvv" + "a" * 16,
+        [shape_of(LOW, TOKENS, WIDTH)] + [packed] * 4,
+        "v" * 5,
+        [held_shape, pltpu.VMEM((CTX, TOKENS, 3 * GROUP), LOW), dma],
+        2 * TOKENS * 3 * square,
+    )
+    qkv_pieces = [own] + [swap(part, "ctx", bit) for bit, part in zip((1, 2, 3), sent)]
+
+    sequence_low = pltpu.VMEM((SPAN, GROUP), LOW)
+    sequence_wide = pltpu.VMEM((SPAN, GROUP), WIDE)
+    own, *sent = call(
+        attend_kernel,
+        (meta, *qkv_pieces),
+        "s" + "v" * 4,
+        [single] * 4,
+        "v" * 4,
+        [sequence_low] * 3 + [sequence_wide],
+        2 * SPAN * SPAN * GROUP * 2,
+    )
+    att_pieces = [own] + [swap(part, "ctx", bit) for bit, part in zip((1, 2, 3), sent)]
+
+    tokens_low = shape_of(LOW, TOKENS, WIDTH)
+    hidden_low = shape_of(LOW, CTX, TOKENS, WIDTH)
+    out, att, h_two, act, dpre, datt, dmid, own, *sent = call(
+        middle_kernel,
+        (
+            meta,
+            inputs,
+            grad_low,
+            params,
+            fc_bias,
+            *att_pieces,
+            *parts_one,
+            *parts_two,
+            *parts_three,
+        ),
+        "svvvv" + "v" * 4 + "a" * 48,
+        [
+            tokens_low,
+            tokens_low,
+            tokens_low,
+            hidden_low,
+            hidden_low,
+            tokens_low,
+            shape_of(WIDE, TOKENS, WIDTH),
+        ]
+        + [single] * 4
+        + [shape_of(WIDE, 8, WIDTH), shape_of(WIDE, CTX, 1, WIDTH)],
+        "v" * 13,
+        [
+            pltpu.VMEM((CTX, WIDTH, TILE), LOW),
+            pltpu.VMEM((WIDTH, WIDTH), LOW),
+            held_shape,
+            proj_shape,
+            pltpu.VMEM((CTX, TOKENS, GROUP), LOW),
+            pltpu.VMEM((TOKENS, WIDTH), WIDE),
+            pltpu.VMEM((TOKENS, WIDTH), WIDE),
+            dma,
+            dma,
+            dma,
+        ],
+        2 * TOKENS * 18 * square,
+    )
+    sent, (rows_two, dbias_fc) = sent[:3], sent[3:]
+    grad_pieces = [own] + [swap(part, "ctx", bit) for bit, part in zip((1, 2, 3), sent)]
+
+    row_parts = [shape_of(LOW, BATCH // 2, CTX, rows, WIDTH)] * 2
+    column_parts = [shape_of(LOW, BATCH // 2, CTX, GROUP, FF_SIDE)] * 2
+    proj_parts = call(
+        proj_grad_kernel,
+        (meta, grad_low, act),
+        "svv",
+        column_parts,
+        "aa",
+        [proj_shape, dma],
+        2 * TOKENS * 4 * square,
+    )
+    proj_grad = scatter_grad(*proj_parts)
+    fc_parts = call(
+        fc_grad_kernel,
+        (meta, h_two, dpre),
+        "svv",
+        row_parts,
+        "aa",
+        [held_shape, dma],
+        2 * TOKENS * 4 * square,
+    )
+    fc_grad = scatter_grad(*fc_parts)
+
+    own, *sent = call(
+        attend_back_kernel,
+        (meta, *qkv_pieces, *grad_pieces),
+        "s" + "v" * 8,
+        [packed] * 4,
+        "v" * 4,
+        [sequence_low] * 4 + [sequence_wide] * 3,
+        2 * SPAN * SPAN * GROUP * 5,
+    )
+    mixed_pieces = [own] + [swap(part, "ctx", bit) for bit, part in zip((1, 2, 3), sent)]
+
+    mine, theirs, mixed, dbias_qkv = call(
+        qkv_grad_kernel,
+        (meta, h_one, att, datt, *mixed_pieces),
+        "svvv" + "v" * 4,
+        row_parts + [shape_of(LOW, CTX, TOKENS, 3 * GROUP), shape_of(WIDE, CTX, 1, 3 * GROUP)],
+        "aavv",
+        [held_shape, pltpu.VMEM((3 * CTX, TOKENS, GROUP), LOW), dma],
+        2 * TOKENS * 4 * square,
+    )
+    one_grad = scatter_grad(mine, theirs)
+    grad_input, rows_one = call(
+        input_grad_kernel,
+        (meta, inputs, params, dmid, mixed, *parts_one),
+        "svvvv" + "a" * 16,
+        [shape_of(WIDE, TOKENS, WIDTH), shape_of(WIDE, 8, WIDTH)],
+        "vv",
+        [held_shape, dma],
+        2 * TOKENS * 3 * square,
+    )
+
+    dbias_qkv = dbias_qkv.reshape(3, WIDTH)
+    vec_rows = jnp.concatenate(
+        [
+            rows_one[0:2],
+            rows_two[0:2],
+            dbias_qkv[0:1],
+            dbias_qkv[2:3],
+            rows_two[2:4],
+            dbias_fc.reshape(4, WIDTH),
+        ],
+        axis=0,
+    )
+    vec_rows = vec_rows.reshape(12, CTX, GROUP).transpose(1, 0, 2)[order]
+    vec_grad = vec_rows[0] + sum(swap(vec_rows[bit], "ctx", bit) for bit in (1, 2, 3))
+    for bit in (CORE, XBIT, YBIT):
+        vec_grad = vec_grad + swap(vec_grad, "batch", bit)
+
+    qkv_grad, out_grad = one_grad[:, : 3 * GROUP], one_grad[:, 3 * GROUP :]
+    qkv_m, qkv_s, qkv_w = adamw(w_qkv, qkv_grad, qkv_first, qkv_second, 0.06, 0.1)
+    out_m, out_s, out_w = adamw(w_out, out_grad, out_first, out_second, 0.06, 0.1)
+    fc_m, fc_s, fc_w = adamw(w_fc, fc_grad, fc_first, fc_second, 0.06, 0.1)
+    proj_m, proj_s, proj_w = adamw(w_proj, proj_grad.T, proj_first, proj_second, 0.06, 0.1)
+    vec_m, vec_s, vec_w = adamw(vectors, vec_grad, vec_first, vec_second, 0.2, 0.0)
+    return (
+        out.reshape(block_in.shape),
+        grad_input.reshape(block_in.shape),
+        qkv_m,
+        qkv_s,
+        qkv_w,
+        out_m,
+        out_s,
+        out_w,
+        fc_m,
+        fc_s,
+        fc_w,
+        proj_m,
+        proj_s,
+        proj_w,
+        vec_m,
+        vec_s,
+        vec_w,
+    )
+
+
 def solution(mesh):
     in_specs = (
         P("batch", "ctx", None, None),
@@ -339,4 +942,6 @@
         P(None, "ctx"),
         P(None, "ctx"),
     )
+    sizes = (mesh.shape["batch"], mesh.shape["ctx"])
+    local = local_fast if sizes == (BATCH, CTX) else local_any
     return jax.shard_map(local, mesh=mesh, in_specs=in_specs, out_specs=out_specs, check_vma=False)

time: 1270 us -> 397 us (0.31)
  waiting for transfers between devices: 849 us -> 156 us
  starting transfers between devices: 1.2 us -> 124 us
  matrix products: 121 us -> 0 us
  local copies, waits for them, and re-layouts: 126 us -> 16.2 us
  blocking collectives: 102 us -> 0 us
  Pallas kernels: 0 us -> 76.9 us
  other arithmetic: 51.5 us -> 20.7 us
  between operations: 15.4 us -> 1.77 us
    reduce_scatter x6 -> x0, waiting for transfers between devices: 511 us -> none  [the longest x1 161 us: local(): lax.psum_scatter(grad_wfc, 'ctx', scatter_dimension=1, tiled=True)]
    all_gather x10 -> x0, waiting for transfers between devices: 272 us -> none  [the longest x1 86.7 us: local(): lax.all_gather(row_parts[2], 'ctx', axis=1, tiled=True)]
    ppermute x0 -> x96, waiting for transfers between devices: none -> 156 us  [swap(): return lax.ppermute(value, axis, [(i, i ^ bit) for i in range(size)])]
    ppermute x0 -> x96, starting transfers between devices: none -> 124 us  [swap(): return lax.ppermute(value, axis, [(i, i ^ bit) for i in range(size)])]
    dot_general x40 -> x0, matrix products: 121 us -> none  [the longest x12 25.1 us: scores_of(): jnp.einsum('sqhd,skhd->shqk', queries, keys, preferred_element_type=jnp.f...]
    all_gather x6 -> x0, blocking collectives: 78.7 us -> none  [the longest x1 15.1 us: local(): lax.all_gather(total.reshape(seqs, heads, pair, half), 'ctx', axis=2, til...]
    pallas_call x0 -> x8, Pallas kernels: none -> 76.9 us  [call(): pl.pallas_call(kernel, out_shape=tuple(outputs), in_specs=[spec[kind] for...]
    unnamed x22 -> x0, waiting for transfers between devices: 66 us -> none
  transfers between devices with their start and end apart: 19 -> 96, of which waited for: 14 -> 38; matrix products, arithmetic and copies ran while one was open for 22% -> 8% of each run, Pallas kernels for 0% -> 14%
where the time goes in v1:
time: 397 us; the launch traced here: 396 us
  waiting for transfers between devices  156 us (39%)
  starting transfers between devices  124 us (31%)
  Pallas kernels  76.9 us (19%)
  other arithmetic  20.7 us (5%)
  local copies, waits for them, and re-layouts  16.2 us (4%)
    ppermute x96, waiting for transfers between devices, swap(): return lax.ppermute(value, axis, [(i, i ^ bit) for i in range(size)])  156 us
    ppermute x96, starting transfers between devices, swap(): return lax.ppermute(value, axis, [(i, i ^ bit) for i in range(size)])  124 us
    pallas_call x8, Pallas kernels, call(): pl.pallas_call(kernel, out_shape=tuple(outputs), in_specs=[spec[kind] for...  76.9 us
  transfers between devices with their start and end apart: 96, of which 38 were waited for; matrix products, arithmetic and copies ran while one was open for 8% of the time, Pallas kernels for 14%

profile of v1, /device:TPU:0, one launch (start us, length us, event | category | flops | bytes accessed | tf_op | source)
XLA Modules:
  0.0 396.0 jit_solution(10101737183263543674)
XLA Ops:
  1.7 4.1 %collective-permute-start.44 = (bf16[192,384]{1,0:T(8,128)(2,1)S(1)}, bf16[192,384]{1,0:T(8,128)(2,1)S(1)}, u32[]{:S(2)}, u32[]{:S(2)}) collective-permute-start(bf16[192,384]{1,0:T(8,128)(2,1)S(1)} %get-tuple-element.121), channel_id=1, source_target_pairs={{0,2},{1,3},{2,0},{3,1},{4,6},{5,7},{6,4},{7,5},{8,10},{9,11},{10,... | collective-permute-start | bytes 442376 | tf_op jit(solution)/shard_map/ppermute | solution.py:325
  8.1 1.8 collective-permute-start.27
  11.9 8.1 %collective-permute-done.44 = bf16[192,384]{1,0:T(8,128)(2,1)S(1)} collective-permute-done((bf16[192,384]{1,0:T(8,128)(2,1)S(1)}, bf16[192,384]{1,0:T(8,128)(2,1)S(1)}, u32[]{:S(2)}, u32[]{:S(2)}) %collective-permute-start.44) | collective-permute-done | bytes 147488 | tf_op jit(solution)/shard_map/ppermute | solution.py:325
  20.9 5.1 %collective-permute-start.1 = (bf16[12,192]{1,0:T(8,128)(2,1)S(1)}, bf16[12,192]{1,0:T(8,128)(2,1)S(1)}, u32[]{:S(2)}, u32[]{:S(2)}) collective-permute-start(bf16[12,192]{1,0:T(8,128)(2,1)S(1)} %convert_element_type.187), channel_id=1, source_target_pairs={{0,2},{1,3},{2,0},{3,1},{4,6},{5,7},{6,4},{7,5},{8,10},{9,11},{10,... | collective-permute-start | bytes 13832 | tf_op jit(solution)/shard_map/ppermute | solution.py:325
  26.0 1.6 collective-permute-done.1
  31.2 2.7 collective-permute-start.2
  34.0 2.9 collective-permute-done.2
  36.9 2.7 collective-permute-start.28
  39.6 1.7 collective-permute-start.3
  41.3 2.7 collective-permute-start.5
  45.5 1.7 collective-permute-start.49
  47.3 7.4 %collective-permute-done.4 = bf16[96,768]{1,0:T(8,128)(2,1)S(1)} collective-permute-done((bf16[96,768]{1,0:T(8,128)(2,1)S(1)}, bf16[96,768]{1,0:T(8,128)(2,1)S(1)}, u32[]{:S(2)}, u32[]{:S(2)}) %collective-permute-start.4) | collective-permute-done | bytes 147488 | tf_op jit(solution)/shard_map/ppermute | solution.py:325
  54.7 1.9 collective-permute-start.47
  59.0 3.6 collective-permute-done.47.refs_39_
  62.6 2.7 collective-permute-start.9
  65.3 2.5 collective-permute-start.7
  68.9 2.7 collective-permute-start.8
  71.7 2.7 collective-permute-start.6
  75.7 2.2 collective-permute-start.32
  77.9 2.5 collective-permute-start.30
  80.4 1.7 collective-permute-done.6.refs_2_.refs_6_
  82.1 2.1 collective-permute-start.31
  84.2 2.5 collective-permute-start.29
  86.9 1.7 collective-permute-done.30.refs_23_
  88.5 2.0 collective-permute-start.51
  91.7 3.2 collective-permute-done.29.refs_22_
  96.0 3.3 collective-permute-done.51.refs_43_
  99.3 1.9 collective-permute-start.11
  105.0 2.0 gather_fusion
  120.0 6.3 %shard_map.296 = (bf16[256,768]{1,0:T(8,128)(2,1)}, bf16[256,576]{1,0:T(8,128)(2,1)}, bf16[256,576]{1,0:T(8,128)(2,1)}, bf16[256,576]{1,0:T(8,128)(2,1)}, bf16[256,576]{1,0:T(8,128)(2,1)}) custom-call(s32[2]{0:T(128)} %pad_add_fusion.meta, bf16[256,768]{1,0:T(8,128)(2,1)} %bitcast.192, f32[12,768]{1,0:T(8,128)} %reshape.121.vec_ref, ...), custom_call_target="tpu_custom_call" | custom-call | flops 905969664 | bytes 6730760 | tf_op jit(solution)/shard_map/pallas_call | solution.py:682
  126.9 3.1 collective-permute-start.21
  131.3 4.3 %collective-permute-done.33.refs_26_ = bf16[2,96,768]{2,1,0:T(8,128)(2,1)S(1)} collective-permute-done((bf16[2,96,768]{2,1,0:T(8,128)(2,1)}, bf16[2,96,768]{2,1,0:T(8,128)(2,1)S(1)}, u32[]{:S(2)}, u32[]{:S(2)}) %collective-permute-start.33) | collective-permute-done | bytes 294944 | tf_op jit(solution)/shard_map/ppermute | solution.py:325
  135.6 7.4 %collective-permute-done.20.refs_1_ = bf16[256,576]{1,0:T(8,128)(2,1)S(1)} collective-permute-done((bf16[256,576]{1,0:T(8,128)(2,1)}, bf16[256,576]{1,0:T(8,128)(2,1)S(1)}, u32[]{:S(2)}, u32[]{:S(2)}) %collective-permute-start.20) | collective-permute-done | bytes 294944 | tf_op jit(solution)/shard_map/ppermute | solution.py:325
  143.0 9.8 %collective-permute-done.21.refs_2_ = bf16[256,576]{1,0:T(8,128)(2,1)S(1)} collective-permute-done((bf16[256,576]{1,0:T(8,128)(2,1)}, bf16[256,576]{1,0:T(8,128)(2,1)S(1)}, u32[]{:S(2)}, u32[]{:S(2)}) %collective-permute-start.21) | collective-permute-done | bytes 294944 | tf_op jit(solution)/shard_map/ppermute | solution.py:325
  153.7 12.4 %shard_map.297 = (bf16[256,192]{1,0:T(8,128)(2,1)}, bf16[256,192]{1,0:T(8,128)(2,1)}, bf16[256,192]{1,0:T(8,128)(2,1)}, bf16[256,192]{1,0:T(8,128)(2,1)}) custom-call(s32[2]{0:T(128)} %pad_add_fusion.meta, bf16[256,576]{1,0:T(8,128)(2,1)} %get-tuple-element.53.refs_0_, bf16[256,576]{1,0:T(8,128)(2,1)} %copy-done.39, bf16[256,576]{1,0:T(8,128)(2,1)} %copy-done.40, ...), custom_call_target="tpu_custom_call" | custom-call | flops 805306368 | bytes 1572872 | tf_op jit(solution)/shard_map/pallas_call | solution.py:682
  166.1 6.5 %collective-permute-start.23 = (bf16[256,192]{1,0:T(8,128)(2,1)}, bf16[256,192]{1,0:T(8,128)(2,1)S(1)}, u32[]{:S(2)}, u32[]{:S(2)}) collective-permute-start(bf16[256,192]{1,0:T(8,128)(2,1)} %get-tuple-element.58), channel_id=1, source_target_pairs={{0,1},{1,0},{2,3},{3,2},{4,5},{5,4},{6,7},{7,6},{8,9},{9,8},{10,11... | collective-permute-start | bytes 294920 | tf_op jit(solution)/shard_map/ppermute | solution.py:325
  177.7 7.9 %collective-permute-done.24.refs_2_ = bf16[256,192]{1,0:T(8,128)(2,1)S(1)} collective-permute-done((bf16[256,192]{1,0:T(8,128)(2,1)}, bf16[256,192]{1,0:T(8,128)(2,1)S(1)}, u32[]{:S(2)}, u32[]{:S(2)}) %collective-permute-start.24) | collective-permute-done | bytes 98336 | tf_op jit(solution)/shard_map/ppermute | solution.py:325
  186.3 16.5 %shard_map.298 = (bf16[256,768]{1,0:T(8,128)(2,1)}, bf16[256,768]{1,0:T(8,128)(2,1)}, bf16[256,768]{1,0:T(8,128)(2,1)}, bf16[4,256,768]{2,1,0:T(8,128)(2,1)}, bf...) custom-call(s32[2]{0:T(128)} %pad_add_fusion.meta, ...), custom_call_target="tpu_custom_call" | custom-call | flops 5435817984 | bytes 21319688 | tf_op jit(solution)/shard_map/pallas_call | solution.py:682
  202.8 5.5 %shard_map.302 = (bf16[4,4,96,768]{3,2,1,0:T(8,128)(2,1)}, bf16[4,4,96,768]{3,2,1,0:T(8,128)(2,1)}) custom-call(s32[2]{0:T(128)} %pad_add_fusion.meta, bf16[256,768]{1,0:T(8,128)(2,1)} %get-tuple-element.78.h_ref, bf16[4,256,768]{2,1,0:T(8,128)(2,1)} %get-tuple-element.79.dpre_ref), custom_call_target="tpu_custom_call" | custom-call | flops 1207959552 | bytes 6684680 | tf_op jit(solution)/shard_map/pallas_call | solution.py:682
  208.4 2.0 collective-permute-start.60
  212.9 5.9 %shard_map.303 = (bf16[4,4,192,384]{3,2,1,0:T(8,128)(2,1)}, bf16[4,4,192,384]{3,2,1,0:T(8,128)(2,1)}) custom-call(s32[2]{0:T(128)} %pad_add_fusion.meta, bf16[256,768]{1,0:T(8,128)(2,1)} %bitcast.209, bf16[4,256,768]{2,1,0:T(8,128)(2,1)} %get-tuple-element.82.act_ref), custom_call_target="tpu_custom_call" | custom-call | flops 1207959552 | bytes 6684680 | tf_op jit(solution)/shard_map/pallas_call | solution.py:682
  218.9 4.4 %collective-permute-done.61.refs_6_ = bf16[256,192]{1,0:T(8,128)(2,1)S(1)} collective-permute-done((bf16[256,192]{1,0:T(8,128)(2,1)S(1)}, bf16[256,192]{1,0:T(8,128)(2,1)S(1)}, u32[]{:S(2)}, u32[]{:S(2)}) %collective-permute-start.61) | collective-permute-done | bytes 98336 | tf_op jit(solution)/shard_map/ppermute | solution.py:325
  224.0 16.0 %shard_map.299 = (bf16[256,576]{1,0:T(8,128)(2,1)}, bf16[256,576]{1,0:T(8,128)(2,1)}, bf16[256,576]{1,0:T(8,128)(2,1)}, bf16[256,576]{1,0:T(8,128)(2,1)}) custom-call(s32[2]{0:T(128)} %pad_add_fusion.meta, bf16[256,576]{1,0:T(8,128)(2,1)} %get-tuple-element.53.refs_0_, bf16[256,576]{1,0:T(8,128)(2,1)} %copy-done.39, bf16[256,576]{1,0:T(8,128)(2,1)} %copy-done.40, ...), custom_call_target="tpu_custom_call" | custom-call | flops 2013265920 | bytes 2752520 | tf_op jit(solution)/shard_map/pallas_call | solution.py:682
  240.0 2.5 collective-permute-start.63
  245.3 10.6 %collective-permute-done.63.refs_1_ = bf16[256,576]{1,0:T(8,128)(2,1)S(1)} collective-permute-done((bf16[256,576]{1,0:T(8,128)(2,1)}, bf16[256,576]{1,0:T(8,128)(2,1)S(1)}, u32[]{:S(2)}, u32[]{:S(2)}) %collective-permute-start.63) | collective-permute-done | bytes 294944 | tf_op jit(solution)/shard_map/ppermute | solution.py:325
  255.9 12.4 %collective-permute-done.64.refs_2_ = bf16[256,576]{1,0:T(8,128)(2,1)S(1)} collective-permute-done((bf16[256,576]{1,0:T(8,128)(2,1)}, bf16[256,576]{1,0:T(8,128)(2,1)S(1)}, u32[]{:S(2)}, u32[]{:S(2)}) %collective-permute-start.64) | collective-permute-done | bytes 294944 | tf_op jit(solution)/shard_map/ppermute | solution.py:325
  269.3 7.4 %shard_map.300 = (bf16[4,4,96,768]{3,2,1,0:T(8,128)(2,1)}, bf16[4,4,96,768]{3,2,1,0:T(8,128)(2,1)}, bf16[4,256,576]{2,1,0:T(8,128)(2,1)}, f32[4,1,576]{2,1,0:T(1,128)}) custom-call(s32[2]{0:T(128)} %pad_add_fusion.meta, bf16[256,768]{1,0:T(8,128)(2,1)} %get-tuple-element.63.h_ref, bf16[256,768]{1,0:T(8,128)(2,1)} %get-tuple-element.64.att_ref, ...), custom_call_target="tpu_custom_call" | custom-call | flops 1207959552 | bytes 8266760 | tf_op jit(solution)/shard_map/pallas_call | solution.py:682
  276.7 7.0 %shard_map.301 = (f32[256,768]{1,0:T(8,128)}, f32[8,768]{1,0:T(8,128)}) custom-call(s32[2]{0:T(128)} %pad_add_fusion.meta, bf16[256,768]{1,0:T(8,128)(2,1)} %bitcast.194, f32[12,768]{1,0:T(8,128)} %reshape.121.vec_ref, f32[256,768]{1,0:T(8,128)} %get-tuple-element.62.dmid_ref, bf16[4,256,576]{2,1,0:T(8,128)(2,1)} %get-tuple-element.74.mixed_ref, ...), custom_call_target="tpu_custom_call" | custom-call | flops 905969664 | bytes 7925768 | tf_op jit(solution)/shard_map/pallas_call | solution.py:682
  285.6 6.5 %collective-permute-start.91 = (f32[12,192]{1,0:T(8,128)S(1)}, f32[12,192]{1,0:T(8,128)S(1)}, u32[]{:S(2)}, u32[]{:S(2)}) collective-permute-start(f32[12,192]{1,0:T(8,128)S(1)} %get-tuple-element.122), channel_id=1, source_target_pairs={{0,2},{1,3},{2,0},{3,1},{4,6},{5,7},{6,4},{7,5},{8,10},{9,11},{10,... | collective-permute-start | bytes 27656 | tf_op jit(solution)/shard_map/ppermute | solution.py:325
  293.9 2.0 collective-permute-done.90
  295.9 1.8 collective-permute-done.92
  300.2 2.4 collective-permute-done.94
  304.0 2.3 collective-permute-done.95
  307.0 2.2 convert_add_fusion.1
  312.2 2.2 convert_add_fusion
  318.2 7.4 %collective-permute-done.75 = bf16[2,2,96,768]{3,2,1,0:T(8,128)(2,1)S(1)} collective-permute-done((bf16[2,2,96,768]{3,2,1,0:T(8,128)(2,1)S(1)}, bf16[2,2,96,768]{3,2,1,0:T(8,128)(2,1)S(1)}, u32[]{:S(2)}, u32[]{:S(2)}) %collective-permute-start.75) | collective-permute-done | bytes 589856 | tf_op jit(solution)/shard_map/ppermute | solution.py:325
  328.2 10.1 %collective-permute-done.83 = bf16[2,2,192,384]{3,2,1,0:T(8,128)(2,1)S(1)} collective-permute-done((bf16[2,2,192,384]{3,2,1,0:T(8,128)(2,1)S(1)}, bf16[2,2,192,384]{3,2,1,0:T(8,128)(2,1)S(1)}, u32[]{:S(2)}, u32[]{:S(2)}) %collective-permute-start.83) | collective-permute-done | bytes 589856 | tf_op jit(solution)/shard_map/ppermute | solution.py:325
  341.3 15.9 %collective-permute-done.79 = bf16[2,96,768]{2,1,0:T(8,128)(2,1)S(1)} collective-permute-done((bf16[2,96,768]{2,1,0:T(8,128)(2,1)S(1)}, bf16[2,96,768]{2,1,0:T(8,128)(2,1)S(1)}, u32[]{:S(2)}, u32[]{:S(2)}) %collective-permute-start.79) | collective-permute-done | bytes 294944 | tf_op jit(solution)/shard_map/ppermute | solution.py:325
  358.6 2.5 collective-permute-start.80
  368.9 5.8 %collective-permute-done.80 = bf16[96,768]{1,0:T(8,128)(2,1)S(1)} collective-permute-done((bf16[96,768]{1,0:T(8,128)(2,1)S(1)}, bf16[96,768]{1,0:T(8,128)(2,1)S(1)}, u32[]{:S(2)}, u32[]{:S(2)}) %collective-permute-start.80) | collective-permute-done | bytes 147488 | tf_op jit(solution)/shard_map/ppermute | solution.py:325
  374.7 3.6 collective-permute-start.85
  381.0 4.0 %collective-permute-done.71 = bf16[2,96,768]{2,1,0:T(8,128)(2,1)S(1)} collective-permute-done((bf16[2,96,768]{2,1,0:T(8,128)(2,1)S(1)}, bf16[2,96,768]{2,1,0:T(8,128)(2,1)S(1)}, u32[]{:S(2)}, u32[]{:S(2)}) %collective-permute-start.71) | collective-permute-done | bytes 294944 | tf_op jit(solution)/shard_map/ppermute | solution.py:325
  386.0 1.6 collective-permute-start.73
  388.7 5.3 %collective-permute-done.72 = bf16[96,768]{1,0:T(8,128)(2,1)S(1)} collective-permute-done((bf16[96,768]{1,0:T(8,128)(2,1)S(1)}, bf16[96,768]{1,0:T(8,128)(2,1)S(1)}, u32[]{:S(2)}, u32[]{:S(2)}) %collective-permute-start.72) | collective-permute-done | bytes 147488 | tf_op jit(solution)/shard_map/ppermute | solution.py:325
  (368 shorter events, 87.0 us)
Async XLA Ops:
  1.7 18.3 %collective-permute-start.44 = (bf16[192,384]{1,0:T(8,128)(2,1)S(1)}, bf16[192,384]{1,0:T(8,128)(2,1)S(1)}, u32[]{:S(2)}, u32[]{:S(2)}) collective-permute-start(bf16[192,384]{1,0:T(8,128)(2,1)S(1)} %get-tuple-element.121), channel_id=1, source_target_pairs={{0,2},{1,3},{2,0},{3,1},{4,6},{5,7},{6,4},{7,5},{8,10},{9,11},{10,... | collective-permute-start | bytes 442376 | tf_op jit(solution)/shard_map/ppermute | solution.py:325
  5.8 14.2 %collective-permute-start.45 = (bf16[192,384]{1,0:T(8,128)(2,1)S(1)}, bf16[192,384]{1,0:T(8,128)(2,1)S(1)}, u32[]{:S(2)}, u32[]{:S(2)}) collective-permute-start(bf16[192,384]{1,0:T(8,128)(2,1)S(1)} %get-tuple-element.121), channel_id=1, source_target_pairs={{0,3},{1,2},{2,1},{3,0},{4,7},{5,6},{6,5},{7,4},{8,11},{9,10},{10,... | collective-permute-start | bytes 442376 | tf_op jit(solution)/shard_map/ppermute | solution.py:325
  8.1 31.5 %collective-permute-start.27 = (bf16[96,768]{1,0:T(8,128)(2,1)S(1)}, bf16[96,768]{1,0:T(8,128)(2,1)S(1)}, u32[]{:S(2)}, u32[]{:S(2)}) collective-permute-start(bf16[96,768]{1,0:T(8,128)(2,1)S(1)} %convert_element_type.192), channel_id=1, source_target_pairs={{0,2},{1,3},{2,0},{3,1},{4,6},{5,7},{6,4},{7,5},{8,10},{9,11},{10,... | collective-permute-start | bytes 442376 | tf_op jit(solution)/shard_map/ppermute | solution.py:325
  9.9 29.7 %collective-permute-start.26 = (bf16[96,768]{1,0:T(8,128)(2,1)S(1)}, bf16[96,768]{1,0:T(8,128)(2,1)S(1)}, u32[]{:S(2)}, u32[]{:S(2)}) collective-permute-start(bf16[96,768]{1,0:T(8,128)(2,1)S(1)} %convert_element_type.192), channel_id=1, source_target_pairs={{0,1},{1,0},{2,3},{3,2},{4,5},{5,4},{6,7},{7,6},{8,9},{9,8},{10,11... | collective-permute-start | bytes 442376 | tf_op jit(solution)/shard_map/ppermute | solution.py:325
  11.2 30.1 %collective-permute-start.43 = (bf16[192,384]{1,0:T(8,128)(2,1)S(1)}, bf16[192,384]{1,0:T(8,128)(2,1)S(1)}, u32[]{:S(2)}, u32[]{:S(2)}) collective-permute-start(bf16[192,384]{1,0:T(8,128)(2,1)S(1)} %get-tuple-element.121), channel_id=1, source_target_pairs={{0,1},{1,0},{2,3},{3,2},{4,5},{5,4},{6,7},{7,6},{8,9},{9,8},{10,11... | collective-permute-start | bytes 442376 | tf_op jit(solution)/shard_map/ppermute | solution.py:325
  20.1 38.1 %collective-permute-start.53 = (bf16[2,192,384]{2,1,0:T(8,128)(2,1)S(1)}, bf16[2,192,384]{2,1,0:T(8,128)(2,1)S(1)}, u32[]{:S(2)}, u32[]{:S(2)}) collective-permute-start(bf16[2,192,384]{2,1,0:T(8,128)(2,1)S(1)} %pad_maximum_fusion.5.refs_37_), channel_id=1, source_target_pairs={{0,4},{4,0},{8,12},{12,8},{16,20},{20,16},{24,28},{28,24},{1,5},{5... | collective-permute-start | bytes 884744 | tf_op jit(solution)/shard_map/ppermute | solution.py:325
  39.6 15.1 %collective-permute-start.4 = (bf16[96,768]{1,0:T(8,128)(2,1)S(1)}, bf16[96,768]{1,0:T(8,128)(2,1)S(1)}, u32[]{:S(2)}, u32[]{:S(2)}) collective-permute-start(bf16[96,768]{1,0:T(8,128)(2,1)S(1)} %pad_maximum_fusion.6), channel_id=1, source_target_pairs={{0,2},{1,3},{2,0},{3,1},{4,6},{5,7},{6,4},{7,5},{8,10},{9,11},{10,... | collective-permute-start | bytes 442376 | tf_op jit(solution)/shard_map/ppermute | solution.py:325
  39.6 16.9 %collective-permute-start.3 = (bf16[96,768]{1,0:T(8,128)(2,1)S(1)}, bf16[96,768]{1,0:T(8,128)(2,1)S(1)}, u32[]{:S(2)}, u32[]{:S(2)}) collective-permute-start(bf16[96,768]{1,0:T(8,128)(2,1)S(1)} %pad_maximum_fusion.6), channel_id=1, source_target_pairs={{0,1},{1,0},{2,3},{3,2},{4,5},{5,4},{6,7},{7,6},{8,9},{9,8},{10,11... | collective-permute-start | bytes 442376 | tf_op jit(solution)/shard_map/ppermute | solution.py:325
  41.3 15.2 %collective-permute-start.5 = (bf16[96,768]{1,0:T(8,128)(2,1)S(1)}, bf16[96,768]{1,0:T(8,128)(2,1)S(1)}, u32[]{:S(2)}, u32[]{:S(2)}) collective-permute-start(bf16[96,768]{1,0:T(8,128)(2,1)S(1)} %pad_maximum_fusion.6), channel_id=1, source_target_pairs={{0,3},{1,2},{2,1},{3,0},{4,7},{5,6},{6,5},{7,4},{8,11},{9,10},{10,... | collective-permute-start | bytes 442376 | tf_op jit(solution)/shard_map/ppermute | solution.py:325
  45.5 13.4 %collective-permute-start.49 = (bf16[2,192,384]{2,1,0:T(8,128)(2,1)S(1)}, bf16[2,192,384]{2,1,0:T(8,128)(2,1)S(1)}, u32[]{:S(2)}, u32[]{:S(2)}) collective-permute-start(bf16[2,192,384]{2,1,0:T(8,128)(2,1)S(1)} %pad_maximum_fusion.5.refs_37_), channel_id=1, source_target_pairs={{0,16},{4,20},{8,24},{12,28},{16,0},{20,4},{24,8},{28,12},{1,17},{... | collective-permute-start | bytes 884744 | tf_op jit(solution)/shard_map/ppermute | solution.py:325
  56.6 11.2 %collective-permute-start.48 = (bf16[2,192,384]{2,1,0:T(8,128)(2,1)S(1)}, bf16[2,192,384]{2,1,0:T(8,128)(2,1)}, u32[]{:S(2)}, u32[]{:S(2)}) collective-permute-start(bf16[2,192,384]{2,1,0:T(8,128)(2,1)S(1)} %pad_maximum_fusion.4.refs_36_), channel_id=1, source_target_pairs={{0,16},{4,20},{8,24},{12,28},{16,0},{20,4},{24,8},{28,12},{1,17},{... | collective-permute-start | bytes 884744 | tf_op jit(solution)/shard_map/ppermute | solution.py:325
  58.1 10.7 %collective-permute-start.46 = (bf16[2,192,384]{2,1,0:T(8,128)(2,1)S(1)}, bf16[2,192,384]{2,1,0:T(8,128)(2,1)}, u32[]{:S(2)}, u32[]{:S(2)}) collective-permute-start(bf16[2,192,384]{2,1,0:T(8,128)(2,1)S(1)} %pad_maximum_fusion.4.refs_36_), channel_id=1, source_target_pairs={{0,8},{4,12},{8,0},{12,4},{16,24},{20,28},{24,16},{28,20},{1,9},{5... | collective-permute-start | bytes 884744 | tf_op jit(solution)/shard_map/ppermute | solution.py:325
  58.9 12.8 %collective-permute-start.13 = (bf16[2,96,768]{2,1,0:T(8,128)(2,1)S(1)}, bf16[2,96,768]{2,1,0:T(8,128)(2,1)S(1)}, u32[]{:S(2)}, u32[]{:S(2)}) collective-permute-start(bf16[2,96,768]{2,1,0:T(8,128)(2,1)S(1)} %pad_maximum_fusion.1.refs_1_.refs_5_), channel_id=1, source_target_pairs={{0,4},{4,0},{8,12},{12,8},{16,20},{20,16},{24,28},{28,24},{1,5},{5... | collective-permute-start | bytes 884744 | tf_op jit(solution)/shard_map/ppermute | solution.py:325
  62.6 11.8 %collective-permute-start.9 = (bf16[2,96,768]{2,1,0:T(8,128)(2,1)S(1)}, bf16[2,96,768]{2,1,0:T(8,128)(2,1)S(1)}, u32[]{:S(2)}, u32[]{:S(2)}) collective-permute-start(bf16[2,96,768]{2,1,0:T(8,128)(2,1)S(1)} %pad_maximum_fusion.1.refs_1_.refs_5_), channel_id=1, source_target_pairs={{0,16},{4,20},{8,24},{12,28},{16,0},{20,4},{24,8},{28,12},{1,17},{... | collective-permute-start | bytes 884744 | tf_op jit(solution)/shard_map/ppermute | solution.py:325
  68.9 11.5 %collective-permute-start.8 = (bf16[2,96,768]{2,1,0:T(8,128)(2,1)S(1)}, bf16[2,96,768]{2,1,0:T(8,128)(2,1)S(1)}, u32[]{:S(2)}, u32[]{:S(2)}) collective-permute-start(bf16[2,96,768]{2,1,0:T(8,128)(2,1)S(1)} %pad_maximum_fusion.refs_0_.refs_4_), channel_id=1, source_target_pairs={{0,16},{4,20},{8,24},{12,28},{16,0},{20,4},{24,8},{28,12},{1,17},{... | collective-permute-start | bytes 884744 | tf_op jit(solution)/shard_map/ppermute | solution.py:325
  75.7 11.1 %collective-permute-start.32 = (bf16[2,96,768]{2,1,0:T(8,128)(2,1)S(1)}, bf16[2,96,768]{2,1,0:T(8,128)(2,1)}, u32[]{:S(2)}, u32[]{:S(2)}) collective-permute-start(bf16[2,96,768]{2,1,0:T(8,128)(2,1)S(1)} %pad_maximum_fusion.3.refs_21_), channel_id=1, source_target_pairs={{0,16},{4,20},{8,24},{12,28},{16,0},{20,4},{24,8},{28,12},{1,17},{... | collective-permute-start | bytes 884744 | tf_op jit(solution)/shard_map/ppermute | solution.py:325
  77.9 10.6 %collective-permute-start.30 = (bf16[2,96,768]{2,1,0:T(8,128)(2,1)S(1)}, bf16[2,96,768]{2,1,0:T(8,128)(2,1)}, u32[]{:S(2)}, u32[]{:S(2)}) collective-permute-start(bf16[2,96,768]{2,1,0:T(8,128)(2,1)S(1)} %pad_maximum_fusion.3.refs_21_), channel_id=1, source_target_pairs={{0,8},{4,12},{8,0},{12,4},{16,24},{20,28},{24,16},{28,20},{1,9},{5... | collective-permute-start | bytes 884744 | tf_op jit(solution)/shard_map/ppermute | solution.py:325
  84.2 10.6 %collective-permute-start.29 = (bf16[2,96,768]{2,1,0:T(8,128)(2,1)S(1)}, bf16[2,96,768]{2,1,0:T(8,128)(2,1)}, u32[]{:S(2)}, u32[]{:S(2)}) collective-permute-start(bf16[2,96,768]{2,1,0:T(8,128)(2,1)S(1)} %pad_maximum_fusion.2.refs_20_), channel_id=1, source_target_pairs={{0,8},{4,12},{8,0},{12,4},{16,24},{20,28},{24,16},{28,20},{1,9},{5... | collective-permute-start | bytes 884744 | tf_op jit(solution)/shard_map/ppermute | solution.py:325
  88.5 10.8 %collective-permute-start.51 = (bf16[2,192,384]{2,1,0:T(8,128)(2,1)S(1)}, bf16[2,192,384]{2,1,0:T(8,128)(2,1)S(1)}, u32[]{:S(2)}, u32[]{:S(2)}) collective-permute-start(bf16[2,192,384]{2,1,0:T(8,128)(2,1)S(1)} %collective-permute-done.49.refs_41_), channel_id=1, source_target_pairs={{0,8},{4,12},{8,0},{12,4},{16,24},{20,28},{24,16},{28,20},{1,9},{5... | collective-permute-start | bytes 884744 | tf_op jit(solution)/shard_map/ppermute | solution.py:325
  90.5 10.7 %collective-permute-start.55 = (bf16[2,192,384]{2,1,0:T(8,128)(2,1)}, bf16[2,192,384]{2,1,0:T(8,128)(2,1)S(1)}, u32[]{:S(2)}, u32[]{:S(2)}) collective-permute-start(bf16[2,192,384]{2,1,0:T(8,128)(2,1)} %copy-done.47), channel_id=1, source_target_pairs={{0,4},{4,0},{8,12},{12,8},{16,20},{20,16},{24,28},{28,24},{1,5},{5... | collective-permute-start | bytes 884744 | tf_op jit(solution)/shard_map/ppermute | solution.py:325
  91.4 11.4 %collective-permute-start.56 = (bf16[2,192,384]{2,1,0:T(8,128)(2,1)}, bf16[2,192,384]{2,1,0:T(8,128)(2,1)S(1)}, u32[]{:S(2)}, u32[]{:S(2)}) collective-permute-start(bf16[2,192,384]{2,1,0:T(8,128)(2,1)} %collective-permute-done.48.refs_40_), channel_id=1, source_target_pairs={{0,4},{4,0},{8,12},{12,8},{16,20},{20,16},{24,28},{28,24},{1,5},{5... | collective-permute-start | bytes 884744 | tf_op jit(solution)/shard_map/ppermute | solution.py:325
  95.5 11.6 %collective-permute-start.17 = (bf16[2,96,768]{2,1,0:T(8,128)(2,1)S(1)}, bf16[2,96,768]{2,1,0:T(8,128)(2,1)S(1)}, u32[]{:S(2)}, u32[]{:S(2)}) collective-permute-start(bf16[2,96,768]{2,1,0:T(8,128)(2,1)S(1)} %collective-permute-done.9.refs_5_.refs_9_), channel_id=1, source_target_pairs={{0,4},{4,0},{8,12},{12,8},{16,20},{20,16},{24,28},{28,24},{1,5},{5... | collective-permute-start | bytes 884744 | tf_op jit(solution)/shard_map/ppermute | solution.py:325
  108.1 11.3 %collective-permute-start.18 = (bf16[2,96,768]{2,1,0:T(8,128)(2,1)S(1)}, bf16[2,96,768]{2,1,0:T(8,128)(2,1)}, u32[]{:S(2)}, u32[]{:S(2)}) collective-permute-start(bf16[2,96,768]{2,1,0:T(8,128)(2,1)S(1)} %collective-permute-done.10.refs_6_.refs_10_), channel_id=1, source_target_pairs={{0,4},{4,0},{8,12},{12,8},{16,20},{20,16},{24,28},{28,24},{1,5},{5... | collective-permute-start | bytes 884744 | tf_op jit(solution)/shard_map/ppermute | solution.py:325
  109.6 16.8 %collective-permute-start.50 = (bf16[2,192,384]{2,1,0:T(8,128)(2,1)}, bf16[2,192,384]{2,1,0:T(8,128)(2,1)}, u32[]{:S(2)}, u32[]{:S(2)}) collective-permute-start(bf16[2,192,384]{2,1,0:T(8,128)(2,1)} %collective-permute-done.46.refs_38_), channel_id=1, source_target_pairs={{0,16},{4,20},{8,24},{12,28},{16,0},{20,4},{24,8},{28,12},{1,17},{... | collective-permute-start | bytes 884744 | tf_op jit(solution)/shard_map/ppermute | solution.py:325
  111.0 15.9 %collective-permute-start.40 = (bf16[2,96,768]{2,1,0:T(8,128)(2,1)}, bf16[2,96,768]{2,1,0:T(8,128)(2,1)}, u32[]{:S(2)}, u32[]{:S(2)}) collective-permute-start(bf16[2,96,768]{2,1,0:T(8,128)(2,1)} %collective-permute-done.32.refs_25_), channel_id=1, source_target_pairs={{0,4},{4,0},{8,12},{12,8},{16,20},{20,16},{24,28},{28,24},{1,5},{5... | collective-permute-start | bytes 884744 | tf_op jit(solution)/shard_map/ppermute | solution.py:325
  114.5 12.3 %collective-permute-start.34 = (bf16[2,96,768]{2,1,0:T(8,128)(2,1)}, bf16[2,96,768]{2,1,0:T(8,128)(2,1)}, u32[]{:S(2)}, u32[]{:S(2)}) collective-permute-start(bf16[2,96,768]{2,1,0:T(8,128)(2,1)} %collective-permute-done.32.refs_25_), channel_id=1, source_target_pairs={{0,8},{4,12},{8,0},{12,4},{16,24},{20,28},{24,16},{28,20},{1,9},{5... | collective-permute-start | bytes 884744 | tf_op jit(solution)/shard_map/ppermute | solution.py:325
  115.2 14.8 %collective-permute-start.38 = (bf16[2,96,768]{2,1,0:T(8,128)(2,1)}, bf16[2,96,768]{2,1,0:T(8,128)(2,1)}, u32[]{:S(2)}, u32[]{:S(2)}) collective-permute-start(bf16[2,96,768]{2,1,0:T(8,128)(2,1)} %collective-permute-done.30.refs_23_), channel_id=1, source_target_pairs={{0,4},{4,0},{8,12},{12,8},{16,20},{20,16},{24,28},{28,24},{1,5},{5... | collective-permute-start | bytes 884744 | tf_op jit(solution)/shard_map/ppermute | solution.py:325
  119.4 11.8 %collective-permute-start.39 = (bf16[2,96,768]{2,1,0:T(8,128)(2,1)}, bf16[2,96,768]{2,1,0:T(8,128)(2,1)S(1)}, u32[]{:S(2)}, u32[]{:S(2)}) collective-permute-start(bf16[2,96,768]{2,1,0:T(8,128)(2,1)} %collective-permute-done.31.refs_24_), channel_id=1, source_target_pairs={{0,4},{4,0},{8,12},{12,8},{16,20},{20,16},{24,28},{28,24},{1,5},{5... | collective-permute-start | bytes 884744 | tf_op jit(solution)/shard_map/ppermute | solution.py:325
  126.8 16.2 %collective-permute-start.20 = (bf16[256,576]{1,0:T(8,128)(2,1)}, bf16[256,576]{1,0:T(8,128)(2,1)S(1)}, u32[]{:S(2)}, u32[]{:S(2)}) collective-permute-start(bf16[256,576]{1,0:T(8,128)(2,1)} %get-tuple-element.54), channel_id=1, source_target_pairs={{0,1},{1,0},{2,3},{3,2},{4,5},{5,4},{6,7},{7,6},{8,9},{9,8},{10,11... | collective-permute-start | bytes 884744 | tf_op jit(solution)/shard_map/ppermute | solution.py:325
  126.9 26.0 %collective-permute-start.21 = (bf16[256,576]{1,0:T(8,128)(2,1)}, bf16[256,576]{1,0:T(8,128)(2,1)S(1)}, u32[]{:S(2)}, u32[]{:S(2)}) collective-permute-start(bf16[256,576]{1,0:T(8,128)(2,1)} %get-tuple-element.55), channel_id=1, source_target_pairs={{0,2},{1,3},{2,0},{3,1},{4,6},{5,7},{6,4},{7,5},{8,10},{9,11},{10,... | collective-permute-start | bytes 884744 | tf_op jit(solution)/shard_map/ppermute | solution.py:325
  130.0 22.8 %collective-permute-start.22 = (bf16[256,576]{1,0:T(8,128)(2,1)}, bf16[256,576]{1,0:T(8,128)(2,1)S(1)}, u32[]{:S(2)}, u32[]{:S(2)}) collective-permute-start(bf16[256,576]{1,0:T(8,128)(2,1)} %get-tuple-element.56), channel_id=1, source_target_pairs={{0,3},{1,2},{2,1},{3,0},{4,7},{5,6},{6,5},{7,4},{8,11},{9,10},{10,... | collective-permute-start | bytes 884744 | tf_op jit(solution)/shard_map/ppermute | solution.py:325
  131.2 34.8 %collective-permute-start.37 = (bf16[2,96,768]{2,1,0:T(8,128)(2,1)}, bf16[2,96,768]{2,1,0:T(8,128)(2,1)S(1)}, u32[]{:S(2)}, u32[]{:S(2)}) collective-permute-start(bf16[2,96,768]{2,1,0:T(8,128)(2,1)} %collective-permute-done.29.refs_22_), channel_id=1, source_target_pairs={{0,4},{4,0},{8,12},{12,8},{16,20},{20,16},{24,28},{28,24},{1,5},{5... | collective-permute-start | bytes 884744 | tf_op jit(solution)/shard_map/ppermute | solution.py:325
  135.6 37.0 %collective-permute-start.59 = (bf16[2,192,384]{2,1,0:T(8,128)(2,1)S(1)}, bf16[2,192,384]{2,1,0:T(8,128)(2,1)S(1)}, u32[]{:S(2)}, u32[]{:S(2)}) collective-permute-start(bf16[2,192,384]{2,1,0:T(8,128)(2,1)S(1)} %copy-done.51), channel_id=1, source_target_pairs={{0,4},{4,0},{8,12},{12,8},{16,20},{20,16},{24,28},{28,24},{1,5},{5... | collective-permute-start | bytes 884744 | tf_op jit(solution)/shard_map/ppermute | solution.py:325
  143.0 30.6 %collective-permute-start.58 = (bf16[2,192,384]{2,1,0:T(8,128)(2,1)}, bf16[2,192,384]{2,1,0:T(8,128)(2,1)S(1)}, u32[]{:S(2)}, u32[]{:S(2)}) collective-permute-start(bf16[2,192,384]{2,1,0:T(8,128)(2,1)} %collective-permute-done.50.refs_42_), channel_id=1, source_target_pairs={{0,4},{4,0},{8,12},{12,8},{16,20},{20,16},{24,28},{28,24},{1,5},{5... | collective-permute-start | bytes 884744 | tf_op jit(solution)/shard_map/ppermute | solution.py:325
  152.8 23.7 %collective-permute-start.42 = (bf16[2,96,768]{2,1,0:T(8,128)(2,1)}, bf16[2,96,768]{2,1,0:T(8,128)(2,1)S(1)}, u32[]{:S(2)}, u32[]{:S(2)}) collective-permute-start(bf16[2,96,768]{2,1,0:T(8,128)(2,1)} %collective-permute-done.34.refs_27_), channel_id=1, source_target_pairs={{0,4},{4,0},{8,12},{12,8},{16,20},{20,16},{24,28},{28,24},{1,5},{5... | collective-permute-start | bytes 884744 | tf_op jit(solution)/shard_map/ppermute | solution.py:325
  152.8 23.7 %collective-permute-start.41 = (bf16[2,96,768]{2,1,0:T(8,128)(2,1)S(1)}, bf16[2,96,768]{2,1,0:T(8,128)(2,1)S(1)}, u32[]{:S(2)}, u32[]{:S(2)}) collective-permute-start(bf16[2,96,768]{2,1,0:T(8,128)(2,1)S(1)} %collective-permute-done.33.refs_26_), channel_id=1, source_target_pairs={{0,4},{4,0},{8,12},{12,8},{16,20},{20,16},{24,28},{28,24},{1,5},{5... | collective-permute-start | bytes 884744 | tf_op jit(solution)/shard_map/ppermute | solution.py:325
  166.1 11.6 %collective-permute-start.23 = (bf16[256,192]{1,0:T(8,128)(2,1)}, bf16[256,192]{1,0:T(8,128)(2,1)S(1)}, u32[]{:S(2)}, u32[]{:S(2)}) collective-permute-start(bf16[256,192]{1,0:T(8,128)(2,1)} %get-tuple-element.58), channel_id=1, source_target_pairs={{0,1},{1,0},{2,3},{3,2},{4,5},{5,4},{6,7},{7,6},{8,9},{9,8},{10,11... | collective-permute-start | bytes 294920 | tf_op jit(solution)/shard_map/ppermute | solution.py:325
  172.6 13.1 %collective-permute-start.24 = (bf16[256,192]{1,0:T(8,128)(2,1)}, bf16[256,192]{1,0:T(8,128)(2,1)S(1)}, u32[]{:S(2)}, u32[]{:S(2)}) collective-permute-start(bf16[256,192]{1,0:T(8,128)(2,1)} %get-tuple-element.59), channel_id=1, source_target_pairs={{0,2},{1,3},{2,0},{3,1},{4,6},{5,7},{6,4},{7,5},{8,10},{9,11},{10,... | collective-permute-start | bytes 294920 | tf_op jit(solution)/shard_map/ppermute | solution.py:325
  173.6 12.0 %collective-permute-start.25 = (bf16[256,192]{1,0:T(8,128)(2,1)}, bf16[256,192]{1,0:T(8,128)(2,1)S(1)}, u32[]{:S(2)}, u32[]{:S(2)}) collective-permute-start(bf16[256,192]{1,0:T(8,128)(2,1)} %get-tuple-element.60), channel_id=1, source_target_pairs={{0,3},{1,2},{2,1},{3,0},{4,7},{5,6},{6,5},{7,4},{8,11},{9,10},{10,... | collective-permute-start | bytes 294920 | tf_op jit(solution)/shard_map/ppermute | solution.py:325
  208.3 98.7 %collective-permute-start.74 = (bf16[4,4,96,768]{3,2,1,0:T(8,128)(2,1)}, bf16[4,4,96,768]{3,2,1,0:T(8,128)(2,1)}, u32[]{:S(2)}, u32[]{:S(2)}) collective-permute-start(bf16[4,4,96,768]{3,2,1,0:T(8,128)(2,1)} %get-tuple-element.81), channel_id=1, source_target_pairs={{0,4},{4,0},{8,12},{12,8},{16,20},{20,16},{24,28},{28,24},{1,5},{5... | collective-permute-start | bytes 7077896 | tf_op jit(solution)/shard_map/ppermute | solution.py:325
  208.4 10.5 %collective-permute-start.60 = (bf16[256,192]{1,0:T(8,128)(2,1)S(1)}, bf16[256,192]{1,0:T(8,128)(2,1)S(1)}, u32[]{:S(2)}, u32[]{:S(2)}) collective-permute-start(bf16[256,192]{1,0:T(8,128)(2,1)S(1)} %copy-done.66), channel_id=1, source_target_pairs={{0,1},{1,0},{2,3},{3,2},{4,5},{5,4},{6,7},{7,6},{8,9},{9,8},{10,11... | collective-permute-start | bytes 294920 | tf_op jit(solution)/shard_map/ppermute | solution.py:325
  210.4 12.9 %collective-permute-start.61 = (bf16[256,192]{1,0:T(8,128)(2,1)S(1)}, bf16[256,192]{1,0:T(8,128)(2,1)S(1)}, u32[]{:S(2)}, u32[]{:S(2)}) collective-permute-start(bf16[256,192]{1,0:T(8,128)(2,1)S(1)} %copy-done.65), channel_id=1, source_target_pairs={{0,2},{1,3},{2,0},{3,1},{4,6},{5,7},{6,4},{7,5},{8,10},{9,11},{10,... | collective-permute-start | bytes 294920 | tf_op jit(solution)/shard_map/ppermute | solution.py:325
  211.4 11.9 %collective-permute-start.62 = (bf16[256,192]{1,0:T(8,128)(2,1)S(1)}, bf16[256,192]{1,0:T(8,128)(2,1)S(1)}, u32[]{:S(2)}, u32[]{:S(2)}) collective-permute-start(bf16[256,192]{1,0:T(8,128)(2,1)S(1)} %copy-done.63), channel_id=1, source_target_pairs={{0,3},{1,2},{2,1},{3,0},{4,7},{5,6},{6,5},{7,4},{8,11},{9,10},{10,... | collective-permute-start | bytes 294920 | tf_op jit(solution)/shard_map/ppermute | solution.py:325
  218.8 93.4 %collective-permute-start.82 = (bf16[4,4,192,384]{3,2,1,0:T(8,128)(2,1)}, bf16[4,4,192,384]{3,2,1,0:T(8,128)(2,1)}, u32[]{:S(2)}, u32[]{:S(2)}) collective-permute-start(bf16[4,4,192,384]{3,2,1,0:T(8,128)(2,1)} %get-tuple-element.84), channel_id=1, source_target_pairs={{0,4},{4,0},{8,12},{12,8},{16,20},{20,16},{24,28},{28,24},{1,5},{5... | collective-permute-start | bytes 7077896 | tf_op jit(solution)/shard_map/ppermute | solution.py:325
  240.0 15.9 %collective-permute-start.63 = (bf16[256,576]{1,0:T(8,128)(2,1)}, bf16[256,576]{1,0:T(8,128)(2,1)S(1)}, u32[]{:S(2)}, u32[]{:S(2)}) collective-permute-start(bf16[256,576]{1,0:T(8,128)(2,1)} %get-tuple-element.71), channel_id=1, source_target_pairs={{0,1},{1,0},{2,3},{3,2},{4,5},{5,4},{6,7},{7,6},{8,9},{9,8},{10,11... | collective-permute-start | bytes 884744 | tf_op jit(solution)/shard_map/ppermute | solution.py:325
  242.6 25.8 %collective-permute-start.64 = (bf16[256,576]{1,0:T(8,128)(2,1)}, bf16[256,576]{1,0:T(8,128)(2,1)S(1)}, u32[]{:S(2)}, u32[]{:S(2)}) collective-permute-start(bf16[256,576]{1,0:T(8,128)(2,1)} %get-tuple-element.72), channel_id=1, source_target_pairs={{0,2},{1,3},{2,0},{3,1},{4,6},{5,7},{6,4},{7,5},{8,10},{9,11},{10,... | collective-permute-start | bytes 884744 | tf_op jit(solution)/shard_map/ppermute | solution.py:325
  243.5 24.9 %collective-permute-start.65 = (bf16[256,576]{1,0:T(8,128)(2,1)}, bf16[256,576]{1,0:T(8,128)(2,1)S(1)}, u32[]{:S(2)}, u32[]{:S(2)}) collective-permute-start(bf16[256,576]{1,0:T(8,128)(2,1)} %get-tuple-element.73), channel_id=1, source_target_pairs={{0,3},{1,2},{2,1},{3,0},{4,7},{5,6},{6,5},{7,4},{8,11},{9,10},{10,... | collective-permute-start | bytes 884744 | tf_op jit(solution)/shard_map/ppermute | solution.py:325
  293.9 22.2 %collective-permute-start.66 = (bf16[4,4,96,768]{3,2,1,0:T(8,128)(2,1)}, bf16[4,4,96,768]{3,2,1,0:T(8,128)(2,1)S(1)}, u32[]{:S(2)}, u32[]{:S(2)}) collective-permute-start(bf16[4,4,96,768]{3,2,1,0:T(8,128)(2,1)} %get-tuple-element.77), channel_id=1, source_target_pairs={{0,4},{4,0},{8,12},{12,8},{16,20},{20,16},{24,28},{28,24},{1,5},{5... | collective-permute-start | bytes 7077896 | tf_op jit(solution)/shard_map/ppermute | solution.py:325
  309.3 16.3 %collective-permute-start.75 = (bf16[2,2,96,768]{3,2,1,0:T(8,128)(2,1)S(1)}, bf16[2,2,96,768]{3,2,1,0:T(8,128)(2,1)S(1)}, u32[]{:S(2)}, u32[]{:S(2)}) collective-permute-start(bf16[2,2,96,768]{3,2,1,0:T(8,128)(2,1)S(1)} %slice_bitcast_fusion.13), channel_id=1, source_target_pairs={{0,16},{4,20},{8,24},{12,28},{16,0},{20,4},{24,8},{28,12},{1,17},{... | collective-permute-start | bytes 1769480 | tf_op jit(solution)/shard_map/ppermute | solution.py:325
  310.8 16.3 %collective-permute-start.78 = (bf16[2,2,96,768]{3,2,1,0:T(8,128)(2,1)S(1)}, bf16[2,2,96,768]{3,2,1,0:T(8,128)(2,1)S(1)}, u32[]{:S(2)}, u32[]{:S(2)}) collective-permute-start(bf16[2,2,96,768]{3,2,1,0:T(8,128)(2,1)S(1)} %slice_bitcast_fusion.11), channel_id=1, source_target_pairs={{0,8},{4,12},{8,0},{12,4},{16,24},{20,28},{24,16},{28,20},{1,9},{5... | collective-permute-start | bytes 1769480 | tf_op jit(solution)/shard_map/ppermute | solution.py:325
  314.5 23.7 %collective-permute-start.83 = (bf16[2,2,192,384]{3,2,1,0:T(8,128)(2,1)S(1)}, bf16[2,2,192,384]{3,2,1,0:T(8,128)(2,1)S(1)}, u32[]{:S(2)}, u32[]{:S(2)}) collective-permute-start(bf16[2,2,192,384]{3,2,1,0:T(8,128)(2,1)S(1)} %slice_bitcast_fusion.9), channel_id=1, source_target_pairs={{0,16},{4,20},{8,24},{12,28},{16,0},{20,4},{24,8},{28,12},{1,17},{... | collective-permute-start | bytes 1769480 | tf_op jit(solution)/shard_map/ppermute | solution.py:325
  315.3 24.5 %collective-permute-start.86 = (bf16[2,2,192,384]{3,2,1,0:T(8,128)(2,1)S(1)}, bf16[2,2,192,384]{3,2,1,0:T(8,128)(2,1)S(1)}, u32[]{:S(2)}, u32[]{:S(2)}) collective-permute-start(bf16[2,2,192,384]{3,2,1,0:T(8,128)(2,1)S(1)} %slice_bitcast_fusion.7), channel_id=1, source_target_pairs={{0,8},{4,12},{8,0},{12,4},{16,24},{20,28},{24,16},{28,20},{1,9},{5... | collective-permute-start | bytes 1769480 | tf_op jit(solution)/shard_map/ppermute | solution.py:325
  316.8 48.8 %collective-permute-start.70 = (bf16[2,2,96,768]{3,2,1,0:T(8,128)(2,1)S(1)}, bf16[2,2,96,768]{3,2,1,0:T(8,128)(2,1)S(1)}, u32[]{:S(2)}, u32[]{:S(2)}) collective-permute-start(bf16[2,2,96,768]{3,2,1,0:T(8,128)(2,1)S(1)} %slice_bitcast_fusion.15), channel_id=1, source_target_pairs={{0,8},{4,12},{8,0},{12,4},{16,24},{20,28},{24,16},{28,20},{1,9},{5... | collective-permute-start | bytes 1769480 | tf_op jit(solution)/shard_map/ppermute | solution.py:325
  325.6 41.4 %collective-permute-start.67 = (bf16[2,2,96,768]{3,2,1,0:T(8,128)(2,1)S(1)}, bf16[2,2,96,768]{3,2,1,0:T(8,128)(2,1)S(1)}, u32[]{:S(2)}, u32[]{:S(2)}) collective-permute-start(bf16[2,2,96,768]{3,2,1,0:T(8,128)(2,1)S(1)} %slice_bitcast_fusion.17), channel_id=1, source_target_pairs={{0,16},{4,20},{8,24},{12,28},{16,0},{20,4},{24,8},{28,12},{1,17},{... | collective-permute-start | bytes 1769480 | tf_op jit(solution)/shard_map/ppermute | solution.py:325
  327.5 29.8 %collective-permute-start.79 = (bf16[2,96,768]{2,1,0:T(8,128)(2,1)S(1)}, bf16[2,96,768]{2,1,0:T(8,128)(2,1)S(1)}, u32[]{:S(2)}, u32[]{:S(2)}) collective-permute-start(bf16[2,96,768]{2,1,0:T(8,128)(2,1)S(1)} %fusion.20), channel_id=1, source_target_pairs={{0,16},{4,20},{8,24},{12,28},{16,0},{20,4},{24,8},{28,12},{1,17},{... | collective-permute-start | bytes 884744 | tf_op jit(solution)/shard_map/ppermute | solution.py:325
  338.3 20.4 %collective-permute-start.76 = (bf16[2,96,768]{2,1,0:T(8,128)(2,1)S(1)}, bf16[2,96,768]{2,1,0:T(8,128)(2,1)S(1)}, u32[]{:S(2)}, u32[]{:S(2)}) collective-permute-start(bf16[2,96,768]{2,1,0:T(8,128)(2,1)S(1)} %fusion.19), channel_id=1, source_target_pairs={{0,8},{4,12},{8,0},{12,4},{16,24},{20,28},{24,16},{28,20},{1,9},{5... | collective-permute-start | bytes 884744 | tf_op jit(solution)/shard_map/ppermute | solution.py:325
  340.0 21.2 %collective-permute-start.87 = (bf16[2,192,384]{2,1,0:T(8,128)(2,1)S(1)}, bf16[2,192,384]{2,1,0:T(8,128)(2,1)S(1)}, u32[]{:S(2)}, u32[]{:S(2)}) collective-permute-start(bf16[2,192,384]{2,1,0:T(8,128)(2,1)S(1)} %fusion.22), channel_id=1, source_target_pairs={{0,16},{4,20},{8,24},{12,28},{16,0},{20,4},{24,8},{28,12},{1,17},{... | collective-permute-start | bytes 884744 | tf_op jit(solution)/shard_map/ppermute | solution.py:325
  358.6 16.0 %collective-permute-start.80 = (bf16[96,768]{1,0:T(8,128)(2,1)S(1)}, bf16[96,768]{1,0:T(8,128)(2,1)S(1)}, u32[]{:S(2)}, u32[]{:S(2)}) collective-permute-start(bf16[96,768]{1,0:T(8,128)(2,1)S(1)} %get-tuple-element.116), channel_id=1, source_target_pairs={{0,2},{1,3},{2,0},{3,1},{4,6},{5,7},{6,4},{7,5},{8,10},{9,11},{10,... | collective-permute-start | bytes 442376 | tf_op jit(solution)/shard_map/ppermute | solution.py:325
  361.2 13.5 %collective-permute-start.81 = (bf16[96,768]{1,0:T(8,128)(2,1)S(1)}, bf16[96,768]{1,0:T(8,128)(2,1)S(1)}, u32[]{:S(2)}, u32[]{:S(2)}) collective-permute-start(bf16[96,768]{1,0:T(8,128)(2,1)S(1)} %get-tuple-element.117), channel_id=1, source_target_pairs={{0,3},{1,2},{2,1},{3,0},{4,7},{5,6},{6,5},{7,4},{8,11},{9,10},{10,... | collective-permute-start | bytes 442376 | tf_op jit(solution)/shard_map/ppermute | solution.py:325
  363.9 14.3 %collective-permute-start.77 = (bf16[96,768]{1,0:T(8,128)(2,1)S(1)}, bf16[96,768]{1,0:T(8,128)(2,1)S(1)}, u32[]{:S(2)}, u32[]{:S(2)}) collective-permute-start(bf16[96,768]{1,0:T(8,128)(2,1)S(1)} %fusion.32), channel_id=1, source_target_pairs={{0,1},{1,0},{2,3},{3,2},{4,5},{5,4},{6,7},{7,6},{8,9},{9,8},{10,11... | collective-permute-start | bytes 442376 | tf_op jit(solution)/shard_map/ppermute | solution.py:325
  365.6 20.4 %collective-permute-start.88 = (bf16[192,384]{1,0:T(8,128)(2,1)S(1)}, bf16[192,384]{1,0:T(8,128)(2,1)S(1)}, u32[]{:S(2)}, u32[]{:S(2)}) collective-permute-start(bf16[192,384]{1,0:T(8,128)(2,1)S(1)} %get-tuple-element.114), channel_id=1, source_target_pairs={{0,2},{1,3},{2,0},{3,1},{4,6},{5,7},{6,4},{7,5},{8,10},{9,11},{10,... | collective-permute-start | bytes 442376 | tf_op jit(solution)/shard_map/ppermute | solution.py:325
  367.4 13.4 %collective-permute-start.68 = (bf16[2,96,768]{2,1,0:T(8,128)(2,1)S(1)}, bf16[2,96,768]{2,1,0:T(8,128)(2,1)S(1)}, u32[]{:S(2)}, u32[]{:S(2)}) collective-permute-start(bf16[2,96,768]{2,1,0:T(8,128)(2,1)S(1)} %fusion.17), channel_id=1, source_target_pairs={{0,8},{4,12},{8,0},{12,4},{16,24},{20,28},{24,16},{28,20},{1,9},{5... | collective-permute-start | bytes 884744 | tf_op jit(solution)/shard_map/ppermute | solution.py:325
  374.7 12.9 %collective-permute-start.89 = (bf16[192,384]{1,0:T(8,128)(2,1)S(1)}, bf16[192,384]{1,0:T(8,128)(2,1)S(1)}, u32[]{:S(2)}, u32[]{:S(2)}) collective-permute-start(bf16[192,384]{1,0:T(8,128)(2,1)S(1)} %get-tuple-element.115), channel_id=1, source_target_pairs={{0,3},{1,2},{2,1},{3,0},{4,7},{5,6},{6,5},{7,4},{8,11},{9,10},{10,... | collective-permute-start | bytes 442376 | tf_op jit(solution)/shard_map/ppermute | solution.py:325
  374.7 12.9 %collective-permute-start.85 = (bf16[192,384]{1,0:T(8,128)(2,1)S(1)}, bf16[192,384]{1,0:T(8,128)(2,1)S(1)}, u32[]{:S(2)}, u32[]{:S(2)}) collective-permute-start(bf16[192,384]{1,0:T(8,128)(2,1)S(1)} %fusion.33), channel_id=1, source_target_pairs={{0,1},{1,0},{2,3},{3,2},{4,5},{5,4},{6,7},{7,6},{8,9},{9,8},{10,11... | collective-permute-start | bytes 442376 | tf_op jit(solution)/shard_map/ppermute | solution.py:325
  (103 other events, 1520.7 us)

commit v2 on v1

--- a/solution.py
+++ b/solution.py
@@ -311,12 +311,14 @@
 TOKENS = 256
 HALF = 128
 FF_SIDE = 384
+ROWS = WIDTH // BATCH
+MLP = WIDTH + 2 * FF_SIDE + 256
 SPAN = TOKENS * CTX
 TILE = 256
 LOW = jnp.bfloat16
 WIDE = jnp.float32
 CORE, XBIT, YBIT = 1, 2, 4
-SOURCES = (0, 0, 2, 2, 4, 4, 6, 6, 1, 1, 3, 3, 5, 5, 7, 7)
+SOURCES = (0, 2, 0, 4, 4, 6, 2, 6, 1, 3, 1, 5, 5, 7, 3, 7)
 VMEM_LIMIT = 56 * 1024 * 1024
 
 
@@ -355,72 +357,109 @@
     return inverse * (part - mean - normed * cross)
 
 
-def gather_weight(piece):
-    near, far, last = swap(piece, "ctx", 1), swap(piece, "ctx", 2), swap(piece, "ctx", 3)
+def exchange(value):
+    return swap(value, "ctx", 1), swap(value, "ctx", 2), swap(value, "ctx", 3)
+
+
+def gather_first(piece, parts):
+    near, far, last = parts
     one, two = jnp.stack([piece, near]), jnp.stack([far, last])
-    one_x, two_y = swap(one, "batch", XBIT), swap(two, "batch", YBIT)
-    one_y, two_x = swap(one, "batch", YBIT), swap(two, "batch", XBIT)
-    one_xy, two_xy = swap(one_x, "batch", YBIT), swap(two_y, "batch", XBIT)
-    held = [one, two, one_x, two_x, one_y, two_y, one_xy, two_xy]
+    return (one, two), (swap(one, "batch", XBIT), swap(two, "batch", YBIT))
+
+
+def gather_second(kept, came):
+    one, two = jnp.stack([kept[0], came[0]]), jnp.stack([kept[1], came[1]])
+    return [one, two, swap(one, "batch", YBIT), swap(two, "batch", XBIT)]
+
+
+def gather_last(held):
     return held + [swap(part, "batch", CORE) for part in held]
 
 
-def scatter_grad(mine, theirs):
-    came = swap(theirs, "batch", CORE)
+def scatter_first(mine, came):
     total = mine.astype(WIDE) + came.astype(WIDE)
     total = total.reshape((2, 2) + total.shape[1:])
     one, two = total[:, :, 0:2], total[:, :, 2:4]
-    one_back = swap(one[1].astype(LOW), "batch", YBIT)
-    two_back = swap(two[:, 1].astype(LOW), "batch", XBIT)
-    one = one[0] + one_back.astype(WIDE)
-    two = two[:, 0] + two_back.astype(WIDE)
-    one_back = swap(one[1].astype(LOW), "batch", XBIT)
-    two_back = swap(two[1].astype(LOW), "batch", YBIT)
-    one = one[0] + one_back.astype(WIDE)
-    two = two[0] + two_back.astype(WIDE)
-    near = swap(one[1].astype(LOW), "ctx", 1)
-    far = swap(two[0].astype(LOW), "ctx", 2)
-    last = swap(two[1].astype(LOW), "ctx", 3)
-    return one[0] + near.astype(WIDE) + (far.astype(WIDE) + last.astype(WIDE))
-
-
-def rows_place(held, batch, ctx):
-    size = WIDTH // BATCH
-    return held.at[ctx, pl.ds(pl.multiple_of(batch * size, 16), size), :]
-
-
-def columns_place(held, batch, ctx):
-    return held.at[batch, pl.ds(pl.multiple_of(ctx * GROUP, 16), GROUP), :]
-
-
-def load_weight(meta, parts, held, place, sems, lanes=None):
+    return (one[0], two[:, 0]), (one[1].astype(LOW), two[:, 1].astype(LOW))
+
+
+def swap_pair(pair, first, second):
+    return swap(pair[0], "batch", first), swap(pair[1], "batch", second)
+
+
+def scatter_second(kept, back):
+    one = kept[0] + back[0].astype(WIDE)
+    two = kept[1] + back[1].astype(WIDE)
+    return (one[0], two[0]), (one[1].astype(LOW), two[1].astype(LOW))
+
+
+def scatter_third(kept, back):
+    one = kept[0] + back[0].astype(WIDE)
+    two = kept[1] + back[1].astype(WIDE)
+    return one[0], (one[1].astype(LOW), two[0].astype(LOW), two[1].astype(LOW))
+
+
+def scatter_last(kept, sent):
+    near, far, last = (swap(part, "ctx", bit) for bit, part in zip((1, 2, 3), sent))
+    return kept + near.astype(WIDE) + (far.astype(WIDE) + last.astype(WIDE))
+
+
+def rows_of(index, size):
+    return pl.ds(pl.multiple_of(index * size, 16), size)
+
+
+def qkv_place(held, batch, ctx):
+    return [(pl.ds(0, 3 * GROUP), held.at[ctx, rows_of(batch, ROWS), :])]
+
+
+def mlp_place(held_out, held_fc, held_proj, batch, ctx):
+    return [
+        (pl.ds(WIDTH + 2 * FF_SIDE, TILE), held_out.at[ctx, rows_of(batch, ROWS), :]),
+        (pl.ds(0, WIDTH), held_fc.at[ctx, rows_of(batch, ROWS), :]),
+        (pl.ds(WIDTH, FF_SIDE), held_proj.at[batch, rows_of(2 * ctx, ROWS), :]),
+        (pl.ds(WIDTH + FF_SIDE, FF_SIDE), held_proj.at[batch, rows_of(2 * ctx + 1, ROWS), :]),
+    ]
+
+
+def load_weight(meta, parts, place, sems):
     copies = []
-    for index, (part, source) in enumerate(zip(parts, SOURCES)):
-        for half in range(2):
-            ctx = meta[1] ^ (2 * (index % 2) + half)
-            origin = part.at[half] if lanes is None else part.at[half, :, lanes]
-            copy = pltpu.make_async_copy(
-                origin, place(held, meta[0] ^ source, ctx), sems.at[2 * index + half]
-            )
-            copy.start()
-            copies.append(copy)
-    return copies
-
-
-def store_grad(meta, held, place, mine, theirs, sems):
+    for index, part in enumerate(parts):
+        for first in range(2):
+            for second in range(2):
+                batch = meta[0] ^ SOURCES[2 * index + first]
+                ctx = meta[1] ^ (2 * (index % 2) + second)
+                copies.append(
+                    [
+                        (part.at[first, second, :, lanes], target)
+                        for lanes, target in place(batch, ctx)
+                    ]
+                )
+    started = []
+    for kind in range(len(copies[0])):
+        group = []
+        for number, copy in enumerate(copies):
+            group.append(pltpu.make_async_copy(*copy[kind], sems.at[kind, number]))
+            group[-1].start()
+        started.append(group)
+    return started
+
+
+def store_grad(meta, place, mine, theirs, sems):
     copies = []
     for batch in range(BATCH):
         for ctx in range(CTX):
             target = theirs if batch % 2 else mine
-            copy = pltpu.make_async_copy(
-                place(held, meta[0] ^ batch, meta[1] ^ ctx),
-                target.at[batch // 2, ctx],
-                sems.at[batch * CTX + ctx],
-            )
-            copy.start()
-            copies.append(copy)
-    for copy in copies:
-        copy.wait()
+            ranges = place(meta[0] ^ batch, meta[1] ^ ctx)
+            for kind, (lanes, source) in enumerate(ranges):
+                copies.append(
+                    pltpu.make_async_copy(
+                        source,
+                        target.at[batch // 2, ctx, :, lanes],
+                        sems.at[kind, batch * CTX + ctx],
+                    )
+                )
+                copies[-1].start()
+    wait_all(copies)
 
 
 def wait_all(copies):
@@ -433,15 +472,24 @@
     return pl.ds(pl.multiple_of(first * HALF, HALF), HALF)
 
 
-def qkv_kernel(meta, x_ref, vec_ref, bias_ref, *refs):
-    parts, (h_ref, own, near, far, last, held, units, sems) = refs[:16], refs[16:]
-    copies = load_weight(meta, parts, held, rows_place, sems)
+def read_vectors(meta, parts, chunks):
+    for ctx, part in enumerate(parts):
+        chunks[meta[1] ^ ctx] = part[...].astype(WIDE)
+    return jnp.concatenate([chunks[index] for index in range(CTX)], axis=1)
+
+
+def qkv_kernel(meta, x_ref, *refs):
+    vectors, parts, refs = refs[:4], refs[4:12], refs[12:]
+    h_ref, own, near, far, last, held, units, chunks, sems = refs
+    (copies,) = load_weight(meta, parts, functools.partial(qkv_place, held), sems)
+    params = read_vectors(meta, vectors, chunks)
+    bias = jnp.concatenate([params[4:5], jnp.zeros((1, WIDTH), WIDE), params[5:6]], axis=1)
     centred, inverse = moments(x_ref[...].astype(WIDE))
-    normed = (centred * inverse * vec_ref[0:1] + vec_ref[1:2]).astype(LOW)
+    normed = (centred * inverse * params[0:1] + params[1:2]).astype(LOW)
     h_ref[...] = normed
     wait_all(copies)
     for chunk in range(CTX):
-        mixed = mm(normed, held[chunk, :, : 3 * GROUP]) + bias_ref[chunk]
+        mixed = mm(normed, held[chunk]) + bias[:, 3 * GROUP * chunk : 3 * GROUP * (chunk + 1)]
         mixed = mixed.astype(LOW)
         for part in range(3):
             unit = 3 * chunk + part
@@ -551,35 +599,35 @@
     write_sequence(meta, results, (dq, dk, dv))
 
 
-def middle_kernel(meta, x_ref, dy_ref, vec_ref, bias_ref, *refs):
-    pieces, refs = refs[:4], refs[4:]
-    parts_one, parts_two, parts_three, refs = refs[:16], refs[16:32], refs[32:48], refs[48:]
+def middle_kernel(meta, x_ref, dy_ref, *refs):
+    vectors, pieces, parts, refs = refs[:4], refs[4:8], refs[8:16], refs[16:]
     (out_ref, att_ref, h_ref, act_ref, dpre_ref, datt_ref, dmid_ref), refs = refs[:7], refs[7:]
     results, (rows_ref, dbias_ref), refs = refs[:4], refs[4:6], refs[6:]
-    out_parts, held_out, held_fc, held_proj, units, total, back, sem_one, sem_two, sem_three = refs
-    lanes = pl.ds(2 * TILE, TILE)
-    copies_one = load_weight(meta, parts_one, out_parts, rows_place, sem_one, lanes)
-    copies_two = load_weight(meta, parts_two, held_fc, rows_place, sem_two)
-    copies_three = load_weight(meta, parts_three, held_proj, columns_place, sem_three)
+    out_parts, held_out, held_fc, held_proj, units, total, back, chunks, bias, sems = refs
+    place = functools.partial(mlp_place, out_parts, held_fc, held_proj)
+    copies = load_weight(meta, parts, place, sems)
+    vec = read_vectors(meta, vectors, chunks)
+    for chunk in range(CTX):
+        bias[chunk] = vec[8 + chunk : 9 + chunk]
     for ctx, piece in enumerate(pieces):
         units[meta[1] ^ ctx] = piece[...]
     att = jnp.concatenate([units[index] for index in range(CTX)], axis=1)
     att_ref[...] = att
-    wait_all(copies_one)
+    wait_all(copies[0])
     for chunk in range(CTX):
-        held_out[:, chunk * GROUP : (chunk + 1) * GROUP] = out_parts[chunk, :, TILE - GROUP :]
-    mid = x_ref[...].astype(WIDE) + mm(att, held_out[...]) + vec_ref[6:7]
+        held_out[:, chunk * GROUP : (chunk + 1) * GROUP] = out_parts[chunk, :, :GROUP]
+    mid = x_ref[...].astype(WIDE) + mm(att, held_out[...]) + vec[6:7]
     centred, inverse = moments(mid)
     normed = centred * inverse
-    h_ref[...] = (normed * vec_ref[2:3] + vec_ref[3:4]).astype(LOW)
-    total[...] = mid + vec_ref[7:8]
+    h_ref[...] = (normed * vec[2:3] + vec[3:4]).astype(LOW)
+    total[...] = mid + vec[7:8]
     back[...] = jnp.zeros_like(back)
-    wait_all(copies_two)
-    wait_all(copies_three)
+    for group in copies[1:]:
+        wait_all(group)
     side = FF_SIDE
 
     def chunk_step(chunk, carry):
-        pre = mm(h_ref[...], held_fc[chunk]) + bias_ref[chunk]
+        pre = mm(h_ref[...], held_fc[chunk]) + bias[chunk]
         square = pre * pre
         tanh = jnp.tanh(0.7978845608028654 * (pre + 0.044715 * square * pre))
         act = (0.5 * pre * (1.0 + tanh)).astype(LOW)
@@ -602,7 +650,7 @@
     out_ref[...] = total[...].astype(LOW)
     grad = back[...]
     dy = dy_ref[...].astype(WIDE)
-    dmid = dy + norm_back(grad, normed, inverse, vec_ref[2:3])
+    dmid = dy + norm_back(grad, normed, inverse, vec[2:3])
     dmid_ref[...] = dmid
     datt = dmid.astype(LOW)
     datt_ref[...] = datt
@@ -618,53 +666,64 @@
         target[...] = units[meta[1] ^ ctx]
 
 
-def proj_grad_kernel(meta, dy_ref, act_ref, mine, theirs, held, sems):
-    left = turned(dy_ref[...])
+def mlp_grad_kernel(meta, dy_ref, act_ref, h_ref, dpre_ref, att_ref, datt_ref, *refs):
+    mine, theirs, held_out, held_fc, held_proj, sems = refs
+    dy, h_two, att = turned(dy_ref[...]), turned(h_ref[...]), turned(att_ref[...])
     for chunk in range(CTX):
+        proj = mm(dy, act_ref[chunk]).astype(LOW)
         for half in range(2):
-            held[2 * chunk + half] = mm(
-                left, act_ref[chunk, :, half * FF_SIDE : (half + 1) * FF_SIDE]
-            ).astype(LOW)
-    store_grad(meta, held, columns_place, mine, theirs, sems)
-
-
-def fc_grad_kernel(meta, h_ref, dpre_ref, mine, theirs, held, sems):
-    left = turned(h_ref[...])
+            held_proj[2 * chunk + half] = proj[:, half * FF_SIDE : (half + 1) * FF_SIDE]
+        held_fc[chunk] = mm(h_two, dpre_ref[chunk]).astype(LOW)
+    grad = mm(att, datt_ref[...]).astype(LOW)
     for chunk in range(CTX):
-        held[chunk] = mm(left, dpre_ref[chunk]).astype(LOW)
-    store_grad(meta, held, rows_place, mine, theirs, sems)
-
-
-def qkv_grad_kernel(meta, h_ref, att_ref, datt_ref, *refs):
+        held_out[chunk, :, :GROUP] = grad[:, chunk * GROUP : (chunk + 1) * GROUP]
+        held_out[chunk, :, GROUP:] = jnp.zeros((WIDTH, TILE - GROUP), LOW)
+    place = functools.partial(mlp_place, held_out, held_fc, held_proj)
+    store_grad(meta, place, mine, theirs, sems)
+
+
+def qkv_grad_kernel(meta, h_ref, *refs):
     pieces, (mine, theirs, mixed_ref, dbias_ref, held, units, sems) = refs[:4], refs[4:]
     for ctx, piece in enumerate(pieces):
         for part in range(3):
             units[CTX * part + (meta[1] ^ ctx)] = piece[:, part * GROUP : (part + 1) * GROUP]
-    left, att = turned(h_ref[...]), turned(att_ref[...])
+    left = turned(h_ref[...])
     for chunk in range(CTX):
         mixed = jnp.concatenate([units[3 * chunk + part] for part in range(3)], axis=1)
         mixed_ref[chunk] = mixed
-        dbias_ref[chunk] = jnp.sum(mixed.astype(WIDE), axis=0, keepdims=True)
-        held[chunk, :, : 3 * GROUP] = mm(left, mixed).astype(LOW)
-        held[chunk, :, 3 * GROUP :] = mm(
-            att, datt_ref[:, chunk * GROUP : (chunk + 1) * GROUP]
-        ).astype(LOW)
-    store_grad(meta, held, rows_place, mine, theirs, sems)
-
-
-def input_grad_kernel(meta, x_ref, vec_ref, dmid_ref, mixed_ref, *refs):
-    parts, (grad_ref, rows_ref, held, sems) = refs[:16], refs[16:]
-    copies = load_weight(meta, parts, held, rows_place, sems)
+        bias = jnp.sum(mixed.astype(WIDE), axis=0, keepdims=True)
+        for part in range(3):
+            dbias_ref[3 * chunk + part] = bias[:, part * GROUP : (part + 1) * GROUP]
+        held[chunk] = mm(left, mixed).astype(LOW)
+    store_grad(meta, functools.partial(qkv_place, held), mine, theirs, sems)
+
+
+def input_grad_kernel(meta, x_ref, dmid_ref, mixed_ref, rows_ref, dfc_ref, dqkv_ref, *refs):
+    vectors, parts, refs = refs[:4], refs[4:12], refs[12:]
+    grad_ref, results, (held, chunks, rows, sums, sems) = refs[0], refs[1:5], refs[5:]
+    (copies,) = load_weight(meta, parts, functools.partial(qkv_place, held), sems)
+    params = read_vectors(meta, vectors, chunks)
     centred, inverse = moments(x_ref[...].astype(WIDE))
     normed = centred * inverse
     wait_all(copies)
     grad = jnp.zeros((TOKENS, WIDTH), WIDE)
     for chunk in range(CTX):
-        grad = grad + mt(mixed_ref[chunk], held[chunk, :, : 3 * GROUP])
-    grad_ref[...] = dmid_ref[...] + norm_back(grad, normed, inverse, vec_ref[0:1])
-    rows_ref[0:1] = jnp.sum(grad * normed, axis=0, keepdims=True)
-    rows_ref[1:2] = jnp.sum(grad, axis=0, keepdims=True)
-    rows_ref[2:8] = jnp.zeros((6, WIDTH), WIDE)
+        grad = grad + mt(mixed_ref[chunk], held[chunk])
+    grad_ref[...] = dmid_ref[...] + norm_back(grad, normed, inverse, params[0:1])
+    rows[0:1] = jnp.sum(grad * normed, axis=0, keepdims=True)
+    rows[1:2] = jnp.sum(grad, axis=0, keepdims=True)
+    rows[2:4] = rows_ref[0:2]
+    for chunk in range(CTX):
+        lanes = slice(chunk * GROUP, (chunk + 1) * GROUP)
+        rows[4:5, lanes] = dqkv_ref[chunk]
+        rows[5:6, lanes] = dqkv_ref[2 * CTX + chunk]
+        rows[8 + chunk : 9 + chunk] = dfc_ref[chunk]
+    rows[6:8] = rows_ref[2:4]
+    rows[12:16] = jnp.zeros((4, WIDTH), WIDE)
+    for chunk in range(CTX):
+        sums[chunk] = rows[:, chunk * GROUP : (chunk + 1) * GROUP]
+    for ctx, target in enumerate(results):
+        target[...] = sums[meta[1] ^ ctx]
 
 
 def shape_of(dtype, *dims):
@@ -715,37 +774,58 @@
     meta = jnp.stack([batch, ctx]).astype(jnp.int32)
     inputs = block_in.reshape(TOKENS, WIDTH)
     grad_low = cotangent.reshape(TOKENS, WIDTH)
-    order = ctx ^ jnp.arange(CTX, dtype=jnp.int32)
-    rows = WIDTH // BATCH
-    dma = pltpu.SemaphoreType.DMA((BATCH * CTX,))
-    held_shape = pltpu.VMEM((CTX, WIDTH, WIDTH), LOW)
-    proj_shape = pltpu.VMEM((BATCH, WIDTH, FF_SIDE), LOW)
-
-    low_vec = vectors.astype(LOW)
-    vec_parts = jnp.stack([low_vec] + [swap(low_vec, "ctx", bit) for bit in (1, 2, 3)])
-    params = vec_parts[order].astype(WIDE).transpose(1, 0, 2).reshape(12, WIDTH)
-    qkv_bias = jnp.concatenate([params[4], jnp.zeros((WIDTH,), WIDE), params[5]])
-    qkv_bias = qkv_bias.reshape(CTX, 1, 3 * GROUP)
-    fc_bias = params[8:12].reshape(CTX, 1, WIDTH)
-
-    piece_one = jnp.concatenate([w_qkv.astype(LOW), w_out.astype(LOW)], axis=1)
-    parts_one = gather_weight(piece_one)
-    parts_two = gather_weight(w_fc.astype(LOW))
-    parts_three = gather_weight(w_proj.astype(LOW).T)
+    tie = lax.optimization_barrier
+
+    qkv_sems = pltpu.SemaphoreType.DMA((1, BATCH * CTX))
+    mlp_sems = pltpu.SemaphoreType.DMA((4, BATCH * CTX))
+    qkv_held = pltpu.VMEM((CTX, WIDTH, 3 * GROUP), LOW)
+    mlp_held = [
+        pltpu.VMEM((CTX, WIDTH, TILE), LOW),
+        pltpu.VMEM((CTX, WIDTH, WIDTH), LOW),
+        pltpu.VMEM((BATCH, WIDTH, FF_SIDE), LOW),
+    ]
+    vec_held = pltpu.VMEM((CTX, 16, GROUP), WIDE)
+
+    piece_one = w_qkv.astype(LOW)
+    low_proj = w_proj.astype(LOW).T
+    piece_two = jnp.concatenate(
+        [
+            w_fc.astype(LOW),
+            low_proj[:ROWS],
+            low_proj[ROWS:],
+            w_out.astype(LOW),
+            jnp.zeros((ROWS, TILE - GROUP), LOW),
+        ],
+        axis=1,
+    )
+    low_vec = jnp.pad(vectors.astype(LOW), ((0, 4), (0, 0)))
+    parts_one = exchange(piece_one)
+    vec_parts = (low_vec,) + exchange(low_vec)
+    piece_two, _ = tie((piece_two, parts_one))
+    parts_two = exchange(piece_two)
+    parts_one = gather_second(*gather_first(piece_one, parts_one))
+    parts_two, _ = tie((parts_two, parts_one))
+    parts_one = gather_last(parts_one)
+    kept_two, came_two = gather_first(piece_two, parts_two)
 
     packed = shape_of(LOW, TOKENS, 3 * GROUP)
     single = shape_of(LOW, TOKENS, GROUP)
+    tokens_low = shape_of(LOW, TOKENS, WIDTH)
+    hidden_low = shape_of(LOW, CTX, TOKENS, WIDTH)
     square = WIDTH * WIDTH
     h_one, own, *sent = call(
         qkv_kernel,
-        (meta, inputs, params, qkv_bias, *parts_one),
-        "svvv" + "a" * 16,
-        [shape_of(LOW, TOKENS, WIDTH)] + [packed] * 4,
+        (meta, inputs, *vec_parts, *parts_one),
+        "s" + "v" * 5 + "a" * 8,
+        [tokens_low] + [packed] * 4,
         "v" * 5,
-        [held_shape, pltpu.VMEM((CTX, TOKENS, 3 * GROUP), LOW), dma],
+        [qkv_held, pltpu.VMEM((CTX, TOKENS, 3 * GROUP), LOW), vec_held, qkv_sems],
         2 * TOKENS * 3 * square,
     )
     qkv_pieces = [own] + [swap(part, "ctx", bit) for bit, part in zip((1, 2, 3), sent)]
+
+    qkv_pieces, came_two = tie((qkv_pieces, came_two))
+    parts_two = gather_second(kept_two, came_two)
 
     sequence_low = pltpu.VMEM((SPAN, GROUP), LOW)
     sequence_wide = pltpu.VMEM((SPAN, GROUP), WIDE)
@@ -758,76 +838,47 @@
         [sequence_low] * 3 + [sequence_wide],
         2 * SPAN * SPAN * GROUP * 2,
     )
+    parts_two, _ = tie((parts_two, own))
+    parts_two = gather_last(parts_two)
     att_pieces = [own] + [swap(part, "ctx", bit) for bit, part in zip((1, 2, 3), sent)]
 
-    tokens_low = shape_of(LOW, TOKENS, WIDTH)
-    hidden_low = shape_of(LOW, CTX, TOKENS, WIDTH)
     out, att, h_two, act, dpre, datt, dmid, own, *sent = call(
         middle_kernel,
-        (
-            meta,
-            inputs,
-            grad_low,
-            params,
-            fc_bias,
-            *att_pieces,
-            *parts_one,
-            *parts_two,
-            *parts_three,
-        ),
-        "svvvv" + "v" * 4 + "a" * 48,
-        [
-            tokens_low,
-            tokens_low,
-            tokens_low,
-            hidden_low,
-            hidden_low,
-            tokens_low,
-            shape_of(WIDE, TOKENS, WIDTH),
-        ]
+        (meta, inputs, grad_low, *vec_parts, *att_pieces, *parts_two),
+        "s" + "v" * 10 + "a" * 8,
+        [tokens_low] * 3
+        + [hidden_low] * 2
+        + [tokens_low, shape_of(WIDE, TOKENS, WIDTH)]
         + [single] * 4
         + [shape_of(WIDE, 8, WIDTH), shape_of(WIDE, CTX, 1, WIDTH)],
         "v" * 13,
-        [
-            pltpu.VMEM((CTX, WIDTH, TILE), LOW),
-            pltpu.VMEM((WIDTH, WIDTH), LOW),
-            held_shape,
-            proj_shape,
+        mlp_held[:1]
+        + [pltpu.VMEM((WIDTH, WIDTH), LOW)]
+        + mlp_held[1:]
+        + [
             pltpu.VMEM((CTX, TOKENS, GROUP), LOW),
             pltpu.VMEM((TOKENS, WIDTH), WIDE),
             pltpu.VMEM((TOKENS, WIDTH), WIDE),
-            dma,
-            dma,
-            dma,
+            vec_held,
+            pltpu.VMEM((CTX, 1, WIDTH), WIDE),
+            mlp_sems,
         ],
         2 * TOKENS * 18 * square,
     )
     sent, (rows_two, dbias_fc) = sent[:3], sent[3:]
     grad_pieces = [own] + [swap(part, "ctx", bit) for bit, part in zip((1, 2, 3), sent)]
 
-    row_parts = [shape_of(LOW, BATCH // 2, CTX, rows, WIDTH)] * 2
-    column_parts = [shape_of(LOW, BATCH // 2, CTX, GROUP, FF_SIDE)] * 2
-    proj_parts = call(
-        proj_grad_kernel,
-        (meta, grad_low, act),
-        "svv",
-        column_parts,
+    mlp_mine, mlp_theirs = call(
+        mlp_grad_kernel,
+        (meta, grad_low, act, h_two, dpre, att, datt),
+        "s" + "v" * 6,
+        [shape_of(LOW, BATCH // 2, CTX, ROWS, MLP)] * 2,
         "aa",
-        [proj_shape, dma],
-        2 * TOKENS * 4 * square,
-    )
-    proj_grad = scatter_grad(*proj_parts)
-    fc_parts = call(
-        fc_grad_kernel,
-        (meta, h_two, dpre),
-        "svv",
-        row_parts,
-        "aa",
-        [held_shape, dma],
-        2 * TOKENS * 4 * square,
-    )
-    fc_grad = scatter_grad(*fc_parts)
-
+        mlp_held + [mlp_sems],
+        2 * TOKENS * 9 * square,
+    )
+    mlp_mine, mlp_theirs, grad_pieces = tie((mlp_mine, mlp_theirs, grad_pieces))
+    mlp_came = swap(mlp_theirs, "batch", CORE)
     own, *sent = call(
         attend_back_kernel,
         (meta, *qkv_pieces, *grad_pieces),
@@ -837,46 +888,56 @@
         [sequence_low] * 4 + [sequence_wide] * 3,
         2 * SPAN * SPAN * GROUP * 5,
     )
+    mlp_came, own, sent = tie((mlp_came, own, sent))
     mixed_pieces = [own] + [swap(part, "ctx", bit) for bit, part in zip((1, 2, 3), sent)]
-
-    mine, theirs, mixed, dbias_qkv = call(
+    mlp_kept, mlp_sent = scatter_first(mlp_mine, mlp_came)
+    mlp_kept, mlp_sent, mixed_pieces = tie((mlp_kept, mlp_sent, mixed_pieces))
+    mlp_back = swap_pair(mlp_sent, YBIT, XBIT)
+
+    qkv_mine, qkv_theirs, mixed, dbias_qkv = call(
         qkv_grad_kernel,
-        (meta, h_one, att, datt, *mixed_pieces),
-        "svvv" + "v" * 4,
-        row_parts + [shape_of(LOW, CTX, TOKENS, 3 * GROUP), shape_of(WIDE, CTX, 1, 3 * GROUP)],
+        (meta, h_one, *mixed_pieces),
+        "s" + "v" * 5,
+        [shape_of(LOW, BATCH // 2, CTX, ROWS, 3 * GROUP)] * 2
+        + [shape_of(LOW, CTX, TOKENS, 3 * GROUP), shape_of(WIDE, 3 * CTX, 1, GROUP)],
         "aavv",
-        [held_shape, pltpu.VMEM((3 * CTX, TOKENS, GROUP), LOW), dma],
-        2 * TOKENS * 4 * square,
-    )
-    one_grad = scatter_grad(mine, theirs)
-    grad_input, rows_one = call(
+        [qkv_held, pltpu.VMEM((3 * CTX, TOKENS, GROUP), LOW), qkv_sems],
+        2 * TOKENS * 3 * square,
+    )
+    qkv_came = swap(qkv_theirs, "batch", CORE)
+    grad_input, own, *sent = call(
         input_grad_kernel,
-        (meta, inputs, params, dmid, mixed, *parts_one),
-        "svvvv" + "a" * 16,
-        [shape_of(WIDE, TOKENS, WIDTH), shape_of(WIDE, 8, WIDTH)],
-        "vv",
-        [held_shape, dma],
+        (meta, inputs, dmid, mixed, rows_two, dbias_fc, dbias_qkv, *vec_parts, *parts_one),
+        "s" + "v" * 10 + "a" * 8,
+        [shape_of(WIDE, TOKENS, WIDTH)] + [shape_of(WIDE, 16, GROUP)] * 4,
+        "v" * 5,
+        [qkv_held, vec_held, pltpu.VMEM((16, WIDTH), WIDE), vec_held, qkv_sems],
         2 * TOKENS * 3 * square,
     )
-
-    dbias_qkv = dbias_qkv.reshape(3, WIDTH)
-    vec_rows = jnp.concatenate(
-        [
-            rows_one[0:2],
-            rows_two[0:2],
-            dbias_qkv[0:1],
-            dbias_qkv[2:3],
-            rows_two[2:4],
-            dbias_fc.reshape(4, WIDTH),
-        ],
-        axis=0,
-    )
-    vec_rows = vec_rows.reshape(12, CTX, GROUP).transpose(1, 0, 2)[order]
-    vec_grad = vec_rows[0] + sum(swap(vec_rows[bit], "ctx", bit) for bit in (1, 2, 3))
+    mlp_back, own = tie((mlp_back, own))
+    mlp_kept, mlp_sent = scatter_second(mlp_kept, mlp_back)
+    mlp_back = swap_pair(mlp_sent, XBIT, YBIT)
+    qkv_kept, qkv_sent = scatter_first(qkv_mine, qkv_came)
+    qkv_back = swap_pair(qkv_sent, YBIT, XBIT)
+    mlp_back, qkv_back = tie((mlp_back, qkv_back))
+    mlp_kept, mlp_sent = scatter_third(mlp_kept, mlp_back)
+    qkv_kept, qkv_sent = scatter_second(qkv_kept, qkv_back)
+    qkv_back = swap_pair(qkv_sent, XBIT, YBIT)
+    mlp_grad = scatter_last(mlp_kept, mlp_sent)
+    qkv_kept, qkv_sent = scatter_third(qkv_kept, qkv_back)
+    qkv_grad = scatter_last(qkv_kept, qkv_sent)
+
+    vec_grad = own + sum(swap(part, "ctx", bit) for bit, part in zip((1, 2, 3), sent))
     for bit in (CORE, XBIT, YBIT):
         vec_grad = vec_grad + swap(vec_grad, "batch", bit)
-
-    qkv_grad, out_grad = one_grad[:, : 3 * GROUP], one_grad[:, 3 * GROUP :]
+    vec_grad = vec_grad[:12]
+    fc_grad = mlp_grad[:, :WIDTH]
+    proj_grad = jnp.concatenate(
+        [mlp_grad[:, WIDTH : WIDTH + FF_SIDE], mlp_grad[:, WIDTH + FF_SIDE : WIDTH + 2 * FF_SIDE]],
+        axis=0,
+    )
+    out_grad = mlp_grad[:, WIDTH + 2 * FF_SIDE : WIDTH + 2 * FF_SIDE + GROUP]
+
     qkv_m, qkv_s, qkv_w = adamw(w_qkv, qkv_grad, qkv_first, qkv_second, 0.06, 0.1)
     out_m, out_s, out_w = adamw(w_out, out_grad, out_first, out_second, 0.06, 0.1)
     fc_m, fc_s, fc_w = adamw(w_fc, fc_grad, fc_first, fc_second, 0.06, 0.1)

time: 397 us -> 368 us (0.927)
  starting transfers between devices: 124 us -> 91.7 us
  waiting for transfers between devices: 156 us -> 164 us
  local copies, waits for them, and re-layouts: 16.2 us -> 12.2 us
    ppermute x96 -> x59, starting transfers between devices: 124 us -> 91.7 us  [swap(): return lax.ppermute(value, axis, [(i, i ^ bit) for i in range(size)])]
    ppermute x96 -> x59, waiting for transfers between devices: 156 us -> 164 us  [swap(): return lax.ppermute(value, axis, [(i, i ^ bit) for i in range(size)])]
    another operation x14 -> x11, other arithmetic: 2.87 us -> 6.92 us  [the longest x8 5.79 us: gather_second(): one, two = (jnp.stack([kept[0], came[0]]), jnp.stack([kept[1], came[1]]))]
    add x11 -> x9, other arithmetic: 6.09 us -> 8.63 us  [the longest x2 6.1 us: scatter_first(): total = mine.astype(WIDE) + came.astype(WIDE)]
    pallas_call x8 -> x7, Pallas kernels: 76.9 us -> 74.9 us  [call(): pl.pallas_call(kernel, out_shape=tuple(outputs), in_specs=[spec[kind] for...]
  transfers between devices with their start and end apart: 96 -> 59, of which waited for: 38 -> 26; matrix products, arithmetic and copies ran while one was open for 8% -> 4% of each run, Pallas kernels for 14% -> 16%
where the time goes in v2:
time: 368 us; the launch traced here: 367 us
  waiting for transfers between devices  164 us (45%)
  starting transfers between devices  91.7 us (25%)
  Pallas kernels  74.9 us (20%)
  other arithmetic  22.7 us (6%)
  local copies, waits for them, and re-layouts  12.2 us (3%)
    ppermute x59, waiting for transfers between devices, swap(): return lax.ppermute(value, axis, [(i, i ^ bit) for i in range(size)])  164 us
    ppermute x59, starting transfers between devices, swap(): return lax.ppermute(value, axis, [(i, i ^ bit) for i in range(size)])  91.7 us
    pallas_call x7, Pallas kernels, call(): pl.pallas_call(kernel, out_shape=tuple(outputs), in_specs=[spec[kind] for...  74.9 us
  transfers between devices with their start and end apart: 59, of which 26 were waited for; matrix products, arithmetic and copies ran while one was open for 4% of the time, Pallas kernels for 16%

profile of v2, /device:TPU:0, one launch (start us, length us, event | category | flops | bytes accessed | tf_op | source)
XLA Modules:
  0.0 367.4 jit_solution(18340835346111438015)
XLA Ops:
  1.7 4.1 %collective-permute-start.5 = (bf16[96,576]{1,0:T(8,128)(2,1)S(1)}, bf16[96,576]{1,0:T(8,128)(2,1)S(1)}, u32[]{:S(2)}, u32[]{:S(2)}) collective-permute-start(bf16[96,576]{1,0:T(8,128)(2,1)S(1)} %convert_element_type.128), channel_id=1, source_target_pairs={{0,2},{1,3},{2,0},{3,1},{4,6},{5,7},{6,4},{7,5},{8,10},{9,11},{10,... | collective-permute-start | bytes 331784 | tf_op jit(solution)/shard_map/ppermute | solution.py:327
  5.8 1.6 collective-permute-start.3
  8.3 3.8 %collective-permute-done.3 = bf16[96,576]{1,0:T(8,128)(2,1)S(1)} collective-permute-done((bf16[96,576]{1,0:T(8,128)(2,1)S(1)}, bf16[96,576]{1,0:T(8,128)(2,1)S(1)}, u32[]{:S(2)}, u32[]{:S(2)}) %collective-permute-start.3) | collective-permute-done | bytes 110624 | tf_op jit(solution)/shard_map/ppermute | solution.py:327
  12.2 1.6 collective-permute-start.4
  13.8 1.8 collective-permute-done.6
  15.6 1.6 collective-permute-start.7
  18.2 4.3 %collective-permute-done.7 = bf16[2,96,576]{2,1,0:T(8,128)(2,1)S(1)} collective-permute-done((bf16[2,96,576]{2,1,0:T(8,128)(2,1)S(1)}, bf16[2,96,576]{2,1,0:T(8,128)(2,1)S(1)}, u32[]{:S(2)}, u32[]{:S(2)}) %collective-permute-start.7) | collective-permute-done | bytes 221216 | tf_op jit(solution)/shard_map/ppermute | solution.py:327
  22.6 1.6 collective-permute-start.9
  24.2 1.6 collective-permute-start.8
  26.0 2.5 collective-permute-start.19
  28.4 2.9 collective-permute-start.18
  31.8 5.7 %collective-permute-done.19 = bf16[96,1792]{1,0:T(8,128)(2,1)S(1)} collective-permute-done((bf16[96,1792]{1,0:T(8,128)(2,1)S(1)}, bf16[96,1792]{1,0:T(8,128)(2,1)S(1)}, u32[]{:S(2)}, u32[]{:S(2)}) %collective-permute-start.19) | collective-permute-done | bytes 344096 | tf_op jit(solution)/shard_map/ppermute | solution.py:327
  37.6 3.5 collective-permute-start.2
  41.0 16.6 %collective-permute-done.18 = bf16[96,1792]{1,0:T(8,128)(2,1)S(1)} collective-permute-done((bf16[96,1792]{1,0:T(8,128)(2,1)S(1)}, bf16[96,1792]{1,0:T(8,128)(2,1)S(1)}, u32[]{:S(2)}, u32[]{:S(2)}) %collective-permute-start.18) | collective-permute-done | bytes 344096 | tf_op jit(solution)/shard_map/ppermute | solution.py:327
  57.7 2.9 collective-permute-start
  62.5 1.9 fusion.26
  67.0 6.2 %shard_map.296 = (bf16[256,768]{1,0:T(8,128)(2,1)}, bf16[256,576]{1,0:T(8,128)(2,1)}, bf16[256,576]{1,0:T(8,128)(2,1)}, bf16[256,576]{1,0:T(8,128)(2,1)}, bf16[256,576]{1,0:T(8,128)(2,1)}) custom-call(s32[2]{0:T(128)} %pad_add_fusion.meta, bf16[256,768]{1,0:T(8,128)(2,1)} %bitcast.124, bf16[16,192]{1,0:T(8,128)(2,1)} %copy-done.25, ...), custom_call_target="tpu_custom_call" | custom-call | flops 905969664 | bytes 5529608 | tf_op jit(solution)/shard_map/pallas_call | solution.py:741
  73.4 2.5 collective-permute-start.15
  75.9 1.8 collective-permute-start.16
  77.7 4.7 %collective-permute-done.20 = bf16[2,96,1792]{2,1,0:T(8,128)(2,1)} collective-permute-done((bf16[2,96,1792]{2,1,0:T(8,128)(2,1)}, bf16[2,96,1792]{2,1,0:T(8,128)(2,1)}, u32[]{:S(2)}, u32[]{:S(2)}) %collective-permute-start.20) | collective-permute-done | bytes 688160 | tf_op jit(solution)/shard_map/ppermute | solution.py:327
  83.5 5.6 %collective-permute-done.14.refs_1_ = bf16[256,576]{1,0:T(8,128)(2,1)S(1)} collective-permute-done((bf16[256,576]{1,0:T(8,128)(2,1)}, bf16[256,576]{1,0:T(8,128)(2,1)S(1)}, u32[]{:S(2)}, u32[]{:S(2)}) %collective-permute-start.14) | collective-permute-done | bytes 294944 | tf_op jit(solution)/shard_map/ppermute | solution.py:327
  89.0 10.2 %collective-permute-done.15.refs_2_ = bf16[256,576]{1,0:T(8,128)(2,1)S(1)} collective-permute-done((bf16[256,576]{1,0:T(8,128)(2,1)}, bf16[256,576]{1,0:T(8,128)(2,1)S(1)}, u32[]{:S(2)}, u32[]{:S(2)}) %collective-permute-start.15) | collective-permute-done | bytes 294944 | tf_op jit(solution)/shard_map/ppermute | solution.py:327
  100.7 1.6 collective-permute-start.26
  103.5 1.6 collective-permute-start.25
  105.1 12.4 %shard_map.297 = (bf16[256,192]{1,0:T(8,128)(2,1)}, bf16[256,192]{1,0:T(8,128)(2,1)}, bf16[256,192]{1,0:T(8,128)(2,1)}, bf16[256,192]{1,0:T(8,128)(2,1)}) custom-call(s32[2]{0:T(128)} %pad_add_fusion.meta, bf16[256,576]{1,0:T(8,128)(2,1)} %get-tuple-element.102.refs_0_, bf16[256,576]{1,0:T(8,128)(2,1)} %copy-done.40, bf16[256,576]{1,0:T(8,128)(2,1)} %copy-done.41, ...), custom_call_target="tpu_custom_call" | custom-call | flops 805306368 | bytes 1572872 | tf_op jit(solution)/shard_map/pallas_call | solution.py:741
  117.5 12.9 %collective-permute-done.26.refs_11_ = bf16[2,2,96,1792]{3,2,1,0:T(8,128)(2,1)S(1)} collective-permute-done((bf16[2,2,96,1792]{3,2,1,0:T(8,128)(2,1)S(1)}, bf16[2,2,96,1792]{3,2,1,0:T(8,128)(2,1)S(1)}, u32[]{:S(2)}, u32[]{:S(2)}) %collective-permute-start.26) | collective-permute-done | bytes 1376288 | tf_op jit(solution)/shard_map/ppermute | solution.py:327
  130.4 2.5 collective-permute-done.25.refs_10_
  133.9 7.5 %collective-permute-start.22 = (bf16[256,192]{1,0:T(8,128)(2,1)}, bf16[256,192]{1,0:T(8,128)(2,1)S(1)}, u32[]{:S(2)}, u32[]{:S(2)}) collective-permute-start(bf16[256,192]{1,0:T(8,128)(2,1)} %get-tuple-element.107), channel_id=1, source_target_pairs={{0,1},{1,0},{2,3},{3,2},{4,5},{5,4},{6,7},{7,6},{8,9},{9,8},{10,11... | collective-permute-start | bytes 294920 | tf_op jit(solution)/shard_map/ppermute | solution.py:327
  141.4 3.9 %collective-permute-done.22.refs_5_ = bf16[256,192]{1,0:T(8,128)(2,1)S(1)} collective-permute-done((bf16[256,192]{1,0:T(8,128)(2,1)}, bf16[256,192]{1,0:T(8,128)(2,1)S(1)}, u32[]{:S(2)}, u32[]{:S(2)}) %collective-permute-start.22) | collective-permute-done | bytes 98336 | tf_op jit(solution)/shard_map/ppermute | solution.py:327
  145.3 2.9 collective-permute-start.23
  148.2 6.0 %collective-permute-done.23.refs_6_ = bf16[256,192]{1,0:T(8,128)(2,1)S(1)} collective-permute-done((bf16[256,192]{1,0:T(8,128)(2,1)}, bf16[256,192]{1,0:T(8,128)(2,1)S(1)}, u32[]{:S(2)}, u32[]{:S(2)}) %collective-permute-start.23) | collective-permute-done | bytes 98336 | tf_op jit(solution)/shard_map/ppermute | solution.py:327
  154.2 2.8 collective-permute-start.24
  157.0 4.3 %collective-permute-done.24.refs_7_ = bf16[256,192]{1,0:T(8,128)(2,1)S(1)} collective-permute-done((bf16[256,192]{1,0:T(8,128)(2,1)}, bf16[256,192]{1,0:T(8,128)(2,1)S(1)}, u32[]{:S(2)}, u32[]{:S(2)}) %collective-permute-start.24) | collective-permute-done | bytes 98336 | tf_op jit(solution)/shard_map/ppermute | solution.py:327
  164.0 16.1 %shard_map.298 = (bf16[256,768]{1,0:T(8,128)(2,1)}, bf16[256,768]{1,0:T(8,128)(2,1)}, bf16[256,768]{1,0:T(8,128)(2,1)}, bf16[4,256,768]{2,1,0:T(8,128)(2,1)}, bf...) custom-call(s32[2]{0:T(128)} %pad_add_fusion.meta, ...), custom_call_target="tpu_custom_call" | custom-call | flops 5435817984 | bytes 18149384 | tf_op jit(solution)/shard_map/pallas_call | solution.py:741
  181.2 2.3 collective-permute-start.32
  184.6 10.7 %shard_map.299 = (bf16[4,4,96,1792]{3,2,1,0:T(8,128)(2,1)}, bf16[4,4,96,1792]{3,2,1,0:T(8,128)(2,1)}) custom-call(s32[2]{0:T(128)} %pad_add_fusion.meta, bf16[256,768]{1,0:T(8,128)(2,1)} %bitcast.138, bf16[4,256,768]{2,1,0:T(8,128)(2,1)} %get-tuple-element.119.act_ref, bf16[256,768]{1,0:T(8,128)(2,1)} %get-tuple-element.120.h_ref, ...), custom_call_target="tpu_custom_call" | custom-call | flops 2717908992 | bytes 15728648 | tf_op jit(solution)/shard_map/pallas_call | solution.py:741
  196.0 15.9 %shard_map.300 = (bf16[256,576]{1,0:T(8,128)(2,1)}, bf16[256,576]{1,0:T(8,128)(2,1)}, bf16[256,576]{1,0:T(8,128)(2,1)}, bf16[256,576]{1,0:T(8,128)(2,1)}) custom-call(s32[2]{0:T(128)} %pad_add_fusion.meta, bf16[256,576]{1,0:T(8,128)(2,1)} %get-tuple-element.102.refs_0_, bf16[256,576]{1,0:T(8,128)(2,1)} %copy-done.40, bf16[256,576]{1,0:T(8,128)(2,1)} %copy-done.41, ...), custom_call_target="tpu_custom_call" | custom-call | flops 2013265920 | bytes 2752520 | tf_op jit(solution)/shard_map/pallas_call | solution.py:741
  212.0 2.4 copy-done.2
  214.4 5.6 %convert_add_fusion = f32[4,4,96,1792]{3,2,1,0:T(8,128)S(1)} fusion(bf16[4,4,96,1792]{3,2,1,0:T(8,128)(2,1)} %copy-done.2, bf16[4,4,96,1792]{3,2,1,0:T(8,128)(2,1)} %get-tuple-element.130), kind=kLoop, calls=%fused_computation.1 | loop fusion | flops 8257536 | bytes 22020096 | tf_op jit(solution)/shard_map/add | solution.py:380
  220.1 1.8 slice_bitcast_fusion
  221.9 1.8 slice_bitcast_fusion.1
  223.8 3.2 collective-permute-start.36
  229.3 10.3 %collective-permute-done.35.refs_1_ = bf16[256,576]{1,0:T(8,128)(2,1)S(1)} collective-permute-done((bf16[256,576]{1,0:T(8,128)(2,1)S(1)}, bf16[256,576]{1,0:T(8,128)(2,1)S(1)}, u32[]{:S(2)}, u32[]{:S(2)}) %collective-permute-start.35) | collective-permute-done | bytes 294944 | tf_op jit(solution)/shard_map/ppermute | solution.py:327
  239.6 10.0 %collective-permute-done.36.refs_2_ = bf16[256,576]{1,0:T(8,128)(2,1)S(1)} collective-permute-done((bf16[256,576]{1,0:T(8,128)(2,1)S(1)}, bf16[256,576]{1,0:T(8,128)(2,1)S(1)}, u32[]{:S(2)}, u32[]{:S(2)}) %collective-permute-start.36) | collective-permute-done | bytes 294944 | tf_op jit(solution)/shard_map/ppermute | solution.py:327
  249.5 1.6 collective-permute-start.39
  251.8 6.5 %shard_map.301 = (bf16[4,4,96,576]{3,2,1,0:T(8,128)(2,1)}, bf16[4,4,96,576]{3,2,1,0:T(8,128)(2,1)}, bf16[4,256,576]{2,1,0:T(8,128)(2,1)}, f32[12,1,192]{2,1,0:T(1,128)}) custom-call(s32[2]{0:T(128)} %pad_add_fusion.meta, bf16[256,768]{1,0:T(8,128)(2,1)} %get-tuple-element.118.h_ref, bf16[256,576]{1,0:T(8,128)(2,1)} %get-tuple-element.145.refs_0_, ...), custom_call_target="tpu_custom_call" | custom-call | flops 905969664 | bytes 6300680 | tf_op jit(solution)/shard_map/pallas_call | solution.py:741
  258.4 7.0 %shard_map.302 = (f32[256,768]{1,0:T(8,128)}, f32[16,192]{1,0:T(8,128)}, f32[16,192]{1,0:T(8,128)}, f32[16,192]{1,0:T(8,128)}, f32[16,192]{1,0:T(8,128)}) custom-call(s32[2]{0:T(128)} %pad_add_fusion.meta, bf16[256,768]{1,0:T(8,128)(2,1)} %bitcast.126, f32[256,768]{1,0:T(8,128)} %get-tuple-element.117.dmid_ref, ...), custom_call_target="tpu_custom_call" | custom-call | flops 905969664 | bytes 6804488 | tf_op jit(solution)/shard_map/pallas_call | solution.py:741
  265.5 14.5 %collective-permute-done.39 = bf16[2,2,96,1792]{3,2,1,0:T(8,128)(2,1)} collective-permute-done((bf16[2,2,96,1792]{3,2,1,0:T(8,128)(2,1)}, bf16[2,2,96,1792]{3,2,1,0:T(8,128)(2,1)}, u32[]{:S(2)}, u32[]{:S(2)}) %collective-permute-start.39) | collective-permute-done | bytes 1376288 | tf_op jit(solution)/shard_map/ppermute | solution.py:327
  280.9 1.7 convert_add_fusion.3
  285.3 1.5 collective-permute-start.43
  288.1 7.6 %collective-permute-start.53 = (f32[16,192]{1,0:T(8,128)S(1)}, f32[16,192]{1,0:T(8,128)S(1)}, u32[]{:S(2)}, u32[]{:S(2)}) collective-permute-start(f32[16,192]{1,0:T(8,128)S(1)} %copy-done.57), channel_id=1, source_target_pairs={{0,1},{1,0},{2,3},{3,2},{4,5},{5,4},{6,7},{7,6},{8,9},{9,8},{10,11... | collective-permute-start | bytes 36872 | tf_op jit(solution)/shard_map/ppermute | solution.py:327
  295.7 1.9 collective-permute-done.53
  297.6 2.8 collective-permute-start.54
  300.4 1.8 collective-permute-done.54
  302.2 2.4 collective-permute-start.55
  304.6 3.1 collective-permute-done.55
  309.7 3.1 collective-permute-done.57
  314.0 1.5 collective-permute-start.47
  316.3 4.0 %collective-permute-start.50 = (bf16[96,1792]{1,0:T(8,128)(2,1)S(1)}, bf16[96,1792]{1,0:T(8,128)(2,1)S(1)}, u32[]{:S(2)}, u32[]{:S(2)}) collective-permute-start(bf16[96,1792]{1,0:T(8,128)(2,1)S(1)} %fusion.12), channel_id=1, source_target_pairs={{0,1},{1,0},{2,3},{3,2},{4,5},{5,4},{6,7},{7,6},{8,9},{9,8},{10,11... | collective-permute-start | bytes 1032200 | tf_op jit(solution)/shard_map/ppermute | solution.py:327
  321.3 1.9 collective-permute-start.52
  323.3 3.2 collective-permute-start.48
  326.6 1.9 collective-permute-start.49
  328.5 29.9 %collective-permute-done.48 = bf16[96,576]{1,0:T(8,128)(2,1)S(1)} collective-permute-done((bf16[96,576]{1,0:T(8,128)(2,1)S(1)}, bf16[96,576]{1,0:T(8,128)(2,1)S(1)}, u32[]{:S(2)}, u32[]{:S(2)}) %collective-permute-start.48) | collective-permute-done | bytes 110624 | tf_op jit(solution)/shard_map/ppermute | solution.py:327
  359.1 4.2 %collective-permute-done.46 = bf16[96,576]{1,0:T(8,128)(2,1)S(1)} collective-permute-done((bf16[96,576]{1,0:T(8,128)(2,1)S(1)}, bf16[96,576]{1,0:T(8,128)(2,1)S(1)}, u32[]{:S(2)}, u32[]{:S(2)}) %collective-permute-start.46) | collective-permute-done | bytes 110624 | tf_op jit(solution)/shard_map/ppermute | solution.py:327
  (229 shorter events, 36.7 us)
Async XLA Ops:
  1.7 12.1 %collective-permute-start.5 = (bf16[96,576]{1,0:T(8,128)(2,1)S(1)}, bf16[96,576]{1,0:T(8,128)(2,1)S(1)}, u32[]{:S(2)}, u32[]{:S(2)}) collective-permute-start(bf16[96,576]{1,0:T(8,128)(2,1)S(1)} %convert_element_type.128), channel_id=1, source_target_pairs={{0,2},{1,3},{2,0},{3,1},{4,6},{5,7},{6,4},{7,5},{8,10},{9,11},{10,... | collective-permute-start | bytes 331784 | tf_op jit(solution)/shard_map/ppermute | solution.py:327
  5.8 6.4 %collective-permute-start.3 = (bf16[96,576]{1,0:T(8,128)(2,1)S(1)}, bf16[96,576]{1,0:T(8,128)(2,1)S(1)}, u32[]{:S(2)}, u32[]{:S(2)}) collective-permute-start(bf16[96,576]{1,0:T(8,128)(2,1)S(1)} %convert_element_type.128), channel_id=1, source_target_pairs={{0,1},{1,0},{2,3},{3,2},{4,5},{5,4},{6,7},{7,6},{8,9},{9,8},{10,11... | collective-permute-start | bytes 331784 | tf_op jit(solution)/shard_map/ppermute | solution.py:327
  7.4 8.2 %collective-permute-start.6 = (bf16[96,576]{1,0:T(8,128)(2,1)S(1)}, bf16[96,576]{1,0:T(8,128)(2,1)S(1)}, u32[]{:S(2)}, u32[]{:S(2)}) collective-permute-start(bf16[96,576]{1,0:T(8,128)(2,1)S(1)} %convert_element_type.128), channel_id=1, source_target_pairs={{0,3},{1,2},{2,1},{3,0},{4,7},{5,6},{6,5},{7,4},{8,11},{9,10},{10,... | collective-permute-start | bytes 331784 | tf_op jit(solution)/shard_map/ppermute | solution.py:327
  12.2 11.9 %collective-permute-start.4 = (bf16[2,96,576]{2,1,0:T(8,128)(2,1)S(1)}, bf16[2,96,576]{2,1,0:T(8,128)(2,1)S(1)}, u32[]{:S(2)}, u32[]{:S(2)}) collective-permute-start(bf16[2,96,576]{2,1,0:T(8,128)(2,1)S(1)} %get-tuple-element.201), channel_id=1, source_target_pairs={{0,8},{4,12},{8,0},{12,4},{16,24},{20,28},{24,16},{28,20},{1,9},{5... | collective-permute-start | bytes 663560 | tf_op jit(solution)/shard_map/ppermute | solution.py:327
  15.6 6.9 %collective-permute-start.7 = (bf16[2,96,576]{2,1,0:T(8,128)(2,1)S(1)}, bf16[2,96,576]{2,1,0:T(8,128)(2,1)S(1)}, u32[]{:S(2)}, u32[]{:S(2)}) collective-permute-start(bf16[2,96,576]{2,1,0:T(8,128)(2,1)S(1)} %get-tuple-element.199), channel_id=1, source_target_pairs={{0,16},{4,20},{8,24},{12,28},{16,0},{20,4},{24,8},{28,12},{1,17},{... | collective-permute-start | bytes 663560 | tf_op jit(solution)/shard_map/ppermute | solution.py:327
  22.6 38.0 %collective-permute-start.9 = (bf16[2,2,96,576]{3,2,1,0:T(8,128)(2,1)S(1)}, bf16[2,2,96,576]{3,2,1,0:T(8,128)(2,1)S(1)}, u32[]{:S(2)}, u32[]{:S(2)}) collective-permute-start(bf16[2,2,96,576]{3,2,1,0:T(8,128)(2,1)S(1)} %pad_maximum_fusion.5.refs_5_), channel_id=1, source_target_pairs={{0,8},{4,12},{8,0},{12,4},{16,24},{20,28},{24,16},{28,20},{1,9},{5... | collective-permute-start | bytes 1327112 | tf_op jit(solution)/shard_map/ppermute | solution.py:327
  24.2 36.4 %collective-permute-start.8 = (bf16[2,2,96,576]{3,2,1,0:T(8,128)(2,1)S(1)}, bf16[2,2,96,576]{3,2,1,0:T(8,128)(2,1)S(1)}, u32[]{:S(2)}, u32[]{:S(2)}) collective-permute-start(bf16[2,2,96,576]{3,2,1,0:T(8,128)(2,1)S(1)} %pad_maximum_fusion.4.refs_4_), channel_id=1, source_target_pairs={{0,16},{4,20},{8,24},{12,28},{16,0},{20,4},{24,8},{28,12},{1,17},{... | collective-permute-start | bytes 1327112 | tf_op jit(solution)/shard_map/ppermute | solution.py:327
  26.0 11.6 %collective-permute-start.19 = (bf16[96,1792]{1,0:T(8,128)(2,1)S(1)}, bf16[96,1792]{1,0:T(8,128)(2,1)S(1)}, u32[]{:S(2)}, u32[]{:S(2)}) collective-permute-start(bf16[96,1792]{1,0:T(8,128)(2,1)S(1)} %concatenate.6), channel_id=1, source_target_pairs={{0,3},{1,2},{2,1},{3,0},{4,7},{5,6},{6,5},{7,4},{8,11},{9,10},{10,... | collective-permute-start | bytes 1032200 | tf_op jit(solution)/shard_map/ppermute | solution.py:327
  28.4 29.2 %collective-permute-start.18 = (bf16[96,1792]{1,0:T(8,128)(2,1)S(1)}, bf16[96,1792]{1,0:T(8,128)(2,1)S(1)}, u32[]{:S(2)}, u32[]{:S(2)}) collective-permute-start(bf16[96,1792]{1,0:T(8,128)(2,1)S(1)} %concatenate.6), channel_id=1, source_target_pairs={{0,2},{1,3},{2,0},{3,1},{4,6},{5,7},{6,4},{7,5},{8,10},{9,11},{10,... | collective-permute-start | bytes 1032200 | tf_op jit(solution)/shard_map/ppermute | solution.py:327
  31.3 26.4 %collective-permute-start.17 = (bf16[96,1792]{1,0:T(8,128)(2,1)S(1)}, bf16[96,1792]{1,0:T(8,128)(2,1)S(1)}, u32[]{:S(2)}, u32[]{:S(2)}) collective-permute-start(bf16[96,1792]{1,0:T(8,128)(2,1)S(1)} %concatenate.6), channel_id=1, source_target_pairs={{0,1},{1,0},{2,3},{3,2},{4,5},{5,4},{6,7},{7,6},{8,9},{9,8},{10,11... | collective-permute-start | bytes 1032200 | tf_op jit(solution)/shard_map/ppermute | solution.py:327
  37.6 24.4 %collective-permute-start.2 = (bf16[16,192]{1,0:T(8,128)(2,1)S(1)}, bf16[16,192]{1,0:T(8,128)(2,1)S(1)}, u32[]{:S(2)}, u32[]{:S(2)}) collective-permute-start(bf16[16,192]{1,0:T(8,128)(2,1)S(1)} %pad.4.refs_0_), channel_id=1, source_target_pairs={{0,3},{1,2},{2,1},{3,0},{4,7},{5,6},{6,5},{7,4},{8,11},{9,10},{10,... | collective-permute-start | bytes 18440 | tf_op jit(solution)/shard_map/ppermute | solution.py:327
  57.7 4.6 %collective-permute-start.1 = (bf16[16,192]{1,0:T(8,128)(2,1)S(1)}, bf16[16,192]{1,0:T(8,128)(2,1)S(1)}, u32[]{:S(2)}, u32[]{:S(2)}) collective-permute-start(bf16[16,192]{1,0:T(8,128)(2,1)S(1)} %pad.4.refs_0_), channel_id=1, source_target_pairs={{0,2},{1,3},{2,0},{3,1},{4,6},{5,7},{6,4},{7,5},{8,10},{9,11},{10,... | collective-permute-start | bytes 18440 | tf_op jit(solution)/shard_map/ppermute | solution.py:327
  57.7 6.8 %collective-permute-start = (bf16[16,192]{1,0:T(8,128)(2,1)S(1)}, bf16[16,192]{1,0:T(8,128)(2,1)S(1)}, u32[]{:S(2)}, u32[]{:S(2)}) collective-permute-start(bf16[16,192]{1,0:T(8,128)(2,1)S(1)} %pad.4.refs_0_), channel_id=1, source_target_pairs={{0,1},{1,0},{2,3},{3,2},{4,5},{5,4},{6,7},{7,6},{8,9},{9,8},{10,11... | collective-permute-start | bytes 18440 | tf_op jit(solution)/shard_map/ppermute | solution.py:327
  60.5 4.5 %collective-permute-start.11 = (bf16[2,2,96,576]{3,2,1,0:T(8,128)(2,1)S(1)}, bf16[2,2,96,576]{3,2,1,0:T(8,128)(2,1)S(1)}, u32[]{:S(2)}, u32[]{:S(2)}) collective-permute-start(bf16[2,2,96,576]{3,2,1,0:T(8,128)(2,1)S(1)} %pad_maximum_fusion.5.refs_5_), channel_id=1, source_target_pairs={{0,4},{4,0},{8,12},{12,8},{16,20},{20,16},{24,28},{28,24},{1,5},{5... | collective-permute-start | bytes 1327112 | tf_op jit(solution)/shard_map/ppermute | solution.py:327
  60.6 6.4 %collective-permute-start.10 = (bf16[2,2,96,576]{3,2,1,0:T(8,128)(2,1)S(1)}, bf16[2,2,96,576]{3,2,1,0:T(8,128)(2,1)}, u32[]{:S(2)}, u32[]{:S(2)}) collective-permute-start(bf16[2,2,96,576]{3,2,1,0:T(8,128)(2,1)S(1)} %pad_maximum_fusion.4.refs_4_), channel_id=1, source_target_pairs={{0,4},{4,0},{8,12},{12,8},{16,20},{20,16},{24,28},{28,24},{1,5},{5... | collective-permute-start | bytes 1327112 | tf_op jit(solution)/shard_map/ppermute | solution.py:327
  62.0 4.9 %collective-permute-start.13 = (bf16[2,2,96,576]{3,2,1,0:T(8,128)(2,1)S(1)}, bf16[2,2,96,576]{3,2,1,0:T(8,128)(2,1)}, u32[]{:S(2)}, u32[]{:S(2)}) collective-permute-start(bf16[2,2,96,576]{3,2,1,0:T(8,128)(2,1)S(1)} %collective-permute-done.9.refs_7_), channel_id=1, source_target_pairs={{0,4},{4,0},{8,12},{12,8},{16,20},{20,16},{24,28},{28,24},{1,5},{5... | collective-permute-start | bytes 1327112 | tf_op jit(solution)/shard_map/ppermute | solution.py:327
  62.3 4.7 %collective-permute-start.12 = (bf16[2,2,96,576]{3,2,1,0:T(8,128)(2,1)S(1)}, bf16[2,2,96,576]{3,2,1,0:T(8,128)(2,1)}, u32[]{:S(2)}, u32[]{:S(2)}) collective-permute-start(bf16[2,2,96,576]{3,2,1,0:T(8,128)(2,1)S(1)} %collective-permute-done.8.refs_6_), channel_id=1, source_target_pairs={{0,4},{4,0},{8,12},{12,8},{16,20},{20,16},{24,28},{28,24},{1,5},{5... | collective-permute-start | bytes 1327112 | tf_op jit(solution)/shard_map/ppermute | solution.py:327
  64.5 18.0 %collective-permute-start.20 = (bf16[2,96,1792]{2,1,0:T(8,128)(2,1)}, bf16[2,96,1792]{2,1,0:T(8,128)(2,1)}, u32[]{:S(2)}, u32[]{:S(2)}) collective-permute-start(bf16[2,96,1792]{2,1,0:T(8,128)(2,1)} %get-tuple-element.195), channel_id=1, source_target_pairs={{0,8},{4,12},{8,0},{12,4},{16,24},{20,28},{24,16},{28,20},{1,9},{5... | collective-permute-start | bytes 2064392 | tf_op jit(solution)/shard_map/ppermute | solution.py:327
  65.9 17.6 %collective-permute-start.21 = (bf16[2,96,1792]{2,1,0:T(8,128)(2,1)}, bf16[2,96,1792]{2,1,0:T(8,128)(2,1)}, u32[]{:S(2)}, u32[]{:S(2)}) collective-permute-start(bf16[2,96,1792]{2,1,0:T(8,128)(2,1)} %get-tuple-element.193), channel_id=1, source_target_pairs={{0,16},{4,20},{8,24},{12,28},{16,0},{20,4},{24,8},{28,12},{1,17},{... | collective-permute-start | bytes 2064392 | tf_op jit(solution)/shard_map/ppermute | solution.py:327
  73.3 15.7 %collective-permute-start.14 = (bf16[256,576]{1,0:T(8,128)(2,1)}, bf16[256,576]{1,0:T(8,128)(2,1)S(1)}, u32[]{:S(2)}, u32[]{:S(2)}) collective-permute-start(bf16[256,576]{1,0:T(8,128)(2,1)} %get-tuple-element.95), channel_id=1, source_target_pairs={{0,1},{1,0},{2,3},{3,2},{4,5},{5,4},{6,7},{7,6},{8,9},{9,8},{10,11... | collective-permute-start | bytes 884744 | tf_op jit(solution)/shard_map/ppermute | solution.py:327
  73.4 25.8 %collective-permute-start.15 = (bf16[256,576]{1,0:T(8,128)(2,1)}, bf16[256,576]{1,0:T(8,128)(2,1)S(1)}, u32[]{:S(2)}, u32[]{:S(2)}) collective-permute-start(bf16[256,576]{1,0:T(8,128)(2,1)} %get-tuple-element.96), channel_id=1, source_target_pairs={{0,2},{1,3},{2,0},{3,1},{4,6},{5,7},{6,4},{7,5},{8,10},{9,11},{10,... | collective-permute-start | bytes 884744 | tf_op jit(solution)/shard_map/ppermute | solution.py:327
  75.9 23.3 %collective-permute-start.16 = (bf16[256,576]{1,0:T(8,128)(2,1)}, bf16[256,576]{1,0:T(8,128)(2,1)S(1)}, u32[]{:S(2)}, u32[]{:S(2)}) collective-permute-start(bf16[256,576]{1,0:T(8,128)(2,1)} %get-tuple-element.97), channel_id=1, source_target_pairs={{0,3},{1,2},{2,1},{3,0},{4,7},{5,6},{6,5},{7,4},{8,11},{9,10},{10,... | collective-permute-start | bytes 884744 | tf_op jit(solution)/shard_map/ppermute | solution.py:327
  100.7 29.7 %collective-permute-start.26 = (bf16[2,2,96,1792]{3,2,1,0:T(8,128)(2,1)S(1)}, bf16[2,2,96,1792]{3,2,1,0:T(8,128)(2,1)S(1)}, u32[]{:S(2)}, u32[]{:S(2)}) collective-permute-start(bf16[2,2,96,1792]{3,2,1,0:T(8,128)(2,1)S(1)} %pad_maximum_fusion.1.refs_9_), channel_id=1, source_target_pairs={{0,8},{4,12},{8,0},{12,4},{16,24},{20,28},{24,16},{28,20},{1,9},{5... | collective-permute-start | bytes 4128776 | tf_op jit(solution)/shard_map/ppermute | solution.py:327
  103.5 60.5 %copy-start.11 = (bf16[2,2,96,1792]{3,2,1,0:T(8,128)(2,1)}, bf16[2,2,96,1792]{3,2,1,0:T(8,128)(2,1)S(1)}, u32[]{:S(2)}) copy-start(bf16[2,2,96,1792]{3,2,1,0:T(8,128)(2,1)S(1)} %pad_maximum_fusion.refs_8_) | copy-start | bytes 4128772
  103.5 29.4 %collective-permute-start.25 = (bf16[2,2,96,1792]{3,2,1,0:T(8,128)(2,1)S(1)}, bf16[2,2,96,1792]{3,2,1,0:T(8,128)(2,1)S(1)}, u32[]{:S(2)}, u32[]{:S(2)}) collective-permute-start(bf16[2,2,96,1792]{3,2,1,0:T(8,128)(2,1)S(1)} %pad_maximum_fusion.refs_8_), channel_id=1, source_target_pairs={{0,16},{4,20},{8,24},{12,28},{16,0},{20,4},{24,8},{28,12},{1,17},{... | collective-permute-start | bytes 4128776 | tf_op jit(solution)/shard_map/ppermute | solution.py:327
  132.9 28.3 %collective-permute-start.27 = (bf16[2,2,96,1792]{3,2,1,0:T(8,128)(2,1)S(1)}, bf16[2,2,96,1792]{3,2,1,0:T(8,128)(2,1)S(1)}, u32[]{:S(2)}, u32[]{:S(2)}) collective-permute-start(bf16[2,2,96,1792]{3,2,1,0:T(8,128)(2,1)S(1)} %pad_maximum_fusion.refs_8_), channel_id=1, source_target_pairs={{0,4},{4,0},{8,12},{12,8},{16,20},{20,16},{24,28},{28,24},{1,5},{5... | collective-permute-start | bytes 4128776 | tf_op jit(solution)/shard_map/ppermute | solution.py:327
  132.9 28.3 %collective-permute-start.28 = (bf16[2,2,96,1792]{3,2,1,0:T(8,128)(2,1)S(1)}, bf16[2,2,96,1792]{3,2,1,0:T(8,128)(2,1)S(1)}, u32[]{:S(2)}, u32[]{:S(2)}) collective-permute-start(bf16[2,2,96,1792]{3,2,1,0:T(8,128)(2,1)S(1)} %pad_maximum_fusion.1.refs_9_), channel_id=1, source_target_pairs={{0,4},{4,0},{8,12},{12,8},{16,20},{20,16},{24,28},{28,24},{1,5},{5... | collective-permute-start | bytes 4128776 | tf_op jit(solution)/shard_map/ppermute | solution.py:327
  133.4 27.9 %collective-permute-start.29 = (bf16[2,2,96,1792]{3,2,1,0:T(8,128)(2,1)S(1)}, bf16[2,2,96,1792]{3,2,1,0:T(8,128)(2,1)S(1)}, u32[]{:S(2)}, u32[]{:S(2)}) collective-permute-start(bf16[2,2,96,1792]{3,2,1,0:T(8,128)(2,1)S(1)} %collective-permute-done.25.refs_10_), channel_id=1, source_target_pairs={{0,4},{4,0},{8,12},{12,8},{16,20},{20,16},{24,28},{28,24},{1,5},{5... | collective-permute-start | bytes 4128776 | tf_op jit(solution)/shard_map/ppermute | solution.py:327
  133.5 27.8 %collective-permute-start.30 = (bf16[2,2,96,1792]{3,2,1,0:T(8,128)(2,1)S(1)}, bf16[2,2,96,1792]{3,2,1,0:T(8,128)(2,1)S(1)}, u32[]{:S(2)}, u32[]{:S(2)}) collective-permute-start(bf16[2,2,96,1792]{3,2,1,0:T(8,128)(2,1)S(1)} %collective-permute-done.26.refs_11_), channel_id=1, source_target_pairs={{0,4},{4,0},{8,12},{12,8},{16,20},{20,16},{24,28},{28,24},{1,5},{5... | collective-permute-start | bytes 4128776 | tf_op jit(solution)/shard_map/ppermute | solution.py:327
  133.9 11.4 %collective-permute-start.22 = (bf16[256,192]{1,0:T(8,128)(2,1)}, bf16[256,192]{1,0:T(8,128)(2,1)S(1)}, u32[]{:S(2)}, u32[]{:S(2)}) collective-permute-start(bf16[256,192]{1,0:T(8,128)(2,1)} %get-tuple-element.107), channel_id=1, source_target_pairs={{0,1},{1,0},{2,3},{3,2},{4,5},{5,4},{6,7},{7,6},{8,9},{9,8},{10,11... | collective-permute-start | bytes 294920 | tf_op jit(solution)/shard_map/ppermute | solution.py:327
  145.3 8.9 %collective-permute-start.23 = (bf16[256,192]{1,0:T(8,128)(2,1)}, bf16[256,192]{1,0:T(8,128)(2,1)S(1)}, u32[]{:S(2)}, u32[]{:S(2)}) collective-permute-start(bf16[256,192]{1,0:T(8,128)(2,1)} %get-tuple-element.108), channel_id=1, source_target_pairs={{0,2},{1,3},{2,0},{3,1},{4,6},{5,7},{6,4},{7,5},{8,10},{9,11},{10,... | collective-permute-start | bytes 294920 | tf_op jit(solution)/shard_map/ppermute | solution.py:327
  154.2 7.0 %collective-permute-start.24 = (bf16[256,192]{1,0:T(8,128)(2,1)}, bf16[256,192]{1,0:T(8,128)(2,1)S(1)}, u32[]{:S(2)}, u32[]{:S(2)}) collective-permute-start(bf16[256,192]{1,0:T(8,128)(2,1)} %get-tuple-element.109), channel_id=1, source_target_pairs={{0,3},{1,2},{2,1},{3,0},{4,7},{5,6},{6,5},{7,4},{8,11},{9,10},{10,... | collective-permute-start | bytes 294920 | tf_op jit(solution)/shard_map/ppermute | solution.py:327
  180.1 15.2 %collective-permute-start.31 = (bf16[256,192]{1,0:T(8,128)(2,1)}, bf16[256,192]{1,0:T(8,128)(2,1)S(1)}, u32[]{:S(2)}, u32[]{:S(2)}) collective-permute-start(bf16[256,192]{1,0:T(8,128)(2,1)} %get-tuple-element.127), channel_id=1, source_target_pairs={{0,1},{1,0},{2,3},{3,2},{4,5},{5,4},{6,7},{7,6},{8,9},{9,8},{10,11... | collective-permute-start | bytes 294920 | tf_op jit(solution)/shard_map/ppermute | solution.py:327
  181.2 14.1 %collective-permute-start.32 = (bf16[256,192]{1,0:T(8,128)(2,1)}, bf16[256,192]{1,0:T(8,128)(2,1)S(1)}, u32[]{:S(2)}, u32[]{:S(2)}) collective-permute-start(bf16[256,192]{1,0:T(8,128)(2,1)} %get-tuple-element.128), channel_id=1, source_target_pairs={{0,2},{1,3},{2,0},{3,1},{4,6},{5,7},{6,4},{7,5},{8,10},{9,11},{10,... | collective-permute-start | bytes 294920 | tf_op jit(solution)/shard_map/ppermute | solution.py:327
  183.5 11.9 %collective-permute-start.33 = (bf16[256,192]{1,0:T(8,128)(2,1)}, bf16[256,192]{1,0:T(8,128)(2,1)S(1)}, u32[]{:S(2)}, u32[]{:S(2)}) collective-permute-start(bf16[256,192]{1,0:T(8,128)(2,1)} %get-tuple-element.129), channel_id=1, source_target_pairs={{0,3},{1,2},{2,1},{3,0},{4,7},{5,6},{6,5},{7,4},{8,11},{9,10},{10,... | collective-permute-start | bytes 294920 | tf_op jit(solution)/shard_map/ppermute | solution.py:327
  195.4 16.6 %collective-permute-start.34 = (bf16[4,4,96,1792]{3,2,1,0:T(8,128)(2,1)}, bf16[4,4,96,1792]{3,2,1,0:T(8,128)(2,1)S(1)}, u32[]{:S(2)}, u32[]{:S(2)}) collective-permute-start(bf16[4,4,96,1792]{3,2,1,0:T(8,128)(2,1)} %get-tuple-element.131), channel_id=1, source_target_pairs={{0,4},{4,0},{8,12},{12,8},{16,20},{20,16},{24,28},{28,24},{1,5},{5... | collective-permute-start | bytes 16515080 | tf_op jit(solution)/shard_map/ppermute | solution.py:327
  223.7 15.9 %collective-permute-start.35 = (bf16[256,576]{1,0:T(8,128)(2,1)S(1)}, bf16[256,576]{1,0:T(8,128)(2,1)S(1)}, u32[]{:S(2)}, u32[]{:S(2)}) collective-permute-start(bf16[256,576]{1,0:T(8,128)(2,1)S(1)} %copy-done.46), channel_id=1, source_target_pairs={{0,1},{1,0},{2,3},{3,2},{4,5},{5,4},{6,7},{7,6},{8,9},{9,8},{10,11... | collective-permute-start | bytes 884744 | tf_op jit(solution)/shard_map/ppermute | solution.py:327
  223.8 25.8 %collective-permute-start.36 = (bf16[256,576]{1,0:T(8,128)(2,1)S(1)}, bf16[256,576]{1,0:T(8,128)(2,1)S(1)}, u32[]{:S(2)}, u32[]{:S(2)}) collective-permute-start(bf16[256,576]{1,0:T(8,128)(2,1)S(1)} %copy-done.44), channel_id=1, source_target_pairs={{0,2},{1,3},{2,0},{3,1},{4,6},{5,7},{6,4},{7,5},{8,10},{9,11},{10,... | collective-permute-start | bytes 884744 | tf_op jit(solution)/shard_map/ppermute | solution.py:327
  226.9 22.6 %collective-permute-start.37 = (bf16[256,576]{1,0:T(8,128)(2,1)S(1)}, bf16[256,576]{1,0:T(8,128)(2,1)S(1)}, u32[]{:S(2)}, u32[]{:S(2)}) collective-permute-start(bf16[256,576]{1,0:T(8,128)(2,1)S(1)} %copy-done.43), channel_id=1, source_target_pairs={{0,3},{1,2},{2,1},{3,0},{4,7},{5,6},{6,5},{7,4},{8,11},{9,10},{10,... | collective-permute-start | bytes 884744 | tf_op jit(solution)/shard_map/ppermute | solution.py:327
  249.5 30.4 %collective-permute-start.39 = (bf16[2,2,96,1792]{3,2,1,0:T(8,128)(2,1)}, bf16[2,2,96,1792]{3,2,1,0:T(8,128)(2,1)}, u32[]{:S(2)}, u32[]{:S(2)}) collective-permute-start(bf16[2,2,96,1792]{3,2,1,0:T(8,128)(2,1)} %slice_bitcast_fusion.5), channel_id=1, source_target_pairs={{0,16},{4,20},{8,24},{12,28},{16,0},{20,4},{24,8},{28,12},{1,17},{... | collective-permute-start | bytes 4128776 | tf_op jit(solution)/shard_map/ppermute | solution.py:327
  251.1 29.8 %collective-permute-start.40 = (bf16[2,2,96,1792]{3,2,1,0:T(8,128)(2,1)S(1)}, bf16[2,2,96,1792]{3,2,1,0:T(8,128)(2,1)S(1)}, u32[]{:S(2)}, u32[]{:S(2)}) collective-permute-start(bf16[2,2,96,1792]{3,2,1,0:T(8,128)(2,1)S(1)} %slice_bitcast_fusion.4), channel_id=1, source_target_pairs={{0,8},{4,12},{8,0},{12,4},{16,24},{20,28},{24,16},{28,20},{1,9},{5... | collective-permute-start | bytes 4128776 | tf_op jit(solution)/shard_map/ppermute | solution.py:327
  258.3 26.3 %collective-permute-start.38 = (bf16[4,4,96,576]{3,2,1,0:T(8,128)(2,1)}, bf16[4,4,96,576]{3,2,1,0:T(8,128)(2,1)S(1)}, u32[]{:S(2)}, u32[]{:S(2)}) collective-permute-start(bf16[4,4,96,576]{3,2,1,0:T(8,128)(2,1)} %get-tuple-element.155), channel_id=1, source_target_pairs={{0,4},{4,0},{8,12},{12,8},{16,20},{20,16},{24,28},{28,24},{1,5},{5... | collective-permute-start | bytes 5308424 | tf_op jit(solution)/shard_map/ppermute | solution.py:327
  282.7 30.6 %collective-permute-start.41 = (bf16[2,96,1792]{2,1,0:T(8,128)(2,1)S(1)}, bf16[2,96,1792]{2,1,0:T(8,128)(2,1)S(1)}, u32[]{:S(2)}, u32[]{:S(2)}) collective-permute-start(bf16[2,96,1792]{2,1,0:T(8,128)(2,1)S(1)} %fusion.5), channel_id=1, source_target_pairs={{0,8},{4,12},{8,0},{12,4},{16,24},{20,28},{24,16},{28,20},{1,9},{5... | collective-permute-start | bytes 2064392 | tf_op jit(solution)/shard_map/ppermute | solution.py:327
  283.9 29.5 %collective-permute-start.42 = (bf16[2,96,1792]{2,1,0:T(8,128)(2,1)S(1)}, bf16[2,96,1792]{2,1,0:T(8,128)(2,1)S(1)}, u32[]{:S(2)}, u32[]{:S(2)}) collective-permute-start(bf16[2,96,1792]{2,1,0:T(8,128)(2,1)S(1)} %fusion.6), channel_id=1, source_target_pairs={{0,16},{4,20},{8,24},{12,28},{16,0},{20,4},{24,8},{28,12},{1,17},{... | collective-permute-start | bytes 2064392 | tf_op jit(solution)/shard_map/ppermute | solution.py:327
  285.3 28.1 %collective-permute-start.43 = (bf16[2,2,96,576]{3,2,1,0:T(8,128)(2,1)S(1)}, bf16[2,2,96,576]{3,2,1,0:T(8,128)(2,1)S(1)}, u32[]{:S(2)}, u32[]{:S(2)}) collective-permute-start(bf16[2,2,96,576]{3,2,1,0:T(8,128)(2,1)S(1)} %slice_bitcast_fusion.12), channel_id=1, source_target_pairs={{0,16},{4,20},{8,24},{12,28},{16,0},{20,4},{24,8},{28,12},{1,17},{... | collective-permute-start | bytes 1327112 | tf_op jit(solution)/shard_map/ppermute | solution.py:327
  286.8 26.6 %collective-permute-start.44 = (bf16[2,2,96,576]{3,2,1,0:T(8,128)(2,1)S(1)}, bf16[2,2,96,576]{3,2,1,0:T(8,128)(2,1)S(1)}, u32[]{:S(2)}, u32[]{:S(2)}) collective-permute-start(bf16[2,2,96,576]{3,2,1,0:T(8,128)(2,1)S(1)} %slice_bitcast_fusion.11), channel_id=1, source_target_pairs={{0,8},{4,12},{8,0},{12,4},{16,24},{20,28},{24,16},{28,20},{1,9},{5... | collective-permute-start | bytes 1327112 | tf_op jit(solution)/shard_map/ppermute | solution.py:327
  288.1 9.5 %collective-permute-start.53 = (f32[16,192]{1,0:T(8,128)S(1)}, f32[16,192]{1,0:T(8,128)S(1)}, u32[]{:S(2)}, u32[]{:S(2)}) collective-permute-start(f32[16,192]{1,0:T(8,128)S(1)} %copy-done.57), channel_id=1, source_target_pairs={{0,1},{1,0},{2,3},{3,2},{4,5},{5,4},{6,7},{7,6},{8,9},{9,8},{10,11... | collective-permute-start | bytes 36872 | tf_op jit(solution)/shard_map/ppermute | solution.py:327
  297.6 4.6 %collective-permute-start.54 = (f32[16,192]{1,0:T(8,128)S(1)}, f32[16,192]{1,0:T(8,128)S(1)}, u32[]{:S(2)}, u32[]{:S(2)}) collective-permute-start(f32[16,192]{1,0:T(8,128)S(1)} %copy-done.56), channel_id=1, source_target_pairs={{0,2},{1,3},{2,0},{3,1},{4,6},{5,7},{6,4},{7,5},{8,10},{9,11},{10,... | collective-permute-start | bytes 36872 | tf_op jit(solution)/shard_map/ppermute | solution.py:327
  302.2 5.5 %collective-permute-start.55 = (f32[16,192]{1,0:T(8,128)S(1)}, f32[16,192]{1,0:T(8,128)S(1)}, u32[]{:S(2)}, u32[]{:S(2)}) collective-permute-start(f32[16,192]{1,0:T(8,128)S(1)} %copy-done.55), channel_id=1, source_target_pairs={{0,3},{1,2},{2,1},{3,0},{4,7},{5,6},{6,5},{7,4},{8,11},{9,10},{10,... | collective-permute-start | bytes 36872 | tf_op jit(solution)/shard_map/ppermute | solution.py:327
  307.8 1.2 collective-permute-start.56
  309.0 3.7 %collective-permute-start.57 = (f32[16,192]{1,0:T(8,128)S(1)}, f32[16,192]{1,0:T(8,128)S(1)}, u32[]{:S(2)}, u32[]{:S(2)}) collective-permute-start(f32[16,192]{1,0:T(8,128)S(1)} %add.182), channel_id=1, source_target_pairs={{0,8},{4,12},{8,0},{12,4},{16,24},{20,28},{24,16},{28,20},{1,9},{5... | collective-permute-start | bytes 36872 | tf_op jit(solution)/shard_map/ppermute | solution.py:327
  312.8 13.8 %collective-permute-start.58 = (f32[16,192]{1,0:T(8,128)S(1)}, f32[16,192]{1,0:T(8,128)S(1)}, u32[]{:S(2)}, u32[]{:S(2)}) collective-permute-start(f32[16,192]{1,0:T(8,128)S(1)} %add.183), channel_id=1, source_target_pairs={{0,16},{4,20},{8,24},{12,28},{16,0},{20,4},{24,8},{28,12},{1,17},{... | collective-permute-start | bytes 36872 | tf_op jit(solution)/shard_map/ppermute | solution.py:327
  313.8 44.6 %copy-start.27 = (f32[12,192]{1,0:T(8,128)S(1)}, f32[12,192]{1,0:T(8,128)}, u32[]{:S(2)}) copy-start(f32[12,192]{1,0:T(8,128)} %param.23) | copy-start | bytes 27652
  313.9 49.4 %copy-start.5 = (f32[96,576]{1,0:T(8,128)S(1)}, f32[96,576]{1,0:T(8,128)}, u32[]{:S(2)}) copy-start(f32[96,576]{1,0:T(8,128)} %param.19) | copy-start | bytes 663556
  313.9 49.4 %copy-start.21 = (f32[96,576]{1,0:T(8,128)S(1)}, f32[96,576]{1,0:T(8,128)}, u32[]{:S(2)}) copy-start(f32[96,576]{1,0:T(8,128)} %param.25) | copy-start | bytes 663556
  313.9 49.4 %copy-start.22 = (f32[96,576]{1,0:T(8,128)S(1)}, f32[96,576]{1,0:T(8,128)}, u32[]{:S(2)}) copy-start(f32[96,576]{1,0:T(8,128)} %param.24) | copy-start | bytes 663556
  314.0 7.3 %collective-permute-start.47 = (bf16[2,96,576]{2,1,0:T(8,128)(2,1)S(1)}, bf16[2,96,576]{2,1,0:T(8,128)(2,1)S(1)}, u32[]{:S(2)}, u32[]{:S(2)}) collective-permute-start(bf16[2,96,576]{2,1,0:T(8,128)(2,1)S(1)} %fusion.17), channel_id=1, source_target_pairs={{0,16},{4,20},{8,24},{12,28},{16,0},{20,4},{24,8},{28,12},{1,17},{... | collective-permute-start | bytes 663560 | tf_op jit(solution)/shard_map/ppermute | solution.py:327
  315.5 7.8 %collective-permute-start.45 = (bf16[2,96,576]{2,1,0:T(8,128)(2,1)S(1)}, bf16[2,96,576]{2,1,0:T(8,128)(2,1)S(1)}, u32[]{:S(2)}, u32[]{:S(2)}) collective-permute-start(bf16[2,96,576]{2,1,0:T(8,128)(2,1)S(1)} %fusion.16), channel_id=1, source_target_pairs={{0,8},{4,12},{8,0},{12,4},{16,24},{20,28},{24,16},{28,20},{1,9},{5... | collective-permute-start | bytes 663560 | tf_op jit(solution)/shard_map/ppermute | solution.py:327
  316.3 48.1 %collective-permute-start.50 = (bf16[96,1792]{1,0:T(8,128)(2,1)S(1)}, bf16[96,1792]{1,0:T(8,128)(2,1)S(1)}, u32[]{:S(2)}, u32[]{:S(2)}) collective-permute-start(bf16[96,1792]{1,0:T(8,128)(2,1)S(1)} %fusion.12), channel_id=1, source_target_pairs={{0,1},{1,0},{2,3},{3,2},{4,5},{5,4},{6,7},{7,6},{8,9},{9,8},{10,11... | collective-permute-start | bytes 1032200 | tf_op jit(solution)/shard_map/ppermute | solution.py:327
  320.2 44.1 %collective-permute-start.51 = (bf16[96,1792]{1,0:T(8,128)(2,1)S(1)}, bf16[96,1792]{1,0:T(8,128)(2,1)S(1)}, u32[]{:S(2)}, u32[]{:S(2)}) collective-permute-start(bf16[96,1792]{1,0:T(8,128)(2,1)S(1)} %get-tuple-element.190), channel_id=1, source_target_pairs={{0,2},{1,3},{2,0},{3,1},{4,6},{5,7},{6,4},{7,5},{8,10},{9,11},{10,... | collective-permute-start | bytes 1032200 | tf_op jit(solution)/shard_map/ppermute | solution.py:327
  321.3 43.1 %collective-permute-start.52 = (bf16[96,1792]{1,0:T(8,128)(2,1)S(1)}, bf16[96,1792]{1,0:T(8,128)(2,1)S(1)}, u32[]{:S(2)}, u32[]{:S(2)}) collective-permute-start(bf16[96,1792]{1,0:T(8,128)(2,1)S(1)} %get-tuple-element.191), channel_id=1, source_target_pairs={{0,3},{1,2},{2,1},{3,0},{4,7},{5,6},{6,5},{7,4},{8,11},{9,10},{10,... | collective-permute-start | bytes 1032200 | tf_op jit(solution)/shard_map/ppermute | solution.py:327
  323.3 35.1 %collective-permute-start.48 = (bf16[96,576]{1,0:T(8,128)(2,1)S(1)}, bf16[96,576]{1,0:T(8,128)(2,1)S(1)}, u32[]{:S(2)}, u32[]{:S(2)}) collective-permute-start(bf16[96,576]{1,0:T(8,128)(2,1)S(1)} %get-tuple-element.196), channel_id=1, source_target_pairs={{0,2},{1,3},{2,0},{3,1},{4,6},{5,7},{6,4},{7,5},{8,10},{9,11},{10,... | collective-permute-start | bytes 331784 | tf_op jit(solution)/shard_map/ppermute | solution.py:327
  326.6 32.5 %collective-permute-start.49 = (bf16[96,576]{1,0:T(8,128)(2,1)S(1)}, bf16[96,576]{1,0:T(8,128)(2,1)S(1)}, u32[]{:S(2)}, u32[]{:S(2)}) collective-permute-start(bf16[96,576]{1,0:T(8,128)(2,1)S(1)} %get-tuple-element.197), channel_id=1, source_target_pairs={{0,3},{1,2},{2,1},{3,0},{4,7},{5,6},{6,5},{7,4},{8,11},{9,10},{10,... | collective-permute-start | bytes 331784 | tf_op jit(solution)/shard_map/ppermute | solution.py:327
  358.4 4.9 %collective-permute-start.46 = (bf16[96,576]{1,0:T(8,128)(2,1)S(1)}, bf16[96,576]{1,0:T(8,128)(2,1)S(1)}, u32[]{:S(2)}, u32[]{:S(2)}) collective-permute-start(bf16[96,576]{1,0:T(8,128)(2,1)S(1)} %fusion.20), channel_id=1, source_target_pairs={{0,1},{1,0},{2,3},{3,2},{4,5},{5,4},{6,7},{7,6},{8,9},{9,8},{10,11... | collective-permute-start | bytes 331784 | tf_op jit(solution)/shard_map/ppermute | solution.py:327
  (53 other events, 711.6 us)

commit v3 on v2

--- a/solution.py
+++ b/solution.py
@@ -376,20 +376,13 @@
     return held + [swap(part, "batch", CORE) for part in held]
 
 
-def scatter_first(mine, came):
-    total = mine.astype(WIDE) + came.astype(WIDE)
-    total = total.reshape((2, 2) + total.shape[1:])
-    one, two = total[:, :, 0:2], total[:, :, 2:4]
-    return (one[0], two[:, 0]), (one[1].astype(LOW), two[:, 1].astype(LOW))
-
-
 def swap_pair(pair, first, second):
     return swap(pair[0], "batch", first), swap(pair[1], "batch", second)
 
 
 def scatter_second(kept, back):
-    one = kept[0] + back[0].astype(WIDE)
-    two = kept[1] + back[1].astype(WIDE)
+    one = kept[0].astype(WIDE) + back[0].astype(WIDE)
+    two = kept[1].astype(WIDE) + back[1].astype(WIDE)
     return (one[0], two[0]), (one[1].astype(LOW), two[1].astype(LOW))
 
 
@@ -444,22 +437,37 @@
     return started
 
 
-def store_grad(meta, place, mine, theirs, sems):
+def store_grad(held, targets, sems):
+    one_kept, one_sent, two_kept, two_sent = targets
     copies = []
-    for batch in range(BATCH):
-        for ctx in range(CTX):
-            target = theirs if batch % 2 else mine
-            ranges = place(meta[0] ^ batch, meta[1] ^ ctx)
-            for kind, (lanes, source) in enumerate(ranges):
-                copies.append(
-                    pltpu.make_async_copy(
-                        source,
-                        target.at[batch // 2, ctx, :, lanes],
-                        sems.at[kind, batch * CTX + ctx],
+    for y in range(2):
+        for x in range(2):
+            for ctx in range(CTX):
+                if ctx < 2:
+                    target = (one_sent if y else one_kept).at[x, ctx]
+                else:
+                    target = (two_sent if x else two_kept).at[y, ctx - 2]
+                for kind, (lanes, source) in enumerate(held(2 * y + x, ctx)):
+                    number = (2 * y + x) * CTX + ctx
+                    copies.append(
+                        pltpu.make_async_copy(source, target.at[:, lanes], sems.at[kind, number])
                     )
-                )
-                copies[-1].start()
+                    copies[-1].start()
     wait_all(copies)
+
+
+def half_rows(meta, pair, held):
+    for index, value in enumerate(pair):
+        held[index] = turned(value)
+    parts = []
+    for index in range(2):
+        rows = [held[index, rows_of(meta[0] ^ (2 * part), ROWS), :] for part in range(BATCH // 2)]
+        parts.append(jnp.concatenate(rows, axis=0))
+    return parts
+
+
+def over_both(left, right):
+    return mm(left[0], right[0]) + mm(left[1], right[1])
 
 
 def wait_all(copies):
@@ -599,11 +607,11 @@
     write_sequence(meta, results, (dq, dk, dv))
 
 
-def middle_kernel(meta, x_ref, dy_ref, *refs):
+def middle_kernel(meta, x_ref, dy_ref, h_one_ref, *refs):
     vectors, pieces, parts, refs = refs[:4], refs[4:8], refs[8:16], refs[16:]
-    (out_ref, att_ref, h_ref, act_ref, dpre_ref, datt_ref, dmid_ref), refs = refs[:7], refs[7:]
+    (out_ref, pack_ref, mine, theirs, dmid_ref), refs = refs[:5], refs[5:]
     results, (rows_ref, dbias_ref), refs = refs[:4], refs[4:6], refs[6:]
-    out_parts, held_out, held_fc, held_proj, units, total, back, chunks, bias, sems = refs
+    out_parts, held_out, held_fc, held_proj, units, total, back, chunks, bias, acts, sems = refs
     place = functools.partial(mlp_place, out_parts, held_fc, held_proj)
     copies = load_weight(meta, parts, place, sems)
     vec = read_vectors(meta, vectors, chunks)
@@ -612,14 +620,16 @@
     for ctx, piece in enumerate(pieces):
         units[meta[1] ^ ctx] = piece[...]
     att = jnp.concatenate([units[index] for index in range(CTX)], axis=1)
-    att_ref[...] = att
+    pack_ref[CTX + 1] = att
+    pack_ref[CTX + 3] = dy_ref[...]
+    pack_ref[CTX + 4] = h_one_ref[...]
     wait_all(copies[0])
     for chunk in range(CTX):
         held_out[:, chunk * GROUP : (chunk + 1) * GROUP] = out_parts[chunk, :, :GROUP]
     mid = x_ref[...].astype(WIDE) + mm(att, held_out[...]) + vec[6:7]
     centred, inverse = moments(mid)
     normed = centred * inverse
-    h_ref[...] = (normed * vec[2:3] + vec[3:4]).astype(LOW)
+    pack_ref[CTX] = (normed * vec[2:3] + vec[3:4]).astype(LOW)
     total[...] = mid + vec[7:8]
     back[...] = jnp.zeros_like(back)
     for group in copies[1:]:
@@ -627,33 +637,38 @@
     side = FF_SIDE
 
     def chunk_step(chunk, carry):
-        pre = mm(h_ref[...], held_fc[chunk]) + bias[chunk]
+        pre = mm(pack_ref[CTX], held_fc[chunk]) + bias[chunk]
         square = pre * pre
         tanh = jnp.tanh(0.7978845608028654 * (pre + 0.044715 * square * pre))
         act = (0.5 * pre * (1.0 + tanh)).astype(LOW)
         slope = 0.5 * (1.0 + tanh) + 0.5 * pre * (1.0 - tanh * tanh) * (
             0.7978845608028654 * (1.0 + 3.0 * 0.044715 * square)
         )
-        act_ref[chunk] = act
         grads = []
         for half in range(2):
             weight = held_proj[2 * chunk + half]
-            total[...] += mt(act[:, half * side : (half + 1) * side], weight)
+            part = act[:, half * side : (half + 1) * side]
+            acts[2 * chunk + half] = part
+            total[...] += mt(part, weight)
             grads.append(mm(dy_ref[...], weight))
         dpre = (jnp.concatenate(grads, axis=1) * slope).astype(LOW)
-        dpre_ref[chunk] = dpre
+        pack_ref[chunk] = dpre
         dbias_ref[chunk] = jnp.sum(dpre.astype(WIDE), axis=0, keepdims=True)
         back[...] += mt(dpre, held_fc[chunk])
         return carry
 
     lax.fori_loop(0, CTX, chunk_step, 0)
     out_ref[...] = total[...].astype(LOW)
+    core = meta[0] & 1
+    for chunk in range(CTX):
+        mine[chunk] = acts[2 * chunk + core]
+        theirs[chunk] = acts[2 * chunk + 1 - core]
     grad = back[...]
     dy = dy_ref[...].astype(WIDE)
     dmid = dy + norm_back(grad, normed, inverse, vec[2:3])
     dmid_ref[...] = dmid
     datt = dmid.astype(LOW)
-    datt_ref[...] = datt
+    pack_ref[CTX + 2] = datt
     rows_ref[0:1] = jnp.sum(grad * normed, axis=0, keepdims=True)
     rows_ref[1:2] = jnp.sum(grad, axis=0, keepdims=True)
     rows_ref[2:3] = jnp.sum(datt.astype(WIDE), axis=0, keepdims=True)
@@ -666,36 +681,60 @@
         target[...] = units[meta[1] ^ ctx]
 
 
-def mlp_grad_kernel(meta, dy_ref, act_ref, h_ref, dpre_ref, att_ref, datt_ref, *refs):
-    mine, theirs, held_out, held_fc, held_proj, sems = refs
-    dy, h_two, att = turned(dy_ref[...]), turned(h_ref[...]), turned(att_ref[...])
+def mlp_grad_kernel(meta, *refs):
+    acts, packs, targets = refs[:2], refs[2:4], refs[4:8]
+    held_out, held_fc, held_proj, turn, sems = refs[8:]
+    dy = [turned(pack[CTX + 3]) for pack in packs]
     for chunk in range(CTX):
-        proj = mm(dy, act_ref[chunk]).astype(LOW)
-        for half in range(2):
-            held_proj[2 * chunk + half] = proj[:, half * FF_SIDE : (half + 1) * FF_SIDE]
-        held_fc[chunk] = mm(h_two, dpre_ref[chunk]).astype(LOW)
-    grad = mm(att, datt_ref[...]).astype(LOW)
+        held_proj[chunk] = over_both(dy, [act[chunk] for act in acts]).astype(LOW)
+    left = half_rows(meta, [pack[CTX] for pack in packs], turn)
+    for chunk in range(CTX):
+        held_fc[chunk] = over_both(left, [pack[chunk] for pack in packs]).astype(LOW)
+    left = half_rows(meta, [pack[CTX + 1] for pack in packs], turn)
+    grad = over_both(left, [pack[CTX + 2] for pack in packs]).astype(LOW)
     for chunk in range(CTX):
         held_out[chunk, :, :GROUP] = grad[:, chunk * GROUP : (chunk + 1) * GROUP]
-        held_out[chunk, :, GROUP:] = jnp.zeros((WIDTH, TILE - GROUP), LOW)
-    place = functools.partial(mlp_place, held_out, held_fc, held_proj)
-    store_grad(meta, place, mine, theirs, sems)
-
-
-def qkv_grad_kernel(meta, h_ref, *refs):
-    pieces, (mine, theirs, mixed_ref, dbias_ref, held, units, sems) = refs[:4], refs[4:]
-    for ctx, piece in enumerate(pieces):
-        for part in range(3):
-            units[CTX * part + (meta[1] ^ ctx)] = piece[:, part * GROUP : (part + 1) * GROUP]
-    left = turned(h_ref[...])
+        held_out[chunk, :, GROUP:] = jnp.zeros((WIDTH // 2, TILE - GROUP), LOW)
+
+    def place(part, ctx):
+        ctx = meta[1] ^ ctx
+        chunk = (meta[0] ^ (2 * part)) // 2
+        rows = pl.ds(part * ROWS, ROWS)
+        return [
+            (pl.ds(WIDTH + 2 * FF_SIDE, TILE), held_out.at[ctx, rows, :]),
+            (pl.ds(0, WIDTH), held_fc.at[ctx, rows, :]),
+            (pl.ds(WIDTH, FF_SIDE), held_proj.at[chunk, rows_of(2 * ctx, ROWS), :]),
+            (pl.ds(WIDTH + FF_SIDE, FF_SIDE), held_proj.at[chunk, rows_of(2 * ctx + 1, ROWS), :]),
+        ]
+
+    store_grad(place, targets, sems)
+
+
+def qkv_grad_kernel(meta, *refs):
+    pack, pieces, targets = refs[:2], (refs[2:6], refs[6:10]), refs[10:14]
+    mixed_ref, dbias_ref, held, units, turn, sems = refs[14:]
+    for core in range(2):
+        for ctx, piece in enumerate(pieces[core]):
+            for part in range(3):
+                units[core, CTX * part + (meta[1] ^ ctx)] = piece[
+                    :, part * GROUP : (part + 1) * GROUP
+                ]
+    left = half_rows(meta, [pack[0][...], pack[1][...]], turn)
     for chunk in range(CTX):
-        mixed = jnp.concatenate([units[3 * chunk + part] for part in range(3)], axis=1)
-        mixed_ref[chunk] = mixed
-        bias = jnp.sum(mixed.astype(WIDE), axis=0, keepdims=True)
+        mixed = [
+            jnp.concatenate([units[core, 3 * chunk + part] for part in range(3)], axis=1)
+            for core in range(2)
+        ]
+        mixed_ref[chunk] = mixed[0]
+        bias = jnp.sum(mixed[0].astype(WIDE), axis=0, keepdims=True)
         for part in range(3):
             dbias_ref[3 * chunk + part] = bias[:, part * GROUP : (part + 1) * GROUP]
-        held[chunk] = mm(left, mixed).astype(LOW)
-    store_grad(meta, functools.partial(qkv_place, held), mine, theirs, sems)
+        held[chunk] = over_both(left, mixed).astype(LOW)
+
+    def place(part, ctx):
+        return [(pl.ds(0, 3 * GROUP), held.at[meta[1] ^ ctx, pl.ds(part * ROWS, ROWS), :])]
+
+    store_grad(place, targets, sems)
 
 
 def input_grad_kernel(meta, x_ref, dmid_ref, mixed_ref, rows_ref, dfc_ref, dqkv_ref, *refs):
@@ -779,11 +818,6 @@
     qkv_sems = pltpu.SemaphoreType.DMA((1, BATCH * CTX))
     mlp_sems = pltpu.SemaphoreType.DMA((4, BATCH * CTX))
     qkv_held = pltpu.VMEM((CTX, WIDTH, 3 * GROUP), LOW)
-    mlp_held = [
-        pltpu.VMEM((CTX, WIDTH, TILE), LOW),
-        pltpu.VMEM((CTX, WIDTH, WIDTH), LOW),
-        pltpu.VMEM((BATCH, WIDTH, FF_SIDE), LOW),
-    ]
     vec_held = pltpu.VMEM((CTX, 16, GROUP), WIDE)
 
     piece_one = w_qkv.astype(LOW)
@@ -804,9 +838,7 @@
     piece_two, _ = tie((piece_two, parts_one))
     parts_two = exchange(piece_two)
     parts_one = gather_second(*gather_first(piece_one, parts_one))
-    parts_two, _ = tie((parts_two, parts_one))
     parts_one = gather_last(parts_one)
-    kept_two, came_two = gather_first(piece_two, parts_two)
 
     packed = shape_of(LOW, TOKENS, 3 * GROUP)
     single = shape_of(LOW, TOKENS, GROUP)
@@ -822,6 +854,8 @@
         [qkv_held, pltpu.VMEM((CTX, TOKENS, 3 * GROUP), LOW), vec_held, qkv_sems],
         2 * TOKENS * 3 * square,
     )
+    parts_two, _ = tie((parts_two, own))
+    kept_two, came_two = gather_first(piece_two, parts_two)
     qkv_pieces = [own] + [swap(part, "ctx", bit) for bit, part in zip((1, 2, 3), sent)]
 
     qkv_pieces, came_two = tie((qkv_pieces, came_two))
@@ -838,47 +872,59 @@
         [sequence_low] * 3 + [sequence_wide],
         2 * SPAN * SPAN * GROUP * 2,
     )
-    parts_two, _ = tie((parts_two, own))
-    parts_two = gather_last(parts_two)
     att_pieces = [own] + [swap(part, "ctx", bit) for bit, part in zip((1, 2, 3), sent)]
-
-    out, att, h_two, act, dpre, datt, dmid, own, *sent = call(
+    last_two, _ = tie((parts_two[2:], att_pieces[1]))
+    parts_two = gather_last(parts_two[:2] + last_two)
+
+    pack_shape = shape_of(LOW, CTX + 5, TOKENS, WIDTH)
+    act_shape = shape_of(LOW, BATCH // 2, TOKENS, FF_SIDE)
+    out, pack, act_mine, act_theirs, dmid, own, *sent = call(
         middle_kernel,
-        (meta, inputs, grad_low, *vec_parts, *att_pieces, *parts_two),
-        "s" + "v" * 10 + "a" * 8,
-        [tokens_low] * 3
-        + [hidden_low] * 2
-        + [tokens_low, shape_of(WIDE, TOKENS, WIDTH)]
+        (meta, inputs, grad_low, h_one, *vec_parts, *att_pieces, *parts_two),
+        "s" + "v" * 11 + "a" * 8,
+        [tokens_low, pack_shape, act_shape, act_shape, shape_of(WIDE, TOKENS, WIDTH)]
         + [single] * 4
         + [shape_of(WIDE, 8, WIDTH), shape_of(WIDE, CTX, 1, WIDTH)],
-        "v" * 13,
-        mlp_held[:1]
-        + [pltpu.VMEM((WIDTH, WIDTH), LOW)]
-        + mlp_held[1:]
-        + [
+        "v" * 11,
+        [
+            pltpu.VMEM((CTX, WIDTH, TILE), LOW),
+            pltpu.VMEM((WIDTH, WIDTH), LOW),
+            pltpu.VMEM((CTX, WIDTH, WIDTH), LOW),
+            pltpu.VMEM((BATCH, WIDTH, FF_SIDE), LOW),
             pltpu.VMEM((CTX, TOKENS, GROUP), LOW),
             pltpu.VMEM((TOKENS, WIDTH), WIDE),
             pltpu.VMEM((TOKENS, WIDTH), WIDE),
             vec_held,
             pltpu.VMEM((CTX, 1, WIDTH), WIDE),
+            pltpu.VMEM((BATCH, TOKENS, FF_SIDE), LOW),
             mlp_sems,
         ],
         2 * TOKENS * 18 * square,
     )
     sent, (rows_two, dbias_fc) = sent[:3], sent[3:]
     grad_pieces = [own] + [swap(part, "ctx", bit) for bit, part in zip((1, 2, 3), sent)]
-
-    mlp_mine, mlp_theirs = call(
+    act_came, pack_came = swap(act_theirs, "batch", CORE), swap(pack, "batch", CORE)
+
+    half_sems = BATCH * CTX // 2
+    turn_held = pltpu.VMEM((2, WIDTH, TOKENS), LOW)
+    mlp_parts = call(
         mlp_grad_kernel,
-        (meta, grad_low, act, h_two, dpre, att, datt),
-        "s" + "v" * 6,
-        [shape_of(LOW, BATCH // 2, CTX, ROWS, MLP)] * 2,
-        "aa",
-        mlp_held + [mlp_sems],
+        (meta, act_mine, act_came, pack, pack_came),
+        "s" + "v" * 4,
+        [shape_of(LOW, 2, 2, ROWS, MLP)] * 4,
+        "aaaa",
+        [
+            pltpu.VMEM((CTX, WIDTH // 2, TILE), LOW),
+            pltpu.VMEM((CTX, WIDTH // 2, WIDTH), LOW),
+            pltpu.VMEM((BATCH // 2, WIDTH, FF_SIDE), LOW),
+            turn_held,
+            pltpu.SemaphoreType.DMA((4, half_sems)),
+        ],
         2 * TOKENS * 9 * square,
     )
-    mlp_mine, mlp_theirs, grad_pieces = tie((mlp_mine, mlp_theirs, grad_pieces))
-    mlp_came = swap(mlp_theirs, "batch", CORE)
+    mlp_parts, grad_pieces = tie((mlp_parts, grad_pieces))
+    mlp_kept = mlp_parts[0], mlp_parts[2]
+    mlp_back = swap_pair((mlp_parts[1], mlp_parts[3]), YBIT, XBIT)
     own, *sent = call(
         attend_back_kernel,
         (meta, *qkv_pieces, *grad_pieces),
@@ -888,23 +934,29 @@
         [sequence_low] * 4 + [sequence_wide] * 3,
         2 * SPAN * SPAN * GROUP * 5,
     )
-    mlp_came, own, sent = tie((mlp_came, own, sent))
     mixed_pieces = [own] + [swap(part, "ctx", bit) for bit, part in zip((1, 2, 3), sent)]
-    mlp_kept, mlp_sent = scatter_first(mlp_mine, mlp_came)
-    mlp_kept, mlp_sent, mixed_pieces = tie((mlp_kept, mlp_sent, mixed_pieces))
-    mlp_back = swap_pair(mlp_sent, YBIT, XBIT)
-
-    qkv_mine, qkv_theirs, mixed, dbias_qkv = call(
+    mixed_came = [swap(part, "batch", CORE) for part in mixed_pieces]
+    mlp_back, mixed_pieces, mixed_came = tie((mlp_back, mixed_pieces, mixed_came))
+    mlp_kept, mlp_sent = scatter_second(mlp_kept, mlp_back)
+    mlp_back = swap_pair(mlp_sent, XBIT, YBIT)
+
+    *qkv_parts, mixed, dbias_qkv = call(
         qkv_grad_kernel,
-        (meta, h_one, *mixed_pieces),
-        "s" + "v" * 5,
-        [shape_of(LOW, BATCH // 2, CTX, ROWS, 3 * GROUP)] * 2
+        (meta, pack[CTX + 4], pack_came[CTX + 4], *mixed_pieces, *mixed_came),
+        "s" + "v" * 10,
+        [shape_of(LOW, 2, 2, ROWS, 3 * GROUP)] * 4
         + [shape_of(LOW, CTX, TOKENS, 3 * GROUP), shape_of(WIDE, 3 * CTX, 1, GROUP)],
-        "aavv",
-        [qkv_held, pltpu.VMEM((3 * CTX, TOKENS, GROUP), LOW), qkv_sems],
+        "aaaavv",
+        [
+            pltpu.VMEM((CTX, WIDTH // 2, 3 * GROUP), LOW),
+            pltpu.VMEM((2, 3 * CTX, TOKENS, GROUP), LOW),
+            turn_held,
+            pltpu.SemaphoreType.DMA((1, half_sems)),
+        ],
         2 * TOKENS * 3 * square,
     )
-    qkv_came = swap(qkv_theirs, "batch", CORE)
+    qkv_kept = qkv_parts[0], qkv_parts[2]
+    qkv_back = swap_pair((qkv_parts[1], qkv_parts[3]), YBIT, XBIT)
     grad_input, own, *sent = call(
         input_grad_kernel,
         (meta, inputs, dmid, mixed, rows_two, dbias_fc, dbias_qkv, *vec_parts, *parts_one),
@@ -914,12 +966,7 @@
         [qkv_held, vec_held, pltpu.VMEM((16, WIDTH), WIDE), vec_held, qkv_sems],
         2 * TOKENS * 3 * square,
     )
-    mlp_back, own = tie((mlp_back, own))
-    mlp_kept, mlp_sent = scatter_second(mlp_kept, mlp_back)
-    mlp_back = swap_pair(mlp_sent, XBIT, YBIT)
-    qkv_kept, qkv_sent = scatter_first(qkv_mine, qkv_came)
-    qkv_back = swap_pair(qkv_sent, YBIT, XBIT)
-    mlp_back, qkv_back = tie((mlp_back, qkv_back))
+    mlp_back, own, sent = tie((mlp_back, own, sent))
     mlp_kept, mlp_sent = scatter_third(mlp_kept, mlp_back)
     qkv_kept, qkv_sent = scatter_second(qkv_kept, qkv_back)
     qkv_back = swap_pair(qkv_sent, XBIT, YBIT)

time: 368 us -> 347 us (0.943)
  waiting for transfers between devices: 164 us -> 154 us
  other arithmetic: 22.7 us -> 12.8 us
    ppermute x59 -> x63, waiting for transfers between devices: 164 us -> 154 us  [swap(): return lax.ppermute(value, axis, [(i, i ^ bit) for i in range(size)])]
    add x5 -> x4, other arithmetic: 8.31 us -> 2.94 us  [the longest x2 1.54 us: scatter_second(): one = kept[0].astype(WIDE) + back[0].astype(WIDE)]
    another operation x8, other arithmetic: 5.79 us -> 1.66 us  [gather_second(): one, two = (jnp.stack([kept[0], came[0]]), jnp.stack([kept[1], came[1]]))]
    ppermute x59 -> x63, starting transfers between devices: 91.7 us -> 88.3 us  [swap(): return lax.ppermute(value, axis, [(i, i ^ bit) for i in range(size)])]
  transfers between devices with their start and end apart: 59 -> 63, of which waited for: 26 -> 24; matrix products, arithmetic and copies ran while one was open for 4% -> 4% of each run, Pallas kernels for 16% -> 15%
where the time goes in v3:
time: 347 us; the launch traced here: 344 us
  waiting for transfers between devices  154 us (44%)
  starting transfers between devices  88.3 us (25%)
  Pallas kernels  75.8 us (22%)
  other arithmetic  12.8 us (4%)
  local copies, waits for them, and re-layouts  11.9 us (3%)
    ppermute x63, waiting for transfers between devices, swap(): return lax.ppermute(value, axis, [(i, i ^ bit) for i in range(size)])  154 us
    ppermute x63, starting transfers between devices, swap(): return lax.ppermute(value, axis, [(i, i ^ bit) for i in range(size)])  88.3 us
    pallas_call x7, Pallas kernels, call(): pl.pallas_call(kernel, out_shape=tuple(outputs), in_specs=[spec[kind] for...  75.8 us
  transfers between devices with their start and end apart: 63, of which 24 were waited for; matrix products, arithmetic and copies ran while one was open for 4% of the time, Pallas kernels for 15%

profile of v3, /device:TPU:0, one launch (start us, length us, event | category | flops | bytes accessed | tf_op | source)
XLA Modules:
  0.0 344.5 jit_solution(3263089071032451523)
XLA Ops:
  1.6 4.1 %collective-permute-start.5 = (bf16[96,576]{1,0:T(8,128)(2,1)S(1)}, bf16[96,576]{1,0:T(8,128)(2,1)S(1)}, u32[]{:S(2)}, u32[]{:S(2)}) collective-permute-start(bf16[96,576]{1,0:T(8,128)(2,1)S(1)} %convert_element_type.112), channel_id=1, source_target_pairs={{0,2},{1,3},{2,0},{3,1},{4,6},{5,7},{6,4},{7,5},{8,10},{9,11},{10,... | collective-permute-start | bytes 331784 | tf_op jit(solution)/shard_map/ppermute | solution.py:327
  5.7 1.3 collective-permute-start.6
  7.3 7.9 %collective-permute-done.5 = bf16[96,576]{1,0:T(8,128)(2,1)S(1)} collective-permute-done((bf16[96,576]{1,0:T(8,128)(2,1)S(1)}, bf16[96,576]{1,0:T(8,128)(2,1)S(1)}, u32[]{:S(2)}, u32[]{:S(2)}) %collective-permute-start.5) | collective-permute-done | bytes 110624 | tf_op jit(solution)/shard_map/ppermute | solution.py:327
  15.2 1.9 collective-permute-start.7
  18.2 1.6 collective-permute-start.4
  19.8 1.7 collective-permute-done.7
  21.6 1.9 collective-permute-start.9
  23.5 3.6 %collective-permute-done.4 = bf16[2,96,576]{2,1,0:T(8,128)(2,1)S(1)} collective-permute-done((bf16[2,96,576]{2,1,0:T(8,128)(2,1)S(1)}, bf16[2,96,576]{2,1,0:T(8,128)(2,1)S(1)}, u32[]{:S(2)}, u32[]{:S(2)}) %collective-permute-start.4) | collective-permute-done | bytes 221216 | tf_op jit(solution)/shard_map/ppermute | solution.py:327
  27.3 2.0 collective-permute-start.2
  29.3 1.8 collective-permute-start.1
  31.1 1.7 collective-permute-done.2.refs_3_
  33.9 2.3 collective-permute-start
  39.1 3.7 %collective-permute-start.19 = (bf16[96,1792]{1,0:T(8,128)(2,1)S(1)}, bf16[96,1792]{1,0:T(8,128)(2,1)}, u32[]{:S(2)}, u32[]{:S(2)}) collective-permute-start(bf16[96,1792]{1,0:T(8,128)(2,1)S(1)} %concatenate.6), channel_id=1, source_target_pairs={{0,3},{1,2},{2,1},{3,0},{4,7},{5,6},{6,5},{7,4},{8,11},{9,10},{10,... | collective-permute-start | bytes 1032200 | tf_op jit(solution)/shard_map/ppermute | solution.py:327
  42.8 1.9 collective-permute-start.18
  46.0 6.2 %shard_map.296 = (bf16[256,768]{1,0:T(8,128)(2,1)}, bf16[256,576]{1,0:T(8,128)(2,1)}, bf16[256,576]{1,0:T(8,128)(2,1)}, bf16[256,576]{1,0:T(8,128)(2,1)}, bf16[256,576]{1,0:T(8,128)(2,1)}) custom-call(s32[2]{0:T(128)} %pad_add_fusion.meta, bf16[256,768]{1,0:T(8,128)(2,1)} %bitcast.99, bf16[16,192]{1,0:T(8,128)(2,1)} %copy-done.33, ...), custom_call_target="tpu_custom_call" | custom-call | flops 905969664 | bytes 5529608 | tf_op jit(solution)/shard_map/pallas_call | solution.py:780
  52.2 21.4 %collective-permute-done.18 = bf16[96,1792]{1,0:T(8,128)(2,1)S(1)} collective-permute-done((bf16[96,1792]{1,0:T(8,128)(2,1)S(1)}, bf16[96,1792]{1,0:T(8,128)(2,1)S(1)}, u32[]{:S(2)}, u32[]{:S(2)}) %collective-permute-start.18) | collective-permute-done | bytes 344096 | tf_op jit(solution)/shard_map/ppermute | solution.py:327
  73.7 1.6 collective-permute-start.20
  76.3 1.2 collective-permute-start.21
  77.7 3.4 collective-permute-start.15
  82.0 10.9 %collective-permute-done.14.refs_1_ = bf16[256,576]{1,0:T(8,128)(2,1)S(1)} collective-permute-done((bf16[256,576]{1,0:T(8,128)(2,1)S(1)}, bf16[256,576]{1,0:T(8,128)(2,1)S(1)}, u32[]{:S(2)}, u32[]{:S(2)}) %collective-permute-start.14) | collective-permute-done | bytes 294944 | tf_op jit(solution)/shard_map/ppermute | solution.py:327
  92.9 10.8 %collective-permute-done.15.refs_2_ = bf16[256,576]{1,0:T(8,128)(2,1)S(1)} collective-permute-done((bf16[256,576]{1,0:T(8,128)(2,1)S(1)}, bf16[256,576]{1,0:T(8,128)(2,1)S(1)}, u32[]{:S(2)}, u32[]{:S(2)}) %collective-permute-start.15) | collective-permute-done | bytes 294944 | tf_op jit(solution)/shard_map/ppermute | solution.py:327
  105.5 1.3 collective-permute-start.25
  106.8 12.2 %shard_map.297 = (bf16[256,192]{1,0:T(8,128)(2,1)}, bf16[256,192]{1,0:T(8,128)(2,1)}, bf16[256,192]{1,0:T(8,128)(2,1)}, bf16[256,192]{1,0:T(8,128)(2,1)}) custom-call(s32[2]{0:T(128)} %pad_add_fusion.meta, bf16[256,576]{1,0:T(8,128)(2,1)} %get-tuple-element.101.refs_0_, bf16[256,576]{1,0:T(8,128)(2,1)} %copy-done.49, bf16[256,576]{1,0:T(8,128)(2,1)} %copy-done.50, ...), custom_call_target="tpu_custom_call" | custom-call | flops 805306368 | bytes 1572872 | tf_op jit(solution)/shard_map/pallas_call | solution.py:780
  119.0 6.0 %collective-permute-start.22 = (bf16[256,192]{1,0:T(8,128)(2,1)}, bf16[256,192]{1,0:T(8,128)(2,1)S(1)}, u32[]{:S(2)}, u32[]{:S(2)}) collective-permute-start(bf16[256,192]{1,0:T(8,128)(2,1)} %get-tuple-element.106), channel_id=1, source_target_pairs={{0,1},{1,0},{2,3},{3,2},{4,5},{5,4},{6,7},{7,6},{8,9},{9,8},{10,11... | collective-permute-start | bytes 294920 | tf_op jit(solution)/shard_map/ppermute | solution.py:327
  125.5 2.6 collective-permute-done.22.refs_5_
  128.2 5.5 %collective-permute-done.26.refs_11_ = bf16[2,2,96,1792]{3,2,1,0:T(8,128)(2,1)S(1)} collective-permute-done((bf16[2,2,96,1792]{3,2,1,0:T(8,128)(2,1)S(1)}, bf16[2,2,96,1792]{3,2,1,0:T(8,128)(2,1)S(1)}, u32[]{:S(2)}, u32[]{:S(2)}) %collective-permute-start.26) | collective-permute-done | bytes 1376288 | tf_op jit(solution)/shard_map/ppermute | solution.py:327
  135.0 8.6 %collective-permute-start.23 = (bf16[256,192]{1,0:T(8,128)(2,1)}, bf16[256,192]{1,0:T(8,128)(2,1)S(1)}, u32[]{:S(2)}, u32[]{:S(2)}) collective-permute-start(bf16[256,192]{1,0:T(8,128)(2,1)} %get-tuple-element.107), channel_id=1, source_target_pairs={{0,2},{1,3},{2,0},{3,1},{4,6},{5,7},{6,4},{7,5},{8,10},{9,11},{10,... | collective-permute-start | bytes 294920 | tf_op jit(solution)/shard_map/ppermute | solution.py:327
  143.5 6.7 %collective-permute-done.23.refs_6_ = bf16[256,192]{1,0:T(8,128)(2,1)S(1)} collective-permute-done((bf16[256,192]{1,0:T(8,128)(2,1)}, bf16[256,192]{1,0:T(8,128)(2,1)S(1)}, u32[]{:S(2)}, u32[]{:S(2)}) %collective-permute-start.23) | collective-permute-done | bytes 98336 | tf_op jit(solution)/shard_map/ppermute | solution.py:327
  150.2 1.4 collective-permute-start.24
  151.6 5.6 %collective-permute-done.24.refs_7_ = bf16[256,192]{1,0:T(8,128)(2,1)S(1)} collective-permute-done((bf16[256,192]{1,0:T(8,128)(2,1)}, bf16[256,192]{1,0:T(8,128)(2,1)S(1)}, u32[]{:S(2)}, u32[]{:S(2)}) %collective-permute-start.24) | collective-permute-done | bytes 98336 | tf_op jit(solution)/shard_map/ppermute | solution.py:327
  158.4 1.3 copy-done.47
  159.7 18.0 %shard_map.298 = (bf16[256,768]{1,0:T(8,128)(2,1)}, bf16[9,256,768]{2,1,0:T(8,128)(2,1)}, bf16[4,256,384]{2,1,0:T(8,128)(2,1)}, bf16[4,256,384]{2,1,0:T(8,128)(2...) custom-call(s32[2]{0:T(128)} %pad_add_fusion.meta, ...), custom_call_target="tpu_custom_call" | custom-call | flops 5435817984 | bytes 19329032 | tf_op jit(solution)/shard_map/pallas_call | solution.py:780
  178.3 2.1 collective-permute-start.34
  180.3 2.3 collective-permute-start.35
  182.6 2.7 collective-permute-done.32.refs_1_
  187.4 10.1 %shard_map.299 = (bf16[2,2,96,1792]{3,2,1,0:T(8,128)(2,1)}, bf16[2,2,96,1792]{3,2,1,0:T(8,128)(2,1)}, bf16[2,2,96,1792]{3,2,1,0:T(8,128)(2,1)}, bf16[2,2,96,1792]{3,2,1,0:T(8,128)(2,1)}) custom-call(s32[2]{0:T(128)} %pad_add_fusion.meta, bf16[4,256,384]{2,1,0:T(8,128)(2,1)} %get-tuple-element.116.refs_0_, bf16[4,256,384]{2,1,0:T(8,128)(2,1)} %copy-done.48, ...), custom_call_target="tpu_custom_call" | custom-call | flops 2717908992 | bytes 14155784 | tf_op jit(solution)/shard_map/pallas_call | solution.py:780
  197.5 1.2 collective-permute-start.36
  198.8 1.5 collective-permute-start.37
  200.3 15.9 %shard_map.300 = (bf16[256,576]{1,0:T(8,128)(2,1)}, bf16[256,576]{1,0:T(8,128)(2,1)}, bf16[256,576]{1,0:T(8,128)(2,1)}, bf16[256,576]{1,0:T(8,128)(2,1)}) custom-call(s32[2]{0:T(128)} %pad_add_fusion.meta, bf16[256,576]{1,0:T(8,128)(2,1)} %get-tuple-element.101.refs_0_, bf16[256,576]{1,0:T(8,128)(2,1)} %copy-done.49, bf16[256,576]{1,0:T(8,128)(2,1)} %copy-done.50, ...), custom_call_target="tpu_custom_call" | custom-call | flops 2013265920 | bytes 2752520 | tf_op jit(solution)/shard_map/pallas_call | solution.py:780
  216.2 2.1 collective-permute-start.39
  218.3 2.3 collective-permute-start.40
  220.6 11.1 %collective-permute-done.38.refs_3_ = bf16[256,576]{1,0:T(8,128)(2,1)S(1)} collective-permute-done((bf16[256,576]{1,0:T(8,128)(2,1)}, bf16[256,576]{1,0:T(8,128)(2,1)S(1)}, u32[]{:S(2)}, u32[]{:S(2)}) %collective-permute-start.38) | collective-permute-done | bytes 294944 | tf_op jit(solution)/shard_map/ppermute | solution.py:327
  231.7 10.3 %collective-permute-done.39.refs_4_ = bf16[256,576]{1,0:T(8,128)(2,1)S(1)} collective-permute-done((bf16[256,576]{1,0:T(8,128)(2,1)}, bf16[256,576]{1,0:T(8,128)(2,1)S(1)}, u32[]{:S(2)}, u32[]{:S(2)}) %collective-permute-start.39) | collective-permute-done | bytes 294944 | tf_op jit(solution)/shard_map/ppermute | solution.py:327
  242.6 1.8 slice_bitcast_fusion.6.refs_0_
  244.4 1.8 slice_bitcast_fusion.5.refs_1_
  247.2 6.5 %shard_map.301 = (bf16[2,2,96,576]{3,2,1,0:T(8,128)(2,1)}, bf16[2,2,96,576]{3,2,1,0:T(8,128)(2,1)}, bf16[2,2,96,576]{3,2,1,0:T(8,128)(2,1)}, bf16[2,2,96,576]{3,...) custom-call(s32[2]{0:T(128)} %pad_add_fusion.meta, ...), custom_call_target="tpu_custom_call" | custom-call | flops 905969664 | bytes 6104072 | tf_op jit(solution)/shard_map/pallas_call | solution.py:780
  255.5 1.2 collective-permute-start.52
  257.1 1.6 collective-permute-start.53
  258.7 6.9 %shard_map.302 = (f32[256,768]{1,0:T(8,128)}, f32[16,192]{1,0:T(8,128)}, f32[16,192]{1,0:T(8,128)}, f32[16,192]{1,0:T(8,128)}, f32[16,192]{1,0:T(8,128)}) custom-call(s32[2]{0:T(128)} %pad_add_fusion.meta, bf16[256,768]{1,0:T(8,128)(2,1)} %bitcast.101, f32[256,768]{1,0:T(8,128)} %get-tuple-element.114.dmid_ref, ...), custom_call_target="tpu_custom_call" | custom-call | flops 905969664 | bytes 6804488 | tf_op jit(solution)/shard_map/pallas_call | solution.py:780
  265.6 2.6 collective-permute-done.45
  268.1 1.3 convert_add_fusion.3
  272.2 15.5 %collective-permute-done.46 = bf16[2,96,576]{2,1,0:T(8,128)(2,1)S(1)} collective-permute-done((bf16[2,96,576]{2,1,0:T(8,128)(2,1)S(1)}, bf16[2,96,576]{2,1,0:T(8,128)(2,1)S(1)}, u32[]{:S(2)}, u32[]{:S(2)}) %collective-permute-start.46) | collective-permute-done | bytes 221216 | tf_op jit(solution)/shard_map/ppermute | solution.py:327
  287.8 5.9 %collective-permute-start.47 = (bf16[96,576]{1,0:T(8,128)(2,1)S(1)}, bf16[96,576]{1,0:T(8,128)(2,1)S(1)}, u32[]{:S(2)}, u32[]{:S(2)}) collective-permute-start(bf16[96,576]{1,0:T(8,128)(2,1)S(1)} %fusion.18), channel_id=1, source_target_pairs={{0,1},{1,0},{2,3},{3,2},{4,5},{5,4},{6,7},{7,6},{8,9},{9,8},{10,11... | collective-permute-start | bytes 331784 | tf_op jit(solution)/shard_map/ppermute | solution.py:327
  294.2 2.1 collective-permute-start.57
  296.9 1.8 collective-permute-start.59
  298.9 2.1 collective-permute-start.51
  300.9 5.0 %collective-permute-done.58 = f32[16,192]{1,0:T(8,128)S(1)} collective-permute-done((f32[16,192]{1,0:T(8,128)S(1)}, f32[16,192]{1,0:T(8,128)S(1)}, u32[]{:S(2)}, u32[]{:S(2)}) %collective-permute-start.58) | collective-permute-done | bytes 12320 | tf_op jit(solution)/shard_map/ppermute | solution.py:327
  308.1 2.8 collective-permute-done.61
  311.0 1.5 collective-permute-start.62
  313.5 1.2 collective-permute-done.62
  314.7 1.3 collective-permute-start.55
  316.1 1.9 collective-permute-start.56
  319.7 6.7 %collective-permute-done.54 = bf16[96,1792]{1,0:T(8,128)(2,1)S(1)} collective-permute-done((bf16[96,1792]{1,0:T(8,128)(2,1)S(1)}, bf16[96,1792]{1,0:T(8,128)(2,1)S(1)}, u32[]{:S(2)}, u32[]{:S(2)}) %collective-permute-start.54) | collective-permute-done | bytes 344096 | tf_op jit(solution)/shard_map/ppermute | solution.py:327
  326.5 14.9 %collective-permute-done.55 = bf16[96,1792]{1,0:T(8,128)(2,1)S(1)} collective-permute-done((bf16[96,1792]{1,0:T(8,128)(2,1)S(1)}, bf16[96,1792]{1,0:T(8,128)(2,1)S(1)}, u32[]{:S(2)}, u32[]{:S(2)}) %collective-permute-start.55) | collective-permute-done | bytes 344096 | tf_op jit(solution)/shard_map/ppermute | solution.py:327
  (244 shorter events, 32.9 us)
Async XLA Ops:
  1.6 13.6 %collective-permute-start.5 = (bf16[96,576]{1,0:T(8,128)(2,1)S(1)}, bf16[96,576]{1,0:T(8,128)(2,1)S(1)}, u32[]{:S(2)}, u32[]{:S(2)}) collective-permute-start(bf16[96,576]{1,0:T(8,128)(2,1)S(1)} %convert_element_type.112), channel_id=1, source_target_pairs={{0,2},{1,3},{2,0},{3,1},{4,6},{5,7},{6,4},{7,5},{8,10},{9,11},{10,... | collective-permute-start | bytes 331784 | tf_op jit(solution)/shard_map/ppermute | solution.py:327
  5.7 9.5 %collective-permute-start.6 = (bf16[96,576]{1,0:T(8,128)(2,1)S(1)}, bf16[96,576]{1,0:T(8,128)(2,1)S(1)}, u32[]{:S(2)}, u32[]{:S(2)}) collective-permute-start(bf16[96,576]{1,0:T(8,128)(2,1)S(1)} %convert_element_type.112), channel_id=1, source_target_pairs={{0,3},{1,2},{2,1},{3,0},{4,7},{5,6},{6,5},{7,4},{8,11},{9,10},{10,... | collective-permute-start | bytes 331784 | tf_op jit(solution)/shard_map/ppermute | solution.py:327
  7.1 11.1 %collective-permute-start.3 = (bf16[96,576]{1,0:T(8,128)(2,1)S(1)}, bf16[96,576]{1,0:T(8,128)(2,1)S(1)}, u32[]{:S(2)}, u32[]{:S(2)}) collective-permute-start(bf16[96,576]{1,0:T(8,128)(2,1)S(1)} %convert_element_type.112), channel_id=1, source_target_pairs={{0,1},{1,0},{2,3},{3,2},{4,5},{5,4},{6,7},{7,6},{8,9},{9,8},{10,11... | collective-permute-start | bytes 331784 | tf_op jit(solution)/shard_map/ppermute | solution.py:327
  15.2 6.3 %collective-permute-start.7 = (bf16[2,96,576]{2,1,0:T(8,128)(2,1)S(1)}, bf16[2,96,576]{2,1,0:T(8,128)(2,1)S(1)}, u32[]{:S(2)}, u32[]{:S(2)}) collective-permute-start(bf16[2,96,576]{2,1,0:T(8,128)(2,1)S(1)} %get-tuple-element.193), channel_id=1, source_target_pairs={{0,16},{4,20},{8,24},{12,28},{16,0},{20,4},{24,8},{28,12},{1,17},{... | collective-permute-start | bytes 663560 | tf_op jit(solution)/shard_map/ppermute | solution.py:327
  18.2 8.8 %collective-permute-start.4 = (bf16[2,96,576]{2,1,0:T(8,128)(2,1)S(1)}, bf16[2,96,576]{2,1,0:T(8,128)(2,1)S(1)}, u32[]{:S(2)}, u32[]{:S(2)}) collective-permute-start(bf16[2,96,576]{2,1,0:T(8,128)(2,1)S(1)} %get-tuple-element.195), channel_id=1, source_target_pairs={{0,8},{4,12},{8,0},{12,4},{16,24},{20,28},{24,16},{28,20},{1,9},{5... | collective-permute-start | bytes 663560 | tf_op jit(solution)/shard_map/ppermute | solution.py:327
  21.6 14.6 %collective-permute-start.9 = (bf16[2,2,96,576]{3,2,1,0:T(8,128)(2,1)S(1)}, bf16[2,2,96,576]{3,2,1,0:T(8,128)(2,1)S(1)}, u32[]{:S(2)}, u32[]{:S(2)}) collective-permute-start(bf16[2,2,96,576]{3,2,1,0:T(8,128)(2,1)S(1)} %pad_maximum_fusion.5.refs_5_), channel_id=1, source_target_pairs={{0,8},{4,12},{8,0},{12,4},{16,24},{20,28},{24,16},{28,20},{1,9},{5... | collective-permute-start | bytes 1327112 | tf_op jit(solution)/shard_map/ppermute | solution.py:327
  27.1 9.0 %collective-permute-start.8 = (bf16[2,2,96,576]{3,2,1,0:T(8,128)(2,1)S(1)}, bf16[2,2,96,576]{3,2,1,0:T(8,128)(2,1)S(1)}, u32[]{:S(2)}, u32[]{:S(2)}) collective-permute-start(bf16[2,2,96,576]{3,2,1,0:T(8,128)(2,1)S(1)} %pad_maximum_fusion.4.refs_4_), channel_id=1, source_target_pairs={{0,16},{4,20},{8,24},{12,28},{16,0},{20,4},{24,8},{28,12},{1,17},{... | collective-permute-start | bytes 1327112 | tf_op jit(solution)/shard_map/ppermute | solution.py:327
  27.3 5.5 %collective-permute-start.2 = (bf16[16,192]{1,0:T(8,128)(2,1)S(1)}, bf16[16,192]{1,0:T(8,128)(2,1)S(1)}, u32[]{:S(2)}, u32[]{:S(2)}) collective-permute-start(bf16[16,192]{1,0:T(8,128)(2,1)S(1)} %pad.4.refs_0_), channel_id=1, source_target_pairs={{0,3},{1,2},{2,1},{3,0},{4,7},{5,6},{6,5},{7,4},{8,11},{9,10},{10,... | collective-permute-start | bytes 18440 | tf_op jit(solution)/shard_map/ppermute | solution.py:327
  29.3 4.5 %collective-permute-start.1 = (bf16[16,192]{1,0:T(8,128)(2,1)S(1)}, bf16[16,192]{1,0:T(8,128)(2,1)S(1)}, u32[]{:S(2)}, u32[]{:S(2)}) collective-permute-start(bf16[16,192]{1,0:T(8,128)(2,1)S(1)} %pad.4.refs_0_), channel_id=1, source_target_pairs={{0,2},{1,3},{2,0},{3,1},{4,6},{5,7},{6,4},{7,5},{8,10},{9,11},{10,... | collective-permute-start | bytes 18440 | tf_op jit(solution)/shard_map/ppermute | solution.py:327
  31.1 11.7 %collective-permute-start.11 = (bf16[2,2,96,576]{3,2,1,0:T(8,128)(2,1)S(1)}, bf16[2,2,96,576]{3,2,1,0:T(8,128)(2,1)S(1)}, u32[]{:S(2)}, u32[]{:S(2)}) collective-permute-start(bf16[2,2,96,576]{3,2,1,0:T(8,128)(2,1)S(1)} %pad_maximum_fusion.5.refs_5_), channel_id=1, source_target_pairs={{0,4},{4,0},{8,12},{12,8},{16,20},{20,16},{24,28},{28,24},{1,5},{5... | collective-permute-start | bytes 1327112 | tf_op jit(solution)/shard_map/ppermute | solution.py:327
  32.8 11.9 %collective-permute-start.10 = (bf16[2,2,96,576]{3,2,1,0:T(8,128)(2,1)S(1)}, bf16[2,2,96,576]{3,2,1,0:T(8,128)(2,1)S(1)}, u32[]{:S(2)}, u32[]{:S(2)}) collective-permute-start(bf16[2,2,96,576]{3,2,1,0:T(8,128)(2,1)S(1)} %pad_maximum_fusion.4.refs_4_), channel_id=1, source_target_pairs={{0,4},{4,0},{8,12},{12,8},{16,20},{20,16},{24,28},{28,24},{1,5},{5... | collective-permute-start | bytes 1327112 | tf_op jit(solution)/shard_map/ppermute | solution.py:327
  33.9 5.2 %collective-permute-start = (bf16[16,192]{1,0:T(8,128)(2,1)S(1)}, bf16[16,192]{1,0:T(8,128)(2,1)}, u32[]{:S(2)}, u32[]{:S(2)}) collective-permute-start(bf16[16,192]{1,0:T(8,128)(2,1)S(1)} %pad.4.refs_0_), channel_id=1, source_target_pairs={{0,1},{1,0},{2,3},{3,2},{4,5},{5,4},{6,7},{7,6},{8,9},{9,8},{10,11... | collective-permute-start | bytes 18440 | tf_op jit(solution)/shard_map/ppermute | solution.py:327
  36.2 9.7 %collective-permute-start.13 = (bf16[2,2,96,576]{3,2,1,0:T(8,128)(2,1)S(1)}, bf16[2,2,96,576]{3,2,1,0:T(8,128)(2,1)}, u32[]{:S(2)}, u32[]{:S(2)}) collective-permute-start(bf16[2,2,96,576]{3,2,1,0:T(8,128)(2,1)S(1)} %collective-permute-done.9.refs_7_), channel_id=1, source_target_pairs={{0,4},{4,0},{8,12},{12,8},{16,20},{20,16},{24,28},{28,24},{1,5},{5... | collective-permute-start | bytes 1327112 | tf_op jit(solution)/shard_map/ppermute | solution.py:327
  36.2 9.7 %collective-permute-start.12 = (bf16[2,2,96,576]{3,2,1,0:T(8,128)(2,1)S(1)}, bf16[2,2,96,576]{3,2,1,0:T(8,128)(2,1)}, u32[]{:S(2)}, u32[]{:S(2)}) collective-permute-start(bf16[2,2,96,576]{3,2,1,0:T(8,128)(2,1)S(1)} %collective-permute-done.8.refs_6_), channel_id=1, source_target_pairs={{0,4},{4,0},{8,12},{12,8},{16,20},{20,16},{24,28},{28,24},{1,5},{5... | collective-permute-start | bytes 1327112 | tf_op jit(solution)/shard_map/ppermute | solution.py:327
  39.1 13.2 %collective-permute-start.19 = (bf16[96,1792]{1,0:T(8,128)(2,1)S(1)}, bf16[96,1792]{1,0:T(8,128)(2,1)}, u32[]{:S(2)}, u32[]{:S(2)}) collective-permute-start(bf16[96,1792]{1,0:T(8,128)(2,1)S(1)} %concatenate.6), channel_id=1, source_target_pairs={{0,3},{1,2},{2,1},{3,0},{4,7},{5,6},{6,5},{7,4},{8,11},{9,10},{10,... | collective-permute-start | bytes 1032200 | tf_op jit(solution)/shard_map/ppermute | solution.py:327
  42.8 30.8 %collective-permute-start.18 = (bf16[96,1792]{1,0:T(8,128)(2,1)S(1)}, bf16[96,1792]{1,0:T(8,128)(2,1)S(1)}, u32[]{:S(2)}, u32[]{:S(2)}) collective-permute-start(bf16[96,1792]{1,0:T(8,128)(2,1)S(1)} %concatenate.6), channel_id=1, source_target_pairs={{0,2},{1,3},{2,0},{3,1},{4,6},{5,7},{6,4},{7,5},{8,10},{9,11},{10,... | collective-permute-start | bytes 1032200 | tf_op jit(solution)/shard_map/ppermute | solution.py:327
  44.7 28.9 %collective-permute-start.17 = (bf16[96,1792]{1,0:T(8,128)(2,1)S(1)}, bf16[96,1792]{1,0:T(8,128)(2,1)S(1)}, u32[]{:S(2)}, u32[]{:S(2)}) collective-permute-start(bf16[96,1792]{1,0:T(8,128)(2,1)S(1)} %concatenate.6), channel_id=1, source_target_pairs={{0,1},{1,0},{2,3},{3,2},{4,5},{5,4},{6,7},{7,6},{8,9},{9,8},{10,11... | collective-permute-start | bytes 1032200 | tf_op jit(solution)/shard_map/ppermute | solution.py:327
  73.7 30.0 %collective-permute-start.20 = (bf16[2,96,1792]{2,1,0:T(8,128)(2,1)S(1)}, bf16[2,96,1792]{2,1,0:T(8,128)(2,1)S(1)}, u32[]{:S(2)}, u32[]{:S(2)}) collective-permute-start(bf16[2,96,1792]{2,1,0:T(8,128)(2,1)S(1)} %get-tuple-element.189), channel_id=1, source_target_pairs={{0,8},{4,12},{8,0},{12,4},{16,24},{20,28},{24,16},{28,20},{1,9},{5... | collective-permute-start | bytes 2064392 | tf_op jit(solution)/shard_map/ppermute | solution.py:327
  76.3 27.4 %collective-permute-start.21 = (bf16[2,96,1792]{2,1,0:T(8,128)(2,1)S(1)}, bf16[2,96,1792]{2,1,0:T(8,128)(2,1)S(1)}, u32[]{:S(2)}, u32[]{:S(2)}) collective-permute-start(bf16[2,96,1792]{2,1,0:T(8,128)(2,1)S(1)} %get-tuple-element.187), channel_id=1, source_target_pairs={{0,16},{4,20},{8,24},{12,28},{16,0},{20,4},{24,8},{28,12},{1,17},{... | collective-permute-start | bytes 2064392 | tf_op jit(solution)/shard_map/ppermute | solution.py:327
  77.6 15.3 %collective-permute-start.14 = (bf16[256,576]{1,0:T(8,128)(2,1)S(1)}, bf16[256,576]{1,0:T(8,128)(2,1)S(1)}, u32[]{:S(2)}, u32[]{:S(2)}) collective-permute-start(bf16[256,576]{1,0:T(8,128)(2,1)S(1)} %copy-done.54), channel_id=1, source_target_pairs={{0,1},{1,0},{2,3},{3,2},{4,5},{5,4},{6,7},{7,6},{8,9},{9,8},{10,11... | collective-permute-start | bytes 884744 | tf_op jit(solution)/shard_map/ppermute | solution.py:327
  77.7 26.0 %collective-permute-start.15 = (bf16[256,576]{1,0:T(8,128)(2,1)S(1)}, bf16[256,576]{1,0:T(8,128)(2,1)S(1)}, u32[]{:S(2)}, u32[]{:S(2)}) collective-permute-start(bf16[256,576]{1,0:T(8,128)(2,1)S(1)} %copy-done.53), channel_id=1, source_target_pairs={{0,2},{1,3},{2,0},{3,1},{4,6},{5,7},{6,4},{7,5},{8,10},{9,11},{10,... | collective-permute-start | bytes 884744 | tf_op jit(solution)/shard_map/ppermute | solution.py:327
  81.0 22.7 %collective-permute-start.16 = (bf16[256,576]{1,0:T(8,128)(2,1)S(1)}, bf16[256,576]{1,0:T(8,128)(2,1)S(1)}, u32[]{:S(2)}, u32[]{:S(2)}) collective-permute-start(bf16[256,576]{1,0:T(8,128)(2,1)S(1)} %copy-done.52), channel_id=1, source_target_pairs={{0,3},{1,2},{2,1},{3,0},{4,7},{5,6},{6,5},{7,4},{8,11},{9,10},{10,... | collective-permute-start | bytes 884744 | tf_op jit(solution)/shard_map/ppermute | solution.py:327
  104.5 29.1 %collective-permute-start.26 = (bf16[2,2,96,1792]{3,2,1,0:T(8,128)(2,1)S(1)}, bf16[2,2,96,1792]{3,2,1,0:T(8,128)(2,1)S(1)}, u32[]{:S(2)}, u32[]{:S(2)}) collective-permute-start(bf16[2,2,96,1792]{3,2,1,0:T(8,128)(2,1)S(1)} %pad_maximum_fusion.1.refs_9_), channel_id=1, source_target_pairs={{0,8},{4,12},{8,0},{12,4},{16,24},{20,28},{24,16},{28,20},{1,9},{5... | collective-permute-start | bytes 4128776 | tf_op jit(solution)/shard_map/ppermute | solution.py:327
  105.5 28.9 %collective-permute-start.25 = (bf16[2,2,96,1792]{3,2,1,0:T(8,128)(2,1)S(1)}, bf16[2,2,96,1792]{3,2,1,0:T(8,128)(2,1)S(1)}, u32[]{:S(2)}, u32[]{:S(2)}) collective-permute-start(bf16[2,2,96,1792]{3,2,1,0:T(8,128)(2,1)S(1)} %pad_maximum_fusion.refs_8_), channel_id=1, source_target_pairs={{0,16},{4,20},{8,24},{12,28},{16,0},{20,4},{24,8},{28,12},{1,17},{... | collective-permute-start | bytes 4128776 | tf_op jit(solution)/shard_map/ppermute | solution.py:327
  119.0 9.2 %collective-permute-start.22 = (bf16[256,192]{1,0:T(8,128)(2,1)}, bf16[256,192]{1,0:T(8,128)(2,1)S(1)}, u32[]{:S(2)}, u32[]{:S(2)}) collective-permute-start(bf16[256,192]{1,0:T(8,128)(2,1)} %get-tuple-element.106), channel_id=1, source_target_pairs={{0,1},{1,0},{2,3},{3,2},{4,5},{5,4},{6,7},{7,6},{8,9},{9,8},{10,11... | collective-permute-start | bytes 294920 | tf_op jit(solution)/shard_map/ppermute | solution.py:327
  125.0 32.2 %collective-permute-start.28 = (bf16[2,2,96,1792]{3,2,1,0:T(8,128)(2,1)S(1)}, bf16[2,2,96,1792]{3,2,1,0:T(8,128)(2,1)S(1)}, u32[]{:S(2)}, u32[]{:S(2)}) collective-permute-start(bf16[2,2,96,1792]{3,2,1,0:T(8,128)(2,1)S(1)} %pad_maximum_fusion.1.refs_9_), channel_id=1, source_target_pairs={{0,4},{4,0},{8,12},{12,8},{16,20},{20,16},{24,28},{28,24},{1,5},{5... | collective-permute-start | bytes 4128776 | tf_op jit(solution)/shard_map/ppermute | solution.py:327
  125.0 32.2 %collective-permute-start.27 = (bf16[2,2,96,1792]{3,2,1,0:T(8,128)(2,1)S(1)}, bf16[2,2,96,1792]{3,2,1,0:T(8,128)(2,1)S(1)}, u32[]{:S(2)}, u32[]{:S(2)}) collective-permute-start(bf16[2,2,96,1792]{3,2,1,0:T(8,128)(2,1)S(1)} %pad_maximum_fusion.refs_8_), channel_id=1, source_target_pairs={{0,4},{4,0},{8,12},{12,8},{16,20},{20,16},{24,28},{28,24},{1,5},{5... | collective-permute-start | bytes 4128776 | tf_op jit(solution)/shard_map/ppermute | solution.py:327
  133.7 26.0 %copy-start.42 = (bf16[2,2,96,1792]{3,2,1,0:T(8,128)(2,1)}, bf16[2,2,96,1792]{3,2,1,0:T(8,128)(2,1)S(1)}, u32[]{:S(2)}) copy-start(bf16[2,2,96,1792]{3,2,1,0:T(8,128)(2,1)S(1)} %collective-permute-done.26.refs_11_) | copy-start | bytes 4128772
  134.5 22.8 %collective-permute-start.29 = (bf16[2,2,96,1792]{3,2,1,0:T(8,128)(2,1)S(1)}, bf16[2,2,96,1792]{3,2,1,0:T(8,128)(2,1)S(1)}, u32[]{:S(2)}, u32[]{:S(2)}) collective-permute-start(bf16[2,2,96,1792]{3,2,1,0:T(8,128)(2,1)S(1)} %collective-permute-done.25.refs_10_), channel_id=1, source_target_pairs={{0,4},{4,0},{8,12},{12,8},{16,20},{20,16},{24,28},{28,24},{1,5},{5... | collective-permute-start | bytes 4128776 | tf_op jit(solution)/shard_map/ppermute | solution.py:327
  134.5 22.8 %collective-permute-start.30 = (bf16[2,2,96,1792]{3,2,1,0:T(8,128)(2,1)S(1)}, bf16[2,2,96,1792]{3,2,1,0:T(8,128)(2,1)S(1)}, u32[]{:S(2)}, u32[]{:S(2)}) collective-permute-start(bf16[2,2,96,1792]{3,2,1,0:T(8,128)(2,1)S(1)} %collective-permute-done.26.refs_11_), channel_id=1, source_target_pairs={{0,4},{4,0},{8,12},{12,8},{16,20},{20,16},{24,28},{28,24},{1,5},{5... | collective-permute-start | bytes 4128776 | tf_op jit(solution)/shard_map/ppermute | solution.py:327
  135.0 15.2 %collective-permute-start.23 = (bf16[256,192]{1,0:T(8,128)(2,1)}, bf16[256,192]{1,0:T(8,128)(2,1)S(1)}, u32[]{:S(2)}, u32[]{:S(2)}) collective-permute-start(bf16[256,192]{1,0:T(8,128)(2,1)} %get-tuple-element.107), channel_id=1, source_target_pairs={{0,2},{1,3},{2,0},{3,1},{4,6},{5,7},{6,4},{7,5},{8,10},{9,11},{10,... | collective-permute-start | bytes 294920 | tf_op jit(solution)/shard_map/ppermute | solution.py:327
  150.2 7.0 %collective-permute-start.24 = (bf16[256,192]{1,0:T(8,128)(2,1)}, bf16[256,192]{1,0:T(8,128)(2,1)S(1)}, u32[]{:S(2)}, u32[]{:S(2)}) collective-permute-start(bf16[256,192]{1,0:T(8,128)(2,1)} %get-tuple-element.108), channel_id=1, source_target_pairs={{0,3},{1,2},{2,1},{3,0},{4,7},{5,6},{6,5},{7,4},{8,11},{9,10},{10,... | collective-permute-start | bytes 294920 | tf_op jit(solution)/shard_map/ppermute | solution.py:327
  177.7 7.6 %collective-permute-start.31 = (bf16[9,256,768]{2,1,0:T(8,128)(2,1)}, bf16[9,256,768]{2,1,0:T(8,128)(2,1)S(1)}, u32[]{:S(2)}, u32[]{:S(2)}) collective-permute-start(bf16[9,256,768]{2,1,0:T(8,128)(2,1)} %get-tuple-element.115.refs_2_), channel_id=1, source_target_pairs={{0,4},{4,0},{8,12},{12,8},{16,20},{20,16},{24,28},{28,24},{1,5},{5... | collective-permute-start | bytes 10616840 | tf_op jit(solution)/shard_map/ppermute | solution.py:327
  177.8 7.5 %collective-permute-start.32 = (bf16[4,256,384]{2,1,0:T(8,128)(2,1)}, bf16[4,256,384]{2,1,0:T(8,128)(2,1)S(1)}, u32[]{:S(2)}, u32[]{:S(2)}) collective-permute-start(bf16[4,256,384]{2,1,0:T(8,128)(2,1)} %get-tuple-element.117), channel_id=1, source_target_pairs={{0,4},{4,0},{8,12},{12,8},{16,20},{20,16},{24,28},{28,24},{1,5},{5... | collective-permute-start | bytes 2359304 | tf_op jit(solution)/shard_map/ppermute | solution.py:327
  178.3 19.2 %collective-permute-start.33 = (bf16[256,192]{1,0:T(8,128)(2,1)}, bf16[256,192]{1,0:T(8,128)(2,1)S(1)}, u32[]{:S(2)}, u32[]{:S(2)}) collective-permute-start(bf16[256,192]{1,0:T(8,128)(2,1)} %get-tuple-element.123), channel_id=1, source_target_pairs={{0,1},{1,0},{2,3},{3,2},{4,5},{5,4},{6,7},{7,6},{8,9},{9,8},{10,11... | collective-permute-start | bytes 294920 | tf_op jit(solution)/shard_map/ppermute | solution.py:327
  178.3 19.2 %collective-permute-start.34 = (bf16[256,192]{1,0:T(8,128)(2,1)}, bf16[256,192]{1,0:T(8,128)(2,1)S(1)}, u32[]{:S(2)}, u32[]{:S(2)}) collective-permute-start(bf16[256,192]{1,0:T(8,128)(2,1)} %get-tuple-element.124), channel_id=1, source_target_pairs={{0,2},{1,3},{2,0},{3,1},{4,6},{5,7},{6,4},{7,5},{8,10},{9,11},{10,... | collective-permute-start | bytes 294920 | tf_op jit(solution)/shard_map/ppermute | solution.py:327
  180.3 17.2 %collective-permute-start.35 = (bf16[256,192]{1,0:T(8,128)(2,1)}, bf16[256,192]{1,0:T(8,128)(2,1)S(1)}, u32[]{:S(2)}, u32[]{:S(2)}) collective-permute-start(bf16[256,192]{1,0:T(8,128)(2,1)} %get-tuple-element.125), channel_id=1, source_target_pairs={{0,3},{1,2},{2,1},{3,0},{4,7},{5,6},{6,5},{7,4},{8,11},{9,10},{10,... | collective-permute-start | bytes 294920 | tf_op jit(solution)/shard_map/ppermute | solution.py:327
  197.5 48.7 %collective-permute-start.36 = (bf16[2,2,96,1792]{3,2,1,0:T(8,128)(2,1)}, bf16[2,2,96,1792]{3,2,1,0:T(8,128)(2,1)S(1)}, u32[]{:S(2)}, u32[]{:S(2)}) collective-permute-start(bf16[2,2,96,1792]{3,2,1,0:T(8,128)(2,1)} %get-tuple-element.126), channel_id=1, source_target_pairs={{0,16},{4,20},{8,24},{12,28},{16,0},{20,4},{24,8},{28,12},{1,17},{... | collective-permute-start | bytes 4128776 | tf_op jit(solution)/shard_map/ppermute | solution.py:327
  198.8 47.5 %collective-permute-start.37 = (bf16[2,2,96,1792]{3,2,1,0:T(8,128)(2,1)}, bf16[2,2,96,1792]{3,2,1,0:T(8,128)(2,1)S(1)}, u32[]{:S(2)}, u32[]{:S(2)}) collective-permute-start(bf16[2,2,96,1792]{3,2,1,0:T(8,128)(2,1)} %get-tuple-element.127), channel_id=1, source_target_pairs={{0,8},{4,12},{8,0},{12,4},{16,24},{20,28},{24,16},{28,20},{1,9},{5... | collective-permute-start | bytes 4128776 | tf_op jit(solution)/shard_map/ppermute | solution.py:327
  216.2 15.5 %collective-permute-start.38 = (bf16[256,576]{1,0:T(8,128)(2,1)}, bf16[256,576]{1,0:T(8,128)(2,1)S(1)}, u32[]{:S(2)}, u32[]{:S(2)}) collective-permute-start(bf16[256,576]{1,0:T(8,128)(2,1)} %get-tuple-element.133), channel_id=1, source_target_pairs={{0,1},{1,0},{2,3},{3,2},{4,5},{5,4},{6,7},{7,6},{8,9},{9,8},{10,11... | collective-permute-start | bytes 884744 | tf_op jit(solution)/shard_map/ppermute | solution.py:327
  216.2 25.8 %collective-permute-start.39 = (bf16[256,576]{1,0:T(8,128)(2,1)}, bf16[256,576]{1,0:T(8,128)(2,1)S(1)}, u32[]{:S(2)}, u32[]{:S(2)}) collective-permute-start(bf16[256,576]{1,0:T(8,128)(2,1)} %get-tuple-element.134), channel_id=1, source_target_pairs={{0,2},{1,3},{2,0},{3,1},{4,6},{5,7},{6,4},{7,5},{8,10},{9,11},{10,... | collective-permute-start | bytes 884744 | tf_op jit(solution)/shard_map/ppermute | solution.py:327
  218.3 23.8 %collective-permute-start.40 = (bf16[256,576]{1,0:T(8,128)(2,1)}, bf16[256,576]{1,0:T(8,128)(2,1)S(1)}, u32[]{:S(2)}, u32[]{:S(2)}) collective-permute-start(bf16[256,576]{1,0:T(8,128)(2,1)} %get-tuple-element.135), channel_id=1, source_target_pairs={{0,3},{1,2},{2,1},{3,0},{4,7},{5,6},{6,5},{7,4},{8,11},{9,10},{10,... | collective-permute-start | bytes 884744 | tf_op jit(solution)/shard_map/ppermute | solution.py:327
  231.7 10.9 %collective-permute-start.41 = (bf16[256,576]{1,0:T(8,128)(2,1)}, bf16[256,576]{1,0:T(8,128)(2,1)S(1)}, u32[]{:S(2)}, u32[]{:S(2)}) collective-permute-start(bf16[256,576]{1,0:T(8,128)(2,1)} %get-tuple-element.136.refs_2_), channel_id=1, source_target_pairs={{0,4},{4,0},{8,12},{12,8},{16,20},{20,16},{24,28},{28,24},{1,5},{5... | collective-permute-start | bytes 884744 | tf_op jit(solution)/shard_map/ppermute | solution.py:327
  242.0 4.2 %collective-permute-start.42 = (bf16[256,576]{1,0:T(8,128)(2,1)S(1)}, bf16[256,576]{1,0:T(8,128)(2,1)S(1)}, u32[]{:S(2)}, u32[]{:S(2)}) collective-permute-start(bf16[256,576]{1,0:T(8,128)(2,1)S(1)} %collective-permute-done.38.refs_3_), channel_id=1, source_target_pairs={{0,4},{4,0},{8,12},{12,8},{16,20},{20,16},{24,28},{28,24},{1,5},{5... | collective-permute-start | bytes 884744 | tf_op jit(solution)/shard_map/ppermute | solution.py:327
  242.0 4.2 %collective-permute-start.43 = (bf16[256,576]{1,0:T(8,128)(2,1)S(1)}, bf16[256,576]{1,0:T(8,128)(2,1)S(1)}, u32[]{:S(2)}, u32[]{:S(2)}) collective-permute-start(bf16[256,576]{1,0:T(8,128)(2,1)S(1)} %collective-permute-done.39.refs_4_), channel_id=1, source_target_pairs={{0,4},{4,0},{8,12},{12,8},{16,20},{20,16},{24,28},{28,24},{1,5},{5... | collective-permute-start | bytes 884744 | tf_op jit(solution)/shard_map/ppermute | solution.py:327
  242.5 3.7 %collective-permute-start.44 = (bf16[256,576]{1,0:T(8,128)(2,1)S(1)}, bf16[256,576]{1,0:T(8,128)(2,1)S(1)}, u32[]{:S(2)}, u32[]{:S(2)}) collective-permute-start(bf16[256,576]{1,0:T(8,128)(2,1)S(1)} %collective-permute-done.40.refs_5_), channel_id=1, source_target_pairs={{0,4},{4,0},{8,12},{12,8},{16,20},{20,16},{24,28},{28,24},{1,5},{5... | collective-permute-start | bytes 884744 | tf_op jit(solution)/shard_map/ppermute | solution.py:327
  253.7 14.4 %collective-permute-start.45 = (bf16[2,2,96,576]{3,2,1,0:T(8,128)(2,1)}, bf16[2,2,96,576]{3,2,1,0:T(8,128)(2,1)}, u32[]{:S(2)}, u32[]{:S(2)}) collective-permute-start(bf16[2,2,96,576]{3,2,1,0:T(8,128)(2,1)} %get-tuple-element.150), channel_id=1, source_target_pairs={{0,16},{4,20},{8,24},{12,28},{16,0},{20,4},{24,8},{28,12},{1,17},{... | collective-permute-start | bytes 1327112 | tf_op jit(solution)/shard_map/ppermute | solution.py:327
  254.3 15.8 %collective-permute-start.48 = (bf16[2,2,96,576]{3,2,1,0:T(8,128)(2,1)}, bf16[2,2,96,576]{3,2,1,0:T(8,128)(2,1)}, u32[]{:S(2)}, u32[]{:S(2)}) collective-permute-start(bf16[2,2,96,576]{3,2,1,0:T(8,128)(2,1)} %get-tuple-element.152), channel_id=1, source_target_pairs={{0,8},{4,12},{8,0},{12,4},{16,24},{20,28},{24,16},{28,20},{1,9},{5... | collective-permute-start | bytes 1327112 | tf_op jit(solution)/shard_map/ppermute | solution.py:327
  255.5 38.7 %collective-permute-start.52 = (bf16[2,96,1792]{2,1,0:T(8,128)(2,1)S(1)}, bf16[2,96,1792]{2,1,0:T(8,128)(2,1)S(1)}, u32[]{:S(2)}, u32[]{:S(2)}) collective-permute-start(bf16[2,96,1792]{2,1,0:T(8,128)(2,1)S(1)} %fusion.3), channel_id=1, source_target_pairs={{0,8},{4,12},{8,0},{12,4},{16,24},{20,28},{24,16},{28,20},{1,9},{5... | collective-permute-start | bytes 2064392 | tf_op jit(solution)/shard_map/ppermute | solution.py:327
  257.1 37.1 %collective-permute-start.53 = (bf16[2,96,1792]{2,1,0:T(8,128)(2,1)S(1)}, bf16[2,96,1792]{2,1,0:T(8,128)(2,1)S(1)}, u32[]{:S(2)}, u32[]{:S(2)}) collective-permute-start(bf16[2,96,1792]{2,1,0:T(8,128)(2,1)S(1)} %fusion.4), channel_id=1, source_target_pairs={{0,16},{4,20},{8,24},{12,28},{16,0},{20,4},{24,8},{28,12},{1,17},{... | collective-permute-start | bytes 2064392 | tf_op jit(solution)/shard_map/ppermute | solution.py:327
  269.4 18.3 %collective-permute-start.46 = (bf16[2,96,576]{2,1,0:T(8,128)(2,1)S(1)}, bf16[2,96,576]{2,1,0:T(8,128)(2,1)S(1)}, u32[]{:S(2)}, u32[]{:S(2)}) collective-permute-start(bf16[2,96,576]{2,1,0:T(8,128)(2,1)S(1)} %fusion.14), channel_id=1, source_target_pairs={{0,8},{4,12},{8,0},{12,4},{16,24},{20,28},{24,16},{28,20},{1,9},{5... | collective-permute-start | bytes 663560 | tf_op jit(solution)/shard_map/ppermute | solution.py:327
  271.2 22.4 %collective-permute-start.49 = (bf16[2,96,576]{2,1,0:T(8,128)(2,1)S(1)}, bf16[2,96,576]{2,1,0:T(8,128)(2,1)S(1)}, u32[]{:S(2)}, u32[]{:S(2)}) collective-permute-start(bf16[2,96,576]{2,1,0:T(8,128)(2,1)S(1)} %fusion.15), channel_id=1, source_target_pairs={{0,16},{4,20},{8,24},{12,28},{16,0},{20,4},{24,8},{28,12},{1,17},{... | collective-permute-start | bytes 663560 | tf_op jit(solution)/shard_map/ppermute | solution.py:327
  287.8 28.3 %collective-permute-start.47 = (bf16[96,576]{1,0:T(8,128)(2,1)S(1)}, bf16[96,576]{1,0:T(8,128)(2,1)S(1)}, u32[]{:S(2)}, u32[]{:S(2)}) collective-permute-start(bf16[96,576]{1,0:T(8,128)(2,1)S(1)} %fusion.18), channel_id=1, source_target_pairs={{0,1},{1,0},{2,3},{3,2},{4,5},{5,4},{6,7},{7,6},{8,9},{9,8},{10,11... | collective-permute-start | bytes 331784 | tf_op jit(solution)/shard_map/ppermute | solution.py:327
  293.7 24.9 %collective-permute-start.50 = (bf16[96,576]{1,0:T(8,128)(2,1)S(1)}, bf16[96,576]{1,0:T(8,128)(2,1)S(1)}, u32[]{:S(2)}, u32[]{:S(2)}) collective-permute-start(bf16[96,576]{1,0:T(8,128)(2,1)S(1)} %get-tuple-element.190), channel_id=1, source_target_pairs={{0,2},{1,3},{2,0},{3,1},{4,6},{5,7},{6,4},{7,5},{8,10},{9,11},{10,... | collective-permute-start | bytes 331784 | tf_op jit(solution)/shard_map/ppermute | solution.py:327
  294.2 4.6 %collective-permute-start.57 = (f32[16,192]{1,0:T(8,128)S(1)}, f32[16,192]{1,0:T(8,128)S(1)}, u32[]{:S(2)}, u32[]{:S(2)}) collective-permute-start(f32[16,192]{1,0:T(8,128)S(1)} %copy-done.63), channel_id=1, source_target_pairs={{0,1},{1,0},{2,3},{3,2},{4,5},{5,4},{6,7},{7,6},{8,9},{9,8},{10,11... | collective-permute-start | bytes 36872 | tf_op jit(solution)/shard_map/ppermute | solution.py:327
  296.3 9.7 %collective-permute-start.58 = (f32[16,192]{1,0:T(8,128)S(1)}, f32[16,192]{1,0:T(8,128)S(1)}, u32[]{:S(2)}, u32[]{:S(2)}) collective-permute-start(f32[16,192]{1,0:T(8,128)S(1)} %copy-done.62), channel_id=1, source_target_pairs={{0,2},{1,3},{2,0},{3,1},{4,6},{5,7},{6,4},{7,5},{8,10},{9,11},{10,... | collective-permute-start | bytes 36872 | tf_op jit(solution)/shard_map/ppermute | solution.py:327
  296.9 9.1 %collective-permute-start.59 = (f32[16,192]{1,0:T(8,128)S(1)}, f32[16,192]{1,0:T(8,128)S(1)}, u32[]{:S(2)}, u32[]{:S(2)}) collective-permute-start(f32[16,192]{1,0:T(8,128)S(1)} %copy-done.61), channel_id=1, source_target_pairs={{0,3},{1,2},{2,1},{3,0},{4,7},{5,6},{6,5},{7,4},{8,11},{9,10},{10,... | collective-permute-start | bytes 36872 | tf_op jit(solution)/shard_map/ppermute | solution.py:327
  298.9 19.8 %collective-permute-start.51 = (bf16[96,576]{1,0:T(8,128)(2,1)S(1)}, bf16[96,576]{1,0:T(8,128)(2,1)S(1)}, u32[]{:S(2)}, u32[]{:S(2)}) collective-permute-start(bf16[96,576]{1,0:T(8,128)(2,1)S(1)} %get-tuple-element.191), channel_id=1, source_target_pairs={{0,3},{1,2},{2,1},{3,0},{4,7},{5,6},{6,5},{7,4},{8,11},{9,10},{10,... | collective-permute-start | bytes 331784 | tf_op jit(solution)/shard_map/ppermute | solution.py:327
  306.0 1.2 collective-permute-start.60
  307.2 3.7 %collective-permute-start.61 = (f32[16,192]{1,0:T(8,128)S(1)}, f32[16,192]{1,0:T(8,128)S(1)}, u32[]{:S(2)}, u32[]{:S(2)}) collective-permute-start(f32[16,192]{1,0:T(8,128)S(1)} %add.174), channel_id=1, source_target_pairs={{0,8},{4,12},{8,0},{12,4},{16,24},{20,28},{24,16},{28,20},{1,9},{5... | collective-permute-start | bytes 36872 | tf_op jit(solution)/shard_map/ppermute | solution.py:327
  311.0 3.7 %collective-permute-start.62 = (f32[16,192]{1,0:T(8,128)S(1)}, f32[16,192]{1,0:T(8,128)S(1)}, u32[]{:S(2)}, u32[]{:S(2)}) collective-permute-start(f32[16,192]{1,0:T(8,128)S(1)} %add.175), channel_id=1, source_target_pairs={{0,16},{4,20},{8,24},{12,28},{16,0},{20,4},{24,8},{28,12},{1,17},{... | collective-permute-start | bytes 36872 | tf_op jit(solution)/shard_map/ppermute | solution.py:327
  312.5 13.9 %collective-permute-start.54 = (bf16[96,1792]{1,0:T(8,128)(2,1)S(1)}, bf16[96,1792]{1,0:T(8,128)(2,1)S(1)}, u32[]{:S(2)}, u32[]{:S(2)}) collective-permute-start(bf16[96,1792]{1,0:T(8,128)(2,1)S(1)} %fusion.10), channel_id=1, source_target_pairs={{0,1},{1,0},{2,3},{3,2},{4,5},{5,4},{6,7},{7,6},{8,9},{9,8},{10,11... | collective-permute-start | bytes 1032200 | tf_op jit(solution)/shard_map/ppermute | solution.py:327
  314.7 26.6 %collective-permute-start.55 = (bf16[96,1792]{1,0:T(8,128)(2,1)S(1)}, bf16[96,1792]{1,0:T(8,128)(2,1)S(1)}, u32[]{:S(2)}, u32[]{:S(2)}) collective-permute-start(bf16[96,1792]{1,0:T(8,128)(2,1)S(1)} %get-tuple-element.184), channel_id=1, source_target_pairs={{0,2},{1,3},{2,0},{3,1},{4,6},{5,7},{6,4},{7,5},{8,10},{9,11},{10,... | collective-permute-start | bytes 1032200 | tf_op jit(solution)/shard_map/ppermute | solution.py:327
  316.1 25.3 %collective-permute-start.56 = (bf16[96,1792]{1,0:T(8,128)(2,1)S(1)}, bf16[96,1792]{1,0:T(8,128)(2,1)S(1)}, u32[]{:S(2)}, u32[]{:S(2)}) collective-permute-start(bf16[96,1792]{1,0:T(8,128)(2,1)S(1)} %get-tuple-element.185), channel_id=1, source_target_pairs={{0,3},{1,2},{2,1},{3,0},{4,7},{5,6},{6,5},{7,4},{8,11},{9,10},{10,... | collective-permute-start | bytes 1032200 | tf_op jit(solution)/shard_map/ppermute | solution.py:327
  (63 other events, 625.9 us)

commit v4 on v3

--- a/solution.py
+++ b/solution.py
@@ -318,7 +318,19 @@
 LOW = jnp.bfloat16
 WIDE = jnp.float32
 CORE, XBIT, YBIT = 1, 2, 4
-SOURCES = (0, 2, 0, 4, 4, 6, 2, 6, 1, 3, 1, 5, 5, 7, 3, 7)
+SOURCES = (
+    (0, (0, 1, 2, 3)),
+    (XBIT, (0, 1, 2, 3)),
+    (YBIT, (0, 1, 2, 3)),
+    (XBIT + YBIT, (0, 1)),
+    (XBIT + YBIT, (2, 3)),
+    (CORE, (0, 1, 2, 3)),
+    (CORE + XBIT, (0, 1, 2, 3)),
+    (CORE + YBIT, (0, 1, 2, 3)),
+    (CORE + XBIT + YBIT, (0, 1)),
+    (CORE + XBIT + YBIT, (2, 3)),
+)
+PARTS = len(SOURCES)
 VMEM_LIMIT = 56 * 1024 * 1024
 
 
@@ -361,19 +373,16 @@
     return swap(value, "ctx", 1), swap(value, "ctx", 2), swap(value, "ctx", 3)
 
 
-def gather_first(piece, parts):
-    near, far, last = parts
-    one, two = jnp.stack([piece, near]), jnp.stack([far, last])
-    return (one, two), (swap(one, "batch", XBIT), swap(two, "batch", YBIT))
-
-
-def gather_second(kept, came):
-    one, two = jnp.stack([kept[0], came[0]]), jnp.stack([kept[1], came[1]])
-    return [one, two, swap(one, "batch", YBIT), swap(two, "batch", XBIT)]
-
-
-def gather_last(held):
-    return held + [swap(part, "batch", CORE) for part in held]
+def gather_first(own):
+    return swap(own, "batch", XBIT), swap(own, "batch", YBIT)
+
+
+def gather_second(from_x, from_y):
+    return swap(from_x[:2], "batch", YBIT), swap(from_y[2:], "batch", XBIT)
+
+
+def to_core(parts):
+    return [swap(part, "batch", CORE) for part in parts]
 
 
 def swap_pair(pair, first, second):
@@ -414,19 +423,12 @@
     ]
 
 
-def load_weight(meta, parts, place, sems):
+def load_weight(meta, parts, place, sems, shift):
     copies = []
-    for index, part in enumerate(parts):
-        for first in range(2):
-            for second in range(2):
-                batch = meta[0] ^ SOURCES[2 * index + first]
-                ctx = meta[1] ^ (2 * (index % 2) + second)
-                copies.append(
-                    [
-                        (part.at[first, second, :, lanes], target)
-                        for lanes, target in place(batch, ctx)
-                    ]
-                )
+    for part, (source, places) in zip(parts, SOURCES):
+        for index, ctx in enumerate(places):
+            ranges = place(meta[0] ^ source, ctx ^ shift)
+            copies.append([(part.at[index, :, lanes], target) for lanes, target in ranges])
     started = []
     for kind in range(len(copies[0])):
         group = []
@@ -482,14 +484,15 @@
 
 def read_vectors(meta, parts, chunks):
     for ctx, part in enumerate(parts):
-        chunks[meta[1] ^ ctx] = part[...].astype(WIDE)
+        rows = [part[16 * index : 16 * (index + 1), :] for index in range(GROUP // HEAD)]
+        chunks[meta[1] ^ ctx] = jnp.concatenate(rows, axis=1).astype(WIDE)
     return jnp.concatenate([chunks[index] for index in range(CTX)], axis=1)
 
 
 def qkv_kernel(meta, x_ref, *refs):
-    vectors, parts, refs = refs[:4], refs[4:12], refs[12:]
+    vectors, parts, refs = refs[:4], refs[4 : 4 + PARTS], refs[4 + PARTS :]
     h_ref, own, near, far, last, held, units, chunks, sems = refs
-    (copies,) = load_weight(meta, parts, functools.partial(qkv_place, held), sems)
+    (copies,) = load_weight(meta, parts, functools.partial(qkv_place, held), sems, meta[1])
     params = read_vectors(meta, vectors, chunks)
     bias = jnp.concatenate([params[4:5], jnp.zeros((1, WIDTH), WIDE), params[5:6]], axis=1)
     centred, inverse = moments(x_ref[...].astype(WIDE))
@@ -608,12 +611,12 @@
 
 
 def middle_kernel(meta, x_ref, dy_ref, h_one_ref, *refs):
-    vectors, pieces, parts, refs = refs[:4], refs[4:8], refs[8:16], refs[16:]
+    vectors, pieces, parts, refs = refs[:4], refs[4:8], refs[8 : 8 + PARTS], refs[8 + PARTS :]
     (out_ref, pack_ref, mine, theirs, dmid_ref), refs = refs[:5], refs[5:]
     results, (rows_ref, dbias_ref), refs = refs[:4], refs[4:6], refs[6:]
     out_parts, held_out, held_fc, held_proj, units, total, back, chunks, bias, acts, sems = refs
     place = functools.partial(mlp_place, out_parts, held_fc, held_proj)
-    copies = load_weight(meta, parts, place, sems)
+    copies = load_weight(meta, parts, place, sems, 0)
     vec = read_vectors(meta, vectors, chunks)
     for chunk in range(CTX):
         bias[chunk] = vec[8 + chunk : 9 + chunk]
@@ -738,9 +741,9 @@
 
 
 def input_grad_kernel(meta, x_ref, dmid_ref, mixed_ref, rows_ref, dfc_ref, dqkv_ref, *refs):
-    vectors, parts, refs = refs[:4], refs[4:12], refs[12:]
+    vectors, parts, refs = refs[:4], refs[4 : 4 + PARTS], refs[4 + PARTS :]
     grad_ref, results, (held, chunks, rows, sums, sems) = refs[0], refs[1:5], refs[5:]
-    (copies,) = load_weight(meta, parts, functools.partial(qkv_place, held), sems)
+    (copies,) = load_weight(meta, parts, functools.partial(qkv_place, held), sems, meta[1])
     params = read_vectors(meta, vectors, chunks)
     centred, inverse = moments(x_ref[...].astype(WIDE))
     normed = centred * inverse
@@ -774,11 +777,13 @@
         "v": pl.BlockSpec(memory_space=pltpu.VMEM),
         "s": pl.BlockSpec(memory_space=pltpu.SMEM),
         "a": pl.BlockSpec(memory_space=pl.ANY),
+        "h": pl.BlockSpec((None, TOKENS, WIDTH), lambda step: (CTX + 4, 0, 0)),
     }
     moved = sum(math.prod(value.shape) * value.dtype.itemsize for value in arguments)
     moved += sum(math.prod(value.shape) * value.dtype.itemsize for value in outputs)
     return pl.pallas_call(
         kernel,
+        grid=(1,),
         out_shape=tuple(outputs),
         in_specs=[spec[kind] for kind in kinds],
         out_specs=tuple(spec[kind] for kind in out_kinds),
@@ -820,7 +825,10 @@
     qkv_held = pltpu.VMEM((CTX, WIDTH, 3 * GROUP), LOW)
     vec_held = pltpu.VMEM((CTX, 16, GROUP), WIDE)
 
-    piece_one = w_qkv.astype(LOW)
+    low_vec = jnp.pad(vectors.astype(LOW), ((0, 4), (0, 0)))
+    low_vec = [low_vec[:, start : start + HEAD] for start in range(0, GROUP, HEAD)]
+    low_vec = jnp.concatenate(low_vec + [jnp.zeros((ROWS - 48, HEAD), LOW)], axis=0)
+    piece_one = jnp.concatenate([w_qkv.astype(LOW), low_vec], axis=1)
     low_proj = w_proj.astype(LOW).T
     piece_two = jnp.concatenate(
         [
@@ -832,13 +840,15 @@
         ],
         axis=1,
     )
-    low_vec = jnp.pad(vectors.astype(LOW), ((0, 4), (0, 0)))
-    parts_one = exchange(piece_one)
-    vec_parts = (low_vec,) + exchange(low_vec)
-    piece_two, _ = tie((piece_two, parts_one))
-    parts_two = exchange(piece_two)
-    parts_one = gather_second(*gather_first(piece_one, parts_one))
-    parts_one = gather_last(parts_one)
+    parts_one = (piece_one,) + exchange(piece_one)
+    vec_parts = [part[:48, 3 * GROUP :] for part in parts_one]
+    parts_one = [part[:, : 3 * GROUP] for part in parts_one]
+    own_one = jnp.stack(parts_one)
+    piece_two, late_vec = tie((piece_two, vec_parts))
+    own_two = lax.all_gather(piece_two, "ctx", axis=0)
+    x_one, y_one = gather_first(own_one)
+    parts_one = [own_one, x_one, y_one, *gather_second(x_one, y_one)]
+    parts_one = parts_one + to_core(parts_one)
 
     packed = shape_of(LOW, TOKENS, 3 * GROUP)
     single = shape_of(LOW, TOKENS, GROUP)
@@ -848,18 +858,20 @@
     h_one, own, *sent = call(
         qkv_kernel,
         (meta, inputs, *vec_parts, *parts_one),
-        "s" + "v" * 5 + "a" * 8,
+        "s" + "v" * 5 + "a" * PARTS,
         [tokens_low] + [packed] * 4,
         "v" * 5,
         [qkv_held, pltpu.VMEM((CTX, TOKENS, 3 * GROUP), LOW), vec_held, qkv_sems],
         2 * TOKENS * 3 * square,
     )
-    parts_two, _ = tie((parts_two, own))
-    kept_two, came_two = gather_first(piece_two, parts_two)
     qkv_pieces = [own] + [swap(part, "ctx", bit) for bit, part in zip((1, 2, 3), sent)]
 
-    qkv_pieces, came_two = tie((qkv_pieces, came_two))
-    parts_two = gather_second(kept_two, came_two)
+    own_two, late_h = tie((own_two, h_one))
+    x_two, y_two = gather_first(own_two)
+    qkv_pieces, x_two, y_two = tie((qkv_pieces, x_two, y_two))
+    across_two = gather_second(x_two, y_two)
+    parts_two = [own_two, x_two, y_two]
+    swapped_two = to_core(parts_two)
 
     sequence_low = pltpu.VMEM((SPAN, GROUP), LOW)
     sequence_wide = pltpu.VMEM((SPAN, GROUP), WIDE)
@@ -872,16 +884,17 @@
         [sequence_low] * 3 + [sequence_wide],
         2 * SPAN * SPAN * GROUP * 2,
     )
+    sent, swapped_two = tie((sent, swapped_two))
     att_pieces = [own] + [swap(part, "ctx", bit) for bit, part in zip((1, 2, 3), sent)]
-    last_two, _ = tie((parts_two[2:], att_pieces[1]))
-    parts_two = gather_last(parts_two[:2] + last_two)
+    across_two, att_pieces = tie((across_two, att_pieces))
+    parts_two = parts_two + list(across_two) + swapped_two + to_core(across_two)
 
     pack_shape = shape_of(LOW, CTX + 5, TOKENS, WIDTH)
     act_shape = shape_of(LOW, BATCH // 2, TOKENS, FF_SIDE)
     out, pack, act_mine, act_theirs, dmid, own, *sent = call(
         middle_kernel,
-        (meta, inputs, grad_low, h_one, *vec_parts, *att_pieces, *parts_two),
-        "s" + "v" * 11 + "a" * 8,
+        (meta, inputs, grad_low, late_h, *vec_parts, *att_pieces, *parts_two),
+        "s" + "v" * 11 + "a" * PARTS,
         [tokens_low, pack_shape, act_shape, act_shape, shape_of(WIDE, TOKENS, WIDTH)]
         + [single] * 4
         + [shape_of(WIDE, 8, WIDTH), shape_of(WIDE, CTX, 1, WIDTH)],
@@ -935,15 +948,18 @@
         2 * SPAN * SPAN * GROUP * 5,
     )
     mixed_pieces = [own] + [swap(part, "ctx", bit) for bit, part in zip((1, 2, 3), sent)]
-    mixed_came = [swap(part, "batch", CORE) for part in mixed_pieces]
-    mlp_back, mixed_pieces, mixed_came = tie((mlp_back, mixed_pieces, mixed_came))
+    came = to_core(mixed_pieces[:1])
+    mlp_back, received = tie((mlp_back, mixed_pieces[1:]))
+    mixed_pieces = mixed_pieces[:1] + received
+    mixed_came = came + to_core(received)
     mlp_kept, mlp_sent = scatter_second(mlp_kept, mlp_back)
+    mlp_sent, mixed_came = tie((mlp_sent, mixed_came))
     mlp_back = swap_pair(mlp_sent, XBIT, YBIT)
 
     *qkv_parts, mixed, dbias_qkv = call(
         qkv_grad_kernel,
-        (meta, pack[CTX + 4], pack_came[CTX + 4], *mixed_pieces, *mixed_came),
-        "s" + "v" * 10,
+        (meta, pack, pack_came, *mixed_pieces, *mixed_came),
+        "shh" + "v" * 8,
         [shape_of(LOW, 2, 2, ROWS, 3 * GROUP)] * 4
         + [shape_of(LOW, CTX, TOKENS, 3 * GROUP), shape_of(WIDE, 3 * CTX, 1, GROUP)],
         "aaaavv",
@@ -959,18 +975,21 @@
     qkv_back = swap_pair((qkv_parts[1], qkv_parts[3]), YBIT, XBIT)
     grad_input, own, *sent = call(
         input_grad_kernel,
-        (meta, inputs, dmid, mixed, rows_two, dbias_fc, dbias_qkv, *vec_parts, *parts_one),
-        "s" + "v" * 10 + "a" * 8,
+        (meta, inputs, dmid, mixed, rows_two, dbias_fc, dbias_qkv, *late_vec, *parts_one),
+        "s" + "v" * 10 + "a" * PARTS,
         [shape_of(WIDE, TOKENS, WIDTH)] + [shape_of(WIDE, 16, GROUP)] * 4,
         "v" * 5,
         [qkv_held, vec_held, pltpu.VMEM((16, WIDTH), WIDE), vec_held, qkv_sems],
         2 * TOKENS * 3 * square,
     )
-    mlp_back, own, sent = tie((mlp_back, own, sent))
-    mlp_kept, mlp_sent = scatter_third(mlp_kept, mlp_back)
+    mlp_back, qkv_back = tie((mlp_back, qkv_back))
+    mlp_one = mlp_kept[0].astype(WIDE) + mlp_back[0].astype(WIDE)
+    mlp_two = (mlp_kept[1].astype(WIDE) + mlp_back[1].astype(WIDE)).astype(LOW)
+    mlp_two = swap(mlp_two, "ctx", 2)
+    mlp_one = mlp_one + mlp_two.astype(WIDE)
+    mlp_grad = mlp_one[0] + swap(mlp_one[1].astype(LOW), "ctx", 1).astype(WIDE)
     qkv_kept, qkv_sent = scatter_second(qkv_kept, qkv_back)
     qkv_back = swap_pair(qkv_sent, XBIT, YBIT)
-    mlp_grad = scatter_last(mlp_kept, mlp_sent)
     qkv_kept, qkv_sent = scatter_third(qkv_kept, qkv_back)
     qkv_grad = scatter_last(qkv_kept, qkv_sent)
 

time: 347 us -> 321 us (0.925)
  starting transfers between devices: 88.3 us -> 63.8 us
  between operations: 1.6 us -> 14.9 us
  waiting for transfers between devices: 154 us -> 141 us
    ppermute x63 -> x58, starting transfers between devices: 88.3 us -> 63.7 us  [swap(): return lax.ppermute(value, axis, [(i, i ^ bit) for i in range(size)])]
    ppermute x63 -> x58, waiting for transfers between devices: 154 us -> 138 us  [swap(): return lax.ppermute(value, axis, [(i, i ^ bit) for i in range(size)])]
    squeeze x2 -> x0, local copies, waits for them, and re-layouts: 3.57 us -> none  [the longest x1 1.81 us: local_fast(): pack[CTX + 4]]
  transfers between devices with their start and end apart: 63 -> 59, of which waited for: 24 -> 28; matrix products, arithmetic and copies ran while one was open for 4% -> 4% of each run, Pallas kernels for 15% -> 18%
where the time goes in v4:
time: 321 us
  waiting for transfers between devices  141 us (44%)
  Pallas kernels  75.6 us (24%)
  starting transfers between devices  63.8 us (20%)
  other arithmetic  16 us (5%)
  between operations  14.9 us (5%)
  local copies, waits for them, and re-layouts  9.38 us (3%)
    ppermute x58, waiting for transfers between devices, swap(): return lax.ppermute(value, axis, [(i, i ^ bit) for i in range(size)])  138 us
    pallas_call x7, Pallas kernels, call(): pl.pallas_call(kernel, grid=(1,), out_shape=tuple(outputs), in_specs=[spe...  75.6 us
    ppermute x58, starting transfers between devices, swap(): return lax.ppermute(value, axis, [(i, i ^ bit) for i in range(size)])  63.7 us
  transfers between devices with their start and end apart: 59, of which 28 were waited for; matrix products, arithmetic and copies ran while one was open for 4% of the time, Pallas kernels for 18%

profile of v4, /device:TPU:0, one launch (start us, length us, event | category | flops | bytes accessed | tf_op | source)
XLA Modules:
  0.0 320.6 jit_solution(10301724704133641502)
XLA Ops:
  9.2 5.1 %collective-permute-start.2 = (bf16[96,640]{1,0:T(8,128)(2,1)S(1)}, bf16[96,640]{1,0:T(8,128)(2,1)S(1)}, u32[]{:S(2)}, u32[]{:S(2)}) collective-permute-start(bf16[96,640]{1,0:T(8,128)(2,1)S(1)} %maximum_maximum_fusion), channel_id=1, source_target_pairs={{0,3},{1,2},{2,1},{3,0},{4,7},{5,6},{6,5},{7,4},{8,11},{9,10},{10,... | collective-permute-start | bytes 368648 | tf_op jit(solution)/shard_map/ppermute | solution.py:339
  17.4 1.1 collective-permute-done.2
  19.2 5.5 %collective-permute-done.1 = bf16[96,640]{1,0:T(8,128)(2,1)S(1)} collective-permute-done((bf16[96,640]{1,0:T(8,128)(2,1)S(1)}, bf16[96,640]{1,0:T(8,128)(2,1)S(1)}, u32[]{:S(2)}, u32[]{:S(2)}) %collective-permute-start.1) | collective-permute-done | bytes 122912 | tf_op jit(solution)/shard_map/ppermute | solution.py:339
  26.2 1.6 collective-permute-start.4
  27.8 1.5 collective-permute-start.3
  29.3 9.3 %collective-permute-done.4.refs_6_ = bf16[4,96,576]{2,1,0:T(8,128)(2,1)S(1)} collective-permute-done((bf16[4,96,576]{2,1,0:T(8,128)(2,1)S(1)}, bf16[4,96,576]{2,1,0:T(8,128)(2,1)S(1)}, u32[]{:S(2)}, u32[]{:S(2)}) %collective-permute-start.4) | collective-permute-done | bytes 442400 | tf_op jit(solution)/shard_map/ppermute | solution.py:339
  38.6 1.6 collective-permute-start.6
  40.2 1.6 collective-permute-start.5
  42.0 3.2 collective-permute-done.6.refs_8_
  45.2 3.5 %collective-permute-done.5.refs_7_ = bf16[2,96,576]{2,1,0:T(8,128)(2,1)} collective-permute-done((bf16[2,96,576]{2,1,0:T(8,128)(2,1)S(1)}, bf16[2,96,576]{2,1,0:T(8,128)(2,1)}, u32[]{:S(2)}, u32[]{:S(2)}) %collective-permute-start.5) | collective-permute-done | bytes 221216 | tf_op jit(solution)/shard_map/ppermute | solution.py:339
  49.4 1.2 collective-permute-done.10.refs_12_
  51.4 6.3 %shard_map.296 = (bf16[256,768]{1,0:T(8,128)(2,1)}, bf16[256,576]{1,0:T(8,128)(2,1)}, bf16[256,576]{1,0:T(8,128)(2,1)}, bf16[256,576]{1,0:T(8,128)(2,1)}, bf16[256,576]{1,0:T(8,128)(2,1)}) custom-call(s32[2]{0:T(128)} %pad_add_fusion.meta, bf16[256,768]{1,0:T(8,128)(2,1)} %bitcast.79, bf16[48,64]{1,0:T(8,128)(2,1)} %pad_maximum_fusion.1.refs_0_, ...), custom_call_target="tpu_custom_call" | custom-call | flops 905969664 | bytes 5529608 | tf_op jit(solution)/shard_map/pallas_call | solution.py:784
  57.7 2.5 all-gather.3.cloned.1.call-done
  60.1 1.5 collective-permute-start.16
  61.6 1.5 collective-permute-start.15
  63.7 1.2 collective-permute-start.13
  65.0 2.5 collective-permute-start.14
  67.5 9.8 %collective-permute-done.12.refs_1_ = bf16[256,576]{1,0:T(8,128)(2,1)S(1)} collective-permute-done((bf16[256,576]{1,0:T(8,128)(2,1)}, bf16[256,576]{1,0:T(8,128)(2,1)S(1)}, u32[]{:S(2)}, u32[]{:S(2)}) %collective-permute-start.12) | collective-permute-done | bytes 294944 | tf_op jit(solution)/shard_map/ppermute | solution.py:339
  77.3 12.3 %collective-permute-done.13.refs_2_ = bf16[256,576]{1,0:T(8,128)(2,1)S(1)} collective-permute-done((bf16[256,576]{1,0:T(8,128)(2,1)}, bf16[256,576]{1,0:T(8,128)(2,1)S(1)}, u32[]{:S(2)}, u32[]{:S(2)}) %collective-permute-start.13) | collective-permute-done | bytes 294944 | tf_op jit(solution)/shard_map/ppermute | solution.py:339
  89.6 2.0 collective-permute-done.16.refs_10_
  91.6 1.2 collective-permute-done.15.refs_9_
  93.8 1.5 collective-permute-start.18
  96.0 12.4 %shard_map.297 = (bf16[256,192]{1,0:T(8,128)(2,1)}, bf16[256,192]{1,0:T(8,128)(2,1)}, bf16[256,192]{1,0:T(8,128)(2,1)}, bf16[256,192]{1,0:T(8,128)(2,1)}) custom-call(s32[2]{0:T(128)} %pad_add_fusion.meta, bf16[256,576]{1,0:T(8,128)(2,1)} %get-tuple-element.114.refs_0_, bf16[256,576]{1,0:T(8,128)(2,1)} %copy-done.43, bf16[256,576]{1,0:T(8,128)(2,1)} %copy-done.44, ...), custom_call_target="tpu_custom_call" | custom-call | flops 805306368 | bytes 1572872 | tf_op jit(solution)/shard_map/pallas_call | solution.py:784
  108.4 1.9 collective-permute-start.22
  111.3 1.6 collective-permute-start.24
  112.9 2.1 collective-permute-done.22.refs_5_
  115.0 7.7 %collective-permute-done.23.refs_6_ = bf16[256,192]{1,0:T(8,128)(2,1)S(1)} collective-permute-done((bf16[256,192]{1,0:T(8,128)(2,1)}, bf16[256,192]{1,0:T(8,128)(2,1)S(1)}, u32[]{:S(2)}, u32[]{:S(2)}) %collective-permute-start.23) | collective-permute-done | bytes 98336 | tf_op jit(solution)/shard_map/ppermute | solution.py:339
  123.3 2.0 collective-permute-done.25.refs_16_
  126.7 17.7 %shard_map.298 = (bf16[256,768]{1,0:T(8,128)(2,1)}, bf16[9,256,768]{2,1,0:T(8,128)(2,1)}, bf16[4,256,384]{2,1,0:T(8,128)(2,1)}, bf16[4,256,384]{2,1,0:T(8,128)(2...) custom-call(s32[2]{0:T(128)} %pad_add_fusion.meta, ...), custom_call_target="tpu_custom_call" | custom-call | flops 5435817984 | bytes 19329032 | tf_op jit(solution)/shard_map/pallas_call | solution.py:784
  145.0 2.4 collective-permute-start.29
  148.2 1.5 collective-permute-start.31
  149.7 2.3 collective-permute-done.28.refs_1_
  153.0 1.2 copy-done.1
  154.1 10.1 %shard_map.299 = (bf16[2,2,96,1792]{3,2,1,0:T(8,128)(2,1)}, bf16[2,2,96,1792]{3,2,1,0:T(8,128)(2,1)}, bf16[2,2,96,1792]{3,2,1,0:T(8,128)(2,1)}, bf16[2,2,96,1792]{3,2,1,0:T(8,128)(2,1)}) custom-call(s32[2]{0:T(128)} %pad_add_fusion.meta, bf16[4,256,384]{2,1,0:T(8,128)(2,1)} %get-tuple-element.137.refs_0_, bf16[4,256,384]{2,1,0:T(8,128)(2,1)} %copy-done.39, ...), custom_call_target="tpu_custom_call" | custom-call | flops 2717908992 | bytes 14155784 | tf_op jit(solution)/shard_map/pallas_call | solution.py:784
  164.3 1.5 collective-permute-start.32
  165.8 1.5 collective-permute-start.33
  167.3 15.9 %shard_map.300 = (bf16[256,576]{1,0:T(8,128)(2,1)}, bf16[256,576]{1,0:T(8,128)(2,1)}, bf16[256,576]{1,0:T(8,128)(2,1)}, bf16[256,576]{1,0:T(8,128)(2,1)}) custom-call(s32[2]{0:T(128)} %pad_add_fusion.meta, bf16[256,576]{1,0:T(8,128)(2,1)} %get-tuple-element.114.refs_0_, bf16[256,576]{1,0:T(8,128)(2,1)} %copy-done.43, bf16[256,576]{1,0:T(8,128)(2,1)} %copy-done.44, ...), custom_call_target="tpu_custom_call" | custom-call | flops 2013265920 | bytes 2752520 | tf_op jit(solution)/shard_map/pallas_call | solution.py:784
  183.2 2.3 collective-permute-start.34
  186.4 1.5 collective-permute-start.36
  187.9 11.3 %collective-permute-done.34.refs_3_ = bf16[256,576]{1,0:T(8,128)(2,1)S(1)} collective-permute-done((bf16[256,576]{1,0:T(8,128)(2,1)}, bf16[256,576]{1,0:T(8,128)(2,1)S(1)}, u32[]{:S(2)}, u32[]{:S(2)}) %collective-permute-start.34) | collective-permute-done | bytes 294944 | tf_op jit(solution)/shard_map/ppermute | solution.py:339
  199.2 12.1 %collective-permute-done.35.refs_4_ = bf16[256,576]{1,0:T(8,128)(2,1)S(1)} collective-permute-done((bf16[256,576]{1,0:T(8,128)(2,1)}, bf16[256,576]{1,0:T(8,128)(2,1)S(1)}, u32[]{:S(2)}, u32[]{:S(2)}) %collective-permute-start.35) | collective-permute-done | bytes 294944 | tf_op jit(solution)/shard_map/ppermute | solution.py:339
  213.0 2.8 convert_add_fusion
  217.6 6.4 %shard_map.301 = (bf16[2,2,96,576]{3,2,1,0:T(8,128)(2,1)}, bf16[2,2,96,576]{3,2,1,0:T(8,128)(2,1)}, bf16[2,2,96,576]{3,2,1,0:T(8,128)(2,1)}, bf16[2,2,96,576]{3,...) custom-call(s32[2]{0:T(128)} %pad_add_fusion.meta, ...), custom_call_target="tpu_custom_call" | custom-call | flops 905969664 | bytes 12395528 | tf_op jit(solution)/shard_map/pallas_call | solution.py:784
  224.0 1.5 collective-permute-start.43
  225.5 1.2 collective-permute-start.44
  226.7 6.9 %shard_map.302 = (f32[256,768]{1,0:T(8,128)}, f32[16,192]{1,0:T(8,128)}, f32[16,192]{1,0:T(8,128)}, f32[16,192]{1,0:T(8,128)}, f32[16,192]{1,0:T(8,128)}) custom-call(s32[2]{0:T(128)} %pad_add_fusion.meta, bf16[256,768]{1,0:T(8,128)(2,1)} %bitcast.81, f32[256,768]{1,0:T(8,128)} %get-tuple-element.135.dmid_ref, ...), custom_call_target="tpu_custom_call" | custom-call | flops 905969664 | bytes 6804488 | tf_op jit(solution)/shard_map/pallas_call | solution.py:784
  233.6 6.0 %collective-permute-start.52 = (f32[16,192]{1,0:T(8,128)}, f32[16,192]{1,0:T(8,128)S(1)}, u32[]{:S(2)}, u32[]{:S(2)}) collective-permute-start(f32[16,192]{1,0:T(8,128)} %get-tuple-element.188), channel_id=1, source_target_pairs={{0,1},{1,0},{2,3},{3,2},{4,5},{5,4},{6,7},{7,6},{8,9},{9,8},{10,11... | collective-permute-start | bytes 36872 | tf_op jit(solution)/shard_map/ppermute | solution.py:339
  239.5 1.9 collective-permute-done.52
  241.5 2.9 collective-permute-start.53
  244.3 2.0 collective-permute-done.53
  246.3 2.3 collective-permute-start.54
  248.6 3.4 %collective-permute-done.54 = f32[16,192]{1,0:T(8,128)S(1)} collective-permute-done((f32[16,192]{1,0:T(8,128)}, f32[16,192]{1,0:T(8,128)S(1)}, u32[]{:S(2)}, u32[]{:S(2)}) %collective-permute-start.54) | collective-permute-done | bytes 12320 | tf_op jit(solution)/shard_map/ppermute | solution.py:339
  252.8 1.2 collective-permute-done.55
  254.8 2.9 collective-permute-done.56
  258.7 1.1 convert_add_fusion.3
  260.8 1.1 convert_add_fusion.2
  262.0 1.3 collective-permute-start.47
  264.3 2.5 collective-permute-done.45
  267.2 1.4 collective-permute-done.47
  268.7 1.3 collective-permute-start.48
  270.1 1.6 collective-permute-start.49
  271.6 27.8 %collective-permute-done.50 = bf16[2,96,1792]{2,1,0:T(8,128)(2,1)S(1)} collective-permute-done((bf16[2,96,1792]{2,1,0:T(8,128)(2,1)S(1)}, bf16[2,96,1792]{2,1,0:T(8,128)(2,1)S(1)}, u32[]{:S(2)}, u32[]{:S(2)}) %collective-permute-start.50) | collective-permute-done | bytes 688160 | tf_op jit(solution)/shard_map/ppermute | solution.py:339
  299.5 1.3 fusion.3
  303.2 7.6 %collective-permute-done.51 = bf16[96,1792]{1,0:T(8,128)(2,1)S(1)} collective-permute-done((bf16[96,1792]{1,0:T(8,128)(2,1)S(1)}, bf16[96,1792]{1,0:T(8,128)(2,1)S(1)}, u32[]{:S(2)}, u32[]{:S(2)}) %collective-permute-start.51) | collective-permute-done | bytes 344096 | tf_op jit(solution)/shard_map/ppermute | solution.py:339
  (215 shorter events, 31.3 us)
Async XLA Ops:
  7.2 52.9 %all-gather.3.cloned.1.call-start = ((), (), s32[]{:S(2)}) async-start(), calls=%async_computation | async-start | bytes 1720320 | tf_op jit(solution)/shard_map/all_gather | solution.py:848
  9.2 9.3 %collective-permute-start.2 = (bf16[96,640]{1,0:T(8,128)(2,1)S(1)}, bf16[96,640]{1,0:T(8,128)(2,1)S(1)}, u32[]{:S(2)}, u32[]{:S(2)}) collective-permute-start(bf16[96,640]{1,0:T(8,128)(2,1)S(1)} %maximum_maximum_fusion), channel_id=1, source_target_pairs={{0,3},{1,2},{2,1},{3,0},{4,7},{5,6},{6,5},{7,4},{8,11},{9,10},{10,... | collective-permute-start | bytes 368648 | tf_op jit(solution)/shard_map/ppermute | solution.py:339
  14.3 10.4 %collective-permute-start.1 = (bf16[96,640]{1,0:T(8,128)(2,1)S(1)}, bf16[96,640]{1,0:T(8,128)(2,1)S(1)}, u32[]{:S(2)}, u32[]{:S(2)}) collective-permute-start(bf16[96,640]{1,0:T(8,128)(2,1)S(1)} %maximum_maximum_fusion), channel_id=1, source_target_pairs={{0,2},{1,3},{2,0},{3,1},{4,6},{5,7},{6,4},{7,5},{8,10},{9,11},{10,... | collective-permute-start | bytes 368648 | tf_op jit(solution)/shard_map/ppermute | solution.py:339
  14.3 11.0 %collective-permute-start = (bf16[96,640]{1,0:T(8,128)(2,1)S(1)}, bf16[96,640]{1,0:T(8,128)(2,1)S(1)}, u32[]{:S(2)}, u32[]{:S(2)}) collective-permute-start(bf16[96,640]{1,0:T(8,128)(2,1)S(1)} %maximum_maximum_fusion), channel_id=1, source_target_pairs={{0,1},{1,0},{2,3},{3,2},{4,5},{5,4},{6,7},{7,6},{8,9},{9,8},{10,11... | collective-permute-start | bytes 368648 | tf_op jit(solution)/shard_map/ppermute | solution.py:339
  26.2 12.3 %collective-permute-start.4 = (bf16[4,96,576]{2,1,0:T(8,128)(2,1)S(1)}, bf16[4,96,576]{2,1,0:T(8,128)(2,1)S(1)}, u32[]{:S(2)}, u32[]{:S(2)}) collective-permute-start(bf16[4,96,576]{2,1,0:T(8,128)(2,1)S(1)} %pad_maximum_fusion.refs_4_), channel_id=1, source_target_pairs={{0,16},{4,20},{8,24},{12,28},{16,0},{20,4},{24,8},{28,12},{1,17},{... | collective-permute-start | bytes 1327112 | tf_op jit(solution)/shard_map/ppermute | solution.py:339
  27.8 12.3 %collective-permute-start.3 = (bf16[4,96,576]{2,1,0:T(8,128)(2,1)S(1)}, bf16[4,96,576]{2,1,0:T(8,128)(2,1)S(1)}, u32[]{:S(2)}, u32[]{:S(2)}) collective-permute-start(bf16[4,96,576]{2,1,0:T(8,128)(2,1)S(1)} %pad_maximum_fusion.refs_4_), channel_id=1, source_target_pairs={{0,8},{4,12},{8,0},{12,4},{16,24},{20,28},{24,16},{28,20},{1,9},{5... | collective-permute-start | bytes 1327112 | tf_op jit(solution)/shard_map/ppermute | solution.py:339
  29.3 20.1 %collective-permute-start.7 = (bf16[4,96,576]{2,1,0:T(8,128)(2,1)S(1)}, bf16[4,96,576]{2,1,0:T(8,128)(2,1)S(1)}, u32[]{:S(2)}, u32[]{:S(2)}) collective-permute-start(bf16[4,96,576]{2,1,0:T(8,128)(2,1)S(1)} %pad_maximum_fusion.refs_4_), channel_id=1, source_target_pairs={{0,4},{4,0},{8,12},{12,8},{16,20},{20,16},{24,28},{28,24},{1,5},{5... | collective-permute-start | bytes 1327112 | tf_op jit(solution)/shard_map/ppermute | solution.py:339
  38.6 6.6 %collective-permute-start.6 = (bf16[2,96,576]{2,1,0:T(8,128)(2,1)S(1)}, bf16[2,96,576]{2,1,0:T(8,128)(2,1)}, u32[]{:S(2)}, u32[]{:S(2)}) collective-permute-start(bf16[2,96,576]{2,1,0:T(8,128)(2,1)S(1)} %slice.155), channel_id=1, source_target_pairs={{0,8},{4,12},{8,0},{12,4},{16,24},{20,28},{24,16},{28,20},{1,9},{5... | collective-permute-start | bytes 663560 | tf_op jit(solution)/shard_map/ppermute | solution.py:339
  40.2 9.3 %collective-permute-start.9 = (bf16[4,96,576]{2,1,0:T(8,128)(2,1)S(1)}, bf16[4,96,576]{2,1,0:T(8,128)(2,1)S(1)}, u32[]{:S(2)}, u32[]{:S(2)}) collective-permute-start(bf16[4,96,576]{2,1,0:T(8,128)(2,1)S(1)} %collective-permute-done.4.refs_6_), channel_id=1, source_target_pairs={{0,4},{4,0},{8,12},{12,8},{16,20},{20,16},{24,28},{28,24},{1,5},{5... | collective-permute-start | bytes 1327112 | tf_op jit(solution)/shard_map/ppermute | solution.py:339
  40.2 8.5 %collective-permute-start.5 = (bf16[2,96,576]{2,1,0:T(8,128)(2,1)S(1)}, bf16[2,96,576]{2,1,0:T(8,128)(2,1)}, u32[]{:S(2)}, u32[]{:S(2)}) collective-permute-start(bf16[2,96,576]{2,1,0:T(8,128)(2,1)S(1)} %slice.154), channel_id=1, source_target_pairs={{0,16},{4,20},{8,24},{12,28},{16,0},{20,4},{24,8},{28,12},{1,17},{... | collective-permute-start | bytes 663560 | tf_op jit(solution)/shard_map/ppermute | solution.py:339
  41.8 8.8 %collective-permute-start.8 = (bf16[4,96,576]{2,1,0:T(8,128)(2,1)S(1)}, bf16[4,96,576]{2,1,0:T(8,128)(2,1)S(1)}, u32[]{:S(2)}, u32[]{:S(2)}) collective-permute-start(bf16[4,96,576]{2,1,0:T(8,128)(2,1)S(1)} %collective-permute-done.3.refs_5_), channel_id=1, source_target_pairs={{0,4},{4,0},{8,12},{12,8},{16,20},{20,16},{24,28},{28,24},{1,5},{5... | collective-permute-start | bytes 1327112 | tf_op jit(solution)/shard_map/ppermute | solution.py:339
  45.2 4.2 %collective-permute-start.11 = (bf16[2,96,576]{2,1,0:T(8,128)(2,1)}, bf16[2,96,576]{2,1,0:T(8,128)(2,1)}, u32[]{:S(2)}, u32[]{:S(2)}) collective-permute-start(bf16[2,96,576]{2,1,0:T(8,128)(2,1)} %collective-permute-done.6.refs_8_), channel_id=1, source_target_pairs={{0,4},{4,0},{8,12},{12,8},{16,20},{20,16},{24,28},{28,24},{1,5},{5... | collective-permute-start | bytes 663560 | tf_op jit(solution)/shard_map/ppermute | solution.py:339
  48.7 1.9 collective-permute-start.10
  60.1 31.4 %collective-permute-start.16 = (bf16[4,96,1792]{2,1,0:T(8,128)(2,1)}, bf16[4,96,1792]{2,1,0:T(8,128)(2,1)S(1)}, u32[]{:S(2)}, u32[]{:S(2)}) collective-permute-start(bf16[4,96,1792]{2,1,0:T(8,128)(2,1)} %bitcast.82), channel_id=1, source_target_pairs={{0,16},{4,20},{8,24},{12,28},{16,0},{20,4},{24,8},{28,12},{1,17},{... | collective-permute-start | bytes 4128776 | tf_op jit(solution)/shard_map/ppermute | solution.py:339
  61.6 31.1 %collective-permute-start.15 = (bf16[4,96,1792]{2,1,0:T(8,128)(2,1)}, bf16[4,96,1792]{2,1,0:T(8,128)(2,1)S(1)}, u32[]{:S(2)}, u32[]{:S(2)}) collective-permute-start(bf16[4,96,1792]{2,1,0:T(8,128)(2,1)} %bitcast.83), channel_id=1, source_target_pairs={{0,8},{4,12},{8,0},{12,4},{16,24},{20,28},{24,16},{28,20},{1,9},{5... | collective-permute-start | bytes 4128776 | tf_op jit(solution)/shard_map/ppermute | solution.py:339
  63.1 14.2 %collective-permute-start.12 = (bf16[256,576]{1,0:T(8,128)(2,1)}, bf16[256,576]{1,0:T(8,128)(2,1)S(1)}, u32[]{:S(2)}, u32[]{:S(2)}) collective-permute-start(bf16[256,576]{1,0:T(8,128)(2,1)} %get-tuple-element.108), channel_id=1, source_target_pairs={{0,1},{1,0},{2,3},{3,2},{4,5},{5,4},{6,7},{7,6},{8,9},{9,8},{10,11... | collective-permute-start | bytes 884744 | tf_op jit(solution)/shard_map/ppermute | solution.py:339
  63.7 25.8 %collective-permute-start.13 = (bf16[256,576]{1,0:T(8,128)(2,1)}, bf16[256,576]{1,0:T(8,128)(2,1)S(1)}, u32[]{:S(2)}, u32[]{:S(2)}) collective-permute-start(bf16[256,576]{1,0:T(8,128)(2,1)} %get-tuple-element.109), channel_id=1, source_target_pairs={{0,2},{1,3},{2,0},{3,1},{4,6},{5,7},{6,4},{7,5},{8,10},{9,11},{10,... | collective-permute-start | bytes 884744 | tf_op jit(solution)/shard_map/ppermute | solution.py:339
  65.0 24.6 %collective-permute-start.14 = (bf16[256,576]{1,0:T(8,128)(2,1)}, bf16[256,576]{1,0:T(8,128)(2,1)S(1)}, u32[]{:S(2)}, u32[]{:S(2)}) collective-permute-start(bf16[256,576]{1,0:T(8,128)(2,1)} %get-tuple-element.110), channel_id=1, source_target_pairs={{0,3},{1,2},{2,1},{3,0},{4,7},{5,6},{6,5},{7,4},{8,11},{9,10},{10,... | collective-permute-start | bytes 884744 | tf_op jit(solution)/shard_map/ppermute | solution.py:339
  77.3 31.1 %collective-permute-start.19 = (bf16[4,96,1792]{2,1,0:T(8,128)(2,1)}, bf16[4,96,1792]{2,1,0:T(8,128)(2,1)S(1)}, u32[]{:S(2)}, u32[]{:S(2)}) collective-permute-start(bf16[4,96,1792]{2,1,0:T(8,128)(2,1)} %bitcast.84), channel_id=1, source_target_pairs={{0,4},{4,0},{8,12},{12,8},{16,20},{20,16},{24,28},{28,24},{1,5},{5... | collective-permute-start | bytes 4128776 | tf_op jit(solution)/shard_map/ppermute | solution.py:339
  92.8 15.6 %collective-permute-start.20 = (bf16[4,96,1792]{2,1,0:T(8,128)(2,1)S(1)}, bf16[4,96,1792]{2,1,0:T(8,128)(2,1)S(1)}, u32[]{:S(2)}, u32[]{:S(2)}) collective-permute-start(bf16[4,96,1792]{2,1,0:T(8,128)(2,1)S(1)} %collective-permute-done.15.refs_9_), channel_id=1, source_target_pairs={{0,4},{4,0},{8,12},{12,8},{16,20},{20,16},{24,28},{28,24},{1,5},{5... | collective-permute-start | bytes 4128776 | tf_op jit(solution)/shard_map/ppermute | solution.py:339
  92.8 15.7 %collective-permute-start.21 = (bf16[4,96,1792]{2,1,0:T(8,128)(2,1)S(1)}, bf16[4,96,1792]{2,1,0:T(8,128)(2,1)}, u32[]{:S(2)}, u32[]{:S(2)}) collective-permute-start(bf16[4,96,1792]{2,1,0:T(8,128)(2,1)S(1)} %collective-permute-done.16.refs_10_), channel_id=1, source_target_pairs={{0,4},{4,0},{8,12},{12,8},{16,20},{20,16},{24,28},{28,24},{1,5},{5... | collective-permute-start | bytes 4128776 | tf_op jit(solution)/shard_map/ppermute | solution.py:339
  93.8 19.1 %collective-permute-start.18 = (bf16[2,96,1792]{2,1,0:T(8,128)(2,1)S(1)}, bf16[2,96,1792]{2,1,0:T(8,128)(2,1)S(1)}, u32[]{:S(2)}, u32[]{:S(2)}) collective-permute-start(bf16[2,96,1792]{2,1,0:T(8,128)(2,1)S(1)} %slice.126), channel_id=1, source_target_pairs={{0,8},{4,12},{8,0},{12,4},{16,24},{20,28},{24,16},{28,20},{1,9},{5... | collective-permute-start | bytes 2064392 | tf_op jit(solution)/shard_map/ppermute | solution.py:339
  95.3 17.6 %collective-permute-start.17 = (bf16[2,96,1792]{2,1,0:T(8,128)(2,1)S(1)}, bf16[2,96,1792]{2,1,0:T(8,128)(2,1)}, u32[]{:S(2)}, u32[]{:S(2)}) collective-permute-start(bf16[2,96,1792]{2,1,0:T(8,128)(2,1)S(1)} %slice.125), channel_id=1, source_target_pairs={{0,16},{4,20},{8,24},{12,28},{16,0},{20,4},{24,8},{28,12},{1,17},{... | collective-permute-start | bytes 2064392 | tf_op jit(solution)/shard_map/ppermute | solution.py:339
  108.4 6.6 %collective-permute-start.22 = (bf16[256,192]{1,0:T(8,128)(2,1)}, bf16[256,192]{1,0:T(8,128)(2,1)S(1)}, u32[]{:S(2)}, u32[]{:S(2)}) collective-permute-start(bf16[256,192]{1,0:T(8,128)(2,1)} %get-tuple-element.122), channel_id=1, source_target_pairs={{0,1},{1,0},{2,3},{3,2},{4,5},{5,4},{6,7},{7,6},{8,9},{9,8},{10,11... | collective-permute-start | bytes 294920 | tf_op jit(solution)/shard_map/ppermute | solution.py:339
  110.3 12.4 %collective-permute-start.23 = (bf16[256,192]{1,0:T(8,128)(2,1)}, bf16[256,192]{1,0:T(8,128)(2,1)S(1)}, u32[]{:S(2)}, u32[]{:S(2)}) collective-permute-start(bf16[256,192]{1,0:T(8,128)(2,1)} %get-tuple-element.123), channel_id=1, source_target_pairs={{0,2},{1,3},{2,0},{3,1},{4,6},{5,7},{6,4},{7,5},{8,10},{9,11},{10,... | collective-permute-start | bytes 294920 | tf_op jit(solution)/shard_map/ppermute | solution.py:339
  111.3 11.4 %collective-permute-start.24 = (bf16[256,192]{1,0:T(8,128)(2,1)}, bf16[256,192]{1,0:T(8,128)(2,1)S(1)}, u32[]{:S(2)}, u32[]{:S(2)}) collective-permute-start(bf16[256,192]{1,0:T(8,128)(2,1)} %get-tuple-element.124), channel_id=1, source_target_pairs={{0,3},{1,2},{2,1},{3,0},{4,7},{5,6},{6,5},{7,4},{8,11},{9,10},{10,... | collective-permute-start | bytes 294920 | tf_op jit(solution)/shard_map/ppermute | solution.py:339
  122.7 2.6 collective-permute-start.25
  122.8 3.1 collective-permute-start.26
  144.4 7.6 %collective-permute-start.27 = (bf16[9,256,768]{2,1,0:T(8,128)(2,1)}, bf16[9,256,768]{2,1,0:T(8,128)(2,1)S(1)}, u32[]{:S(2)}, u32[]{:S(2)}) collective-permute-start(bf16[9,256,768]{2,1,0:T(8,128)(2,1)} %get-tuple-element.136.refs_2_.refs_0_), channel_id=1, source_target_pairs={{0,4},{4,0},{8,12},{12,8},{16,20},{20,16},{24,28},{28,24},{1,5},{5... | collective-permute-start | bytes 10616840 | tf_op jit(solution)/shard_map/ppermute | solution.py:339
  144.6 7.4 %collective-permute-start.28 = (bf16[4,256,384]{2,1,0:T(8,128)(2,1)}, bf16[4,256,384]{2,1,0:T(8,128)(2,1)S(1)}, u32[]{:S(2)}, u32[]{:S(2)}) collective-permute-start(bf16[4,256,384]{2,1,0:T(8,128)(2,1)} %get-tuple-element.138), channel_id=1, source_target_pairs={{0,4},{4,0},{8,12},{12,8},{16,20},{20,16},{24,28},{28,24},{1,5},{5... | collective-permute-start | bytes 2359304 | tf_op jit(solution)/shard_map/ppermute | solution.py:339
  145.0 19.2 %collective-permute-start.29 = (bf16[256,192]{1,0:T(8,128)(2,1)}, bf16[256,192]{1,0:T(8,128)(2,1)S(1)}, u32[]{:S(2)}, u32[]{:S(2)}) collective-permute-start(bf16[256,192]{1,0:T(8,128)(2,1)} %get-tuple-element.144), channel_id=1, source_target_pairs={{0,1},{1,0},{2,3},{3,2},{4,5},{5,4},{6,7},{7,6},{8,9},{9,8},{10,11... | collective-permute-start | bytes 294920 | tf_op jit(solution)/shard_map/ppermute | solution.py:339
  147.4 16.9 %collective-permute-start.30 = (bf16[256,192]{1,0:T(8,128)(2,1)}, bf16[256,192]{1,0:T(8,128)(2,1)S(1)}, u32[]{:S(2)}, u32[]{:S(2)}) collective-permute-start(bf16[256,192]{1,0:T(8,128)(2,1)} %get-tuple-element.145), channel_id=1, source_target_pairs={{0,2},{1,3},{2,0},{3,1},{4,6},{5,7},{6,4},{7,5},{8,10},{9,11},{10,... | collective-permute-start | bytes 294920 | tf_op jit(solution)/shard_map/ppermute | solution.py:339
  148.2 16.0 %collective-permute-start.31 = (bf16[256,192]{1,0:T(8,128)(2,1)}, bf16[256,192]{1,0:T(8,128)(2,1)S(1)}, u32[]{:S(2)}, u32[]{:S(2)}) collective-permute-start(bf16[256,192]{1,0:T(8,128)(2,1)} %get-tuple-element.146), channel_id=1, source_target_pairs={{0,3},{1,2},{2,1},{3,0},{4,7},{5,6},{6,5},{7,4},{8,11},{9,10},{10,... | collective-permute-start | bytes 294920 | tf_op jit(solution)/shard_map/ppermute | solution.py:339
  164.3 48.7 %copy-start.8 = (bf16[2,2,96,1792]{3,2,1,0:T(8,128)(2,1)S(1)}, bf16[2,2,96,1792]{3,2,1,0:T(8,128)(2,1)}, u32[]{:S(2)}) copy-start(bf16[2,2,96,1792]{3,2,1,0:T(8,128)(2,1)} %get-tuple-element.160) | copy-start | bytes 4128772
  164.3 47.1 %collective-permute-start.32 = (bf16[2,2,96,1792]{3,2,1,0:T(8,128)(2,1)}, bf16[2,2,96,1792]{3,2,1,0:T(8,128)(2,1)S(1)}, u32[]{:S(2)}, u32[]{:S(2)}) collective-permute-start(bf16[2,2,96,1792]{3,2,1,0:T(8,128)(2,1)} %get-tuple-element.152), channel_id=1, source_target_pairs={{0,16},{4,20},{8,24},{12,28},{16,0},{20,4},{24,8},{28,12},{1,17},{... | collective-permute-start | bytes 4128776 | tf_op jit(solution)/shard_map/ppermute | solution.py:339
  165.8 45.6 %collective-permute-start.33 = (bf16[2,2,96,1792]{3,2,1,0:T(8,128)(2,1)}, bf16[2,2,96,1792]{3,2,1,0:T(8,128)(2,1)S(1)}, u32[]{:S(2)}, u32[]{:S(2)}) collective-permute-start(bf16[2,2,96,1792]{3,2,1,0:T(8,128)(2,1)} %get-tuple-element.153), channel_id=1, source_target_pairs={{0,8},{4,12},{8,0},{12,4},{16,24},{20,28},{24,16},{28,20},{1,9},{5... | collective-permute-start | bytes 4128776 | tf_op jit(solution)/shard_map/ppermute | solution.py:339
  183.2 16.0 %collective-permute-start.34 = (bf16[256,576]{1,0:T(8,128)(2,1)}, bf16[256,576]{1,0:T(8,128)(2,1)S(1)}, u32[]{:S(2)}, u32[]{:S(2)}) collective-permute-start(bf16[256,576]{1,0:T(8,128)(2,1)} %get-tuple-element.154), channel_id=1, source_target_pairs={{0,1},{1,0},{2,3},{3,2},{4,5},{5,4},{6,7},{7,6},{8,9},{9,8},{10,11... | collective-permute-start | bytes 884744 | tf_op jit(solution)/shard_map/ppermute | solution.py:339
  185.5 25.8 %collective-permute-start.35 = (bf16[256,576]{1,0:T(8,128)(2,1)}, bf16[256,576]{1,0:T(8,128)(2,1)S(1)}, u32[]{:S(2)}, u32[]{:S(2)}) collective-permute-start(bf16[256,576]{1,0:T(8,128)(2,1)} %get-tuple-element.155), channel_id=1, source_target_pairs={{0,2},{1,3},{2,0},{3,1},{4,6},{5,7},{6,4},{7,5},{8,10},{9,11},{10,... | collective-permute-start | bytes 884744 | tf_op jit(solution)/shard_map/ppermute | solution.py:339
  186.4 24.9 %collective-permute-start.36 = (bf16[256,576]{1,0:T(8,128)(2,1)}, bf16[256,576]{1,0:T(8,128)(2,1)S(1)}, u32[]{:S(2)}, u32[]{:S(2)}) collective-permute-start(bf16[256,576]{1,0:T(8,128)(2,1)} %get-tuple-element.156), channel_id=1, source_target_pairs={{0,3},{1,2},{2,1},{3,0},{4,7},{5,6},{6,5},{7,4},{8,11},{9,10},{10,... | collective-permute-start | bytes 884744 | tf_op jit(solution)/shard_map/ppermute | solution.py:339
  199.2 16.7 %collective-permute-start.37 = (bf16[256,576]{1,0:T(8,128)(2,1)}, bf16[256,576]{1,0:T(8,128)(2,1)S(1)}, u32[]{:S(2)}, u32[]{:S(2)}) collective-permute-start(bf16[256,576]{1,0:T(8,128)(2,1)} %get-tuple-element.151.refs_2_), channel_id=1, source_target_pairs={{0,4},{4,0},{8,12},{12,8},{16,20},{20,16},{24,28},{28,24},{1,5},{5... | collective-permute-start | bytes 884744 | tf_op jit(solution)/shard_map/ppermute | solution.py:339
  211.4 4.6 %collective-permute-start.38 = (bf16[256,576]{1,0:T(8,128)(2,1)S(1)}, bf16[256,576]{1,0:T(8,128)(2,1)S(1)}, u32[]{:S(2)}, u32[]{:S(2)}) collective-permute-start(bf16[256,576]{1,0:T(8,128)(2,1)S(1)} %collective-permute-done.34.refs_3_), channel_id=1, source_target_pairs={{0,4},{4,0},{8,12},{12,8},{16,20},{20,16},{24,28},{28,24},{1,5},{5... | collective-permute-start | bytes 884744 | tf_op jit(solution)/shard_map/ppermute | solution.py:339
  211.5 4.5 %collective-permute-start.39 = (bf16[256,576]{1,0:T(8,128)(2,1)S(1)}, bf16[256,576]{1,0:T(8,128)(2,1)S(1)}, u32[]{:S(2)}, u32[]{:S(2)}) collective-permute-start(bf16[256,576]{1,0:T(8,128)(2,1)S(1)} %collective-permute-done.35.refs_4_), channel_id=1, source_target_pairs={{0,4},{4,0},{8,12},{12,8},{16,20},{20,16},{24,28},{28,24},{1,5},{5... | collective-permute-start | bytes 884744 | tf_op jit(solution)/shard_map/ppermute | solution.py:339
  213.0 3.0 collective-permute-start.40
  216.0 42.3 %collective-permute-start.41 = (bf16[2,96,1792]{2,1,0:T(8,128)(2,1)S(1)}, bf16[2,96,1792]{2,1,0:T(8,128)(2,1)}, u32[]{:S(2)}, u32[]{:S(2)}) collective-permute-start(bf16[2,96,1792]{2,1,0:T(8,128)(2,1)S(1)} %fusion.4), channel_id=1, source_target_pairs={{0,8},{4,12},{8,0},{12,4},{16,24},{20,28},{24,16},{28,20},{1,9},{5... | collective-permute-start | bytes 2064392 | tf_op jit(solution)/shard_map/ppermute | solution.py:339
  217.0 41.3 %collective-permute-start.42 = (bf16[2,96,1792]{2,1,0:T(8,128)(2,1)S(1)}, bf16[2,96,1792]{2,1,0:T(8,128)(2,1)S(1)}, u32[]{:S(2)}, u32[]{:S(2)}) collective-permute-start(bf16[2,96,1792]{2,1,0:T(8,128)(2,1)S(1)} %fusion.5), channel_id=1, source_target_pairs={{0,16},{4,20},{8,24},{12,28},{16,0},{20,4},{24,8},{28,12},{1,17},{... | collective-permute-start | bytes 2064392 | tf_op jit(solution)/shard_map/ppermute | solution.py:339
  224.0 34.3 %collective-permute-start.43 = (bf16[2,2,96,576]{3,2,1,0:T(8,128)(2,1)}, bf16[2,2,96,576]{3,2,1,0:T(8,128)(2,1)}, u32[]{:S(2)}, u32[]{:S(2)}) collective-permute-start(bf16[2,2,96,576]{3,2,1,0:T(8,128)(2,1)} %get-tuple-element.180), channel_id=1, source_target_pairs={{0,16},{4,20},{8,24},{12,28},{16,0},{20,4},{24,8},{28,12},{1,17},{... | collective-permute-start | bytes 1327112 | tf_op jit(solution)/shard_map/ppermute | solution.py:339
  225.5 32.8 %collective-permute-start.44 = (bf16[2,2,96,576]{3,2,1,0:T(8,128)(2,1)}, bf16[2,2,96,576]{3,2,1,0:T(8,128)(2,1)}, u32[]{:S(2)}, u32[]{:S(2)}) collective-permute-start(bf16[2,2,96,576]{3,2,1,0:T(8,128)(2,1)} %get-tuple-element.181), channel_id=1, source_target_pairs={{0,8},{4,12},{8,0},{12,4},{16,24},{20,28},{24,16},{28,20},{1,9},{5... | collective-permute-start | bytes 1327112 | tf_op jit(solution)/shard_map/ppermute | solution.py:339
  233.6 7.9 %collective-permute-start.52 = (f32[16,192]{1,0:T(8,128)}, f32[16,192]{1,0:T(8,128)S(1)}, u32[]{:S(2)}, u32[]{:S(2)}) collective-permute-start(f32[16,192]{1,0:T(8,128)} %get-tuple-element.188), channel_id=1, source_target_pairs={{0,1},{1,0},{2,3},{3,2},{4,5},{5,4},{6,7},{7,6},{8,9},{9,8},{10,11... | collective-permute-start | bytes 36872 | tf_op jit(solution)/shard_map/ppermute | solution.py:339
  241.5 4.8 %collective-permute-start.53 = (f32[16,192]{1,0:T(8,128)}, f32[16,192]{1,0:T(8,128)S(1)}, u32[]{:S(2)}, u32[]{:S(2)}) collective-permute-start(f32[16,192]{1,0:T(8,128)} %get-tuple-element.189), channel_id=1, source_target_pairs={{0,2},{1,3},{2,0},{3,1},{4,6},{5,7},{6,4},{7,5},{8,10},{9,11},{10,... | collective-permute-start | bytes 36872 | tf_op jit(solution)/shard_map/ppermute | solution.py:339
  246.3 5.7 %collective-permute-start.54 = (f32[16,192]{1,0:T(8,128)}, f32[16,192]{1,0:T(8,128)S(1)}, u32[]{:S(2)}, u32[]{:S(2)}) collective-permute-start(f32[16,192]{1,0:T(8,128)} %get-tuple-element.190), channel_id=1, source_target_pairs={{0,3},{1,2},{2,1},{3,0},{4,7},{5,6},{6,5},{7,4},{8,11},{9,10},{10,... | collective-permute-start | bytes 36872 | tf_op jit(solution)/shard_map/ppermute | solution.py:339
  252.8 1.2 collective-permute-start.55
  254.0 3.7 %collective-permute-start.56 = (f32[16,192]{1,0:T(8,128)S(1)}, f32[16,192]{1,0:T(8,128)S(1)}, u32[]{:S(2)}, u32[]{:S(2)}) collective-permute-start(f32[16,192]{1,0:T(8,128)S(1)} %add.170), channel_id=1, source_target_pairs={{0,8},{4,12},{8,0},{12,4},{16,24},{20,28},{24,16},{28,20},{1,9},{5... | collective-permute-start | bytes 36872 | tf_op jit(solution)/shard_map/ppermute | solution.py:339
  257.7 43.2 %collective-permute-start.57 = (f32[16,192]{1,0:T(8,128)S(1)}, f32[16,192]{1,0:T(8,128)S(1)}, u32[]{:S(2)}, u32[]{:S(2)}) collective-permute-start(f32[16,192]{1,0:T(8,128)S(1)} %add.171), channel_id=1, source_target_pairs={{0,16},{4,20},{8,24},{12,28},{16,0},{20,4},{24,8},{28,12},{1,17},{... | collective-permute-start | bytes 36872 | tf_op jit(solution)/shard_map/ppermute | solution.py:339
  259.9 6.9 %collective-permute-start.45 = (bf16[2,96,576]{2,1,0:T(8,128)(2,1)S(1)}, bf16[2,96,576]{2,1,0:T(8,128)(2,1)S(1)}, u32[]{:S(2)}, u32[]{:S(2)}) collective-permute-start(bf16[2,96,576]{2,1,0:T(8,128)(2,1)S(1)} %fusion.14), channel_id=1, source_target_pairs={{0,8},{4,12},{8,0},{12,4},{16,24},{20,28},{24,16},{28,20},{1,9},{5... | collective-permute-start | bytes 663560 | tf_op jit(solution)/shard_map/ppermute | solution.py:339
  262.0 6.7 %collective-permute-start.47 = (bf16[2,96,576]{2,1,0:T(8,128)(2,1)S(1)}, bf16[2,96,576]{2,1,0:T(8,128)(2,1)S(1)}, u32[]{:S(2)}, u32[]{:S(2)}) collective-permute-start(bf16[2,96,576]{2,1,0:T(8,128)(2,1)S(1)} %fusion.15), channel_id=1, source_target_pairs={{0,16},{4,20},{8,24},{12,28},{16,0},{20,4},{24,8},{28,12},{1,17},{... | collective-permute-start | bytes 663560 | tf_op jit(solution)/shard_map/ppermute | solution.py:339
  263.3 36.2 %collective-permute-start.50 = (bf16[2,96,1792]{2,1,0:T(8,128)(2,1)S(1)}, bf16[2,96,1792]{2,1,0:T(8,128)(2,1)S(1)}, u32[]{:S(2)}, u32[]{:S(2)}) collective-permute-start(bf16[2,96,1792]{2,1,0:T(8,128)(2,1)S(1)} %fusion.1), channel_id=1, source_target_pairs={{0,2},{1,3},{2,0},{3,1},{4,6},{5,7},{6,4},{7,5},{8,10},{9,11},{10,... | collective-permute-start | bytes 2064392 | tf_op jit(solution)/shard_map/ppermute | solution.py:339
  266.9 34.6 %collective-permute-start.46 = (bf16[96,576]{1,0:T(8,128)(2,1)S(1)}, bf16[96,576]{1,0:T(8,128)(2,1)S(1)}, u32[]{:S(2)}, u32[]{:S(2)}) collective-permute-start(bf16[96,576]{1,0:T(8,128)(2,1)S(1)} %fusion.18), channel_id=1, source_target_pairs={{0,1},{1,0},{2,3},{3,2},{4,5},{5,4},{6,7},{7,6},{8,9},{9,8},{10,11... | collective-permute-start | bytes 331784 | tf_op jit(solution)/shard_map/ppermute | solution.py:339
  268.7 33.4 %collective-permute-start.48 = (bf16[96,576]{1,0:T(8,128)(2,1)S(1)}, bf16[96,576]{1,0:T(8,128)(2,1)S(1)}, u32[]{:S(2)}, u32[]{:S(2)}) collective-permute-start(bf16[96,576]{1,0:T(8,128)(2,1)S(1)} %get-tuple-element.208), channel_id=1, source_target_pairs={{0,2},{1,3},{2,0},{3,1},{4,6},{5,7},{6,4},{7,5},{8,10},{9,11},{10,... | collective-permute-start | bytes 331784 | tf_op jit(solution)/shard_map/ppermute | solution.py:339
  270.0 30.9 %copy-start.35 = (f32[12,192]{1,0:T(8,128)S(1)}, f32[12,192]{1,0:T(8,128)}, u32[]{:S(2)}) copy-start(f32[12,192]{1,0:T(8,128)} %param.33) | copy-start | bytes 27652
  270.0 30.9 %copy-start.36 = (f32[12,192]{1,0:T(8,128)S(1)}, f32[12,192]{1,0:T(8,128)}, u32[]{:S(2)}) copy-start(f32[12,192]{1,0:T(8,128)} %param.32) | copy-start | bytes 27652
  270.0 32.1 %copy-start.30 = (f32[96,576]{1,0:T(8,128)S(1)}, f32[96,576]{1,0:T(8,128)}, u32[]{:S(2)}) copy-start(f32[96,576]{1,0:T(8,128)} %param.25) | copy-start | bytes 663556
  270.0 32.1 %copy-start.31 = (f32[96,576]{1,0:T(8,128)S(1)}, f32[96,576]{1,0:T(8,128)}, u32[]{:S(2)}) copy-start(f32[96,576]{1,0:T(8,128)} %param.24) | copy-start | bytes 663556
  270.1 32.0 %collective-permute-start.49 = (bf16[96,576]{1,0:T(8,128)(2,1)S(1)}, bf16[96,576]{1,0:T(8,128)(2,1)S(1)}, u32[]{:S(2)}, u32[]{:S(2)}) collective-permute-start(bf16[96,576]{1,0:T(8,128)(2,1)S(1)} %get-tuple-element.209), channel_id=1, source_target_pairs={{0,3},{1,2},{2,1},{3,0},{4,7},{5,6},{6,5},{7,4},{8,11},{9,10},{10,... | collective-permute-start | bytes 331784 | tf_op jit(solution)/shard_map/ppermute | solution.py:339
  300.8 10.0 %collective-permute-start.51 = (bf16[96,1792]{1,0:T(8,128)(2,1)S(1)}, bf16[96,1792]{1,0:T(8,128)(2,1)S(1)}, u32[]{:S(2)}, u32[]{:S(2)}) collective-permute-start(bf16[96,1792]{1,0:T(8,128)(2,1)S(1)} %fusion.10), channel_id=1, source_target_pairs={{0,1},{1,0},{2,3},{3,2},{4,5},{5,4},{6,7},{7,6},{8,9},{9,8},{10,11... | collective-permute-start | bytes 1032200 | tf_op jit(solution)/shard_map/ppermute | solution.py:339
  (47 other events, 301.0 us)
Sparse Core Ops, SparseCore 0:
  26.1 33.9 all-gather.2
